TPU v7x, 32 devices: a whole 2x2x4 slice. The times are simulated.
32 devices in a mesh: dp: 8 (over z, x), head: 4 (over y, core).
Axes of the slice: x: 2, y: 2, z: 4, core: 2. Of those that a mesh axis runs over, the one named last changes fastest.
Arguments:
- layer_input: bfloat16 [81920, 1024], P(('dp', 'head')), may hold values from -6 to 6
- cotangent: bfloat16 [81920, 1024], P(('dp', 'head')), may hold values from -6 to 6
- crop_blocks: int32 [8, 8], P('dp'), may hold values from 1 to 40, 80 in all within a row
- crop_padding: int32 [8, 8], P('dp'), may hold values from 0 to 127
- first_gain: float32 [1024], replicated, may hold values from 0.5 to 1.5
- first_shift: float32 [1024], replicated, may hold values from -1 to 1
- attend_weight: bfloat16 [1024, 3072], P(None, 'head'), may hold values from -0.1875 to 0.1875
- attend_bias: float32 [3072], P('head'), may hold values from -0.6 to 0.6
- output_weight: bfloat16 [1024, 1024], P('head'), may hold values from -1.5 to 1.5
- output_bias: float32 [1024], replicated, may hold values from -1 to 1
- second_gain: float32 [1024], replicated, may hold values from 0.5 to 1.5
- second_shift: float32 [1024], replicated, may hold values from -1 to 1
- expand_weight: bfloat16 [1024, 4096], P(None, 'head'), may hold values from -0.1875 to 0.1875
- expand_bias: float32 [4096], P('head'), may hold values from -1 to 1
- reduce_weight: bfloat16 [4096, 1024], P('head'), may hold values from -0.09375 to 0.09375
- reduce_bias: float32 [1024], replicated, may hold values from -1 to 1
Outputs:
- layer_output: bfloat16 [81920, 1024], P(('dp', 'head'))
- input_grad: float32 [81920, 1024], P(('dp', 'head'))
- first_gain_grad: float32 [1024], replicated
- first_shift_grad: float32 [1024], replicated
- attend_weight_grad: float32 [1024, 3072], P(None, 'head')
- attend_bias_grad: float32 [3072], P('head')
- output_weight_grad: float32 [1024, 1024], P('head')
- output_bias_grad: float32 [1024], replicated
- second_gain_grad: float32 [1024], replicated
- second_shift_grad: float32 [1024], replicated
- expand_weight_grad: float32 [1024, 4096], P(None, 'head')
- expand_bias_grad: float32 [4096], P('head')
- reduce_weight_grad: float32 [4096, 1024], P('head')
- reduce_bias_grad: float32 [1024], replicated
Inputs may be any that keep to these rules, and one draw needn't show every extreme that they name: `crop_blocks`: each group's crop blocks sum to 80; the longest crop of every group has exactly 40 blocks.
All inputs are finite; a program needn't handle non-finite values.
Results may differ from a plain program's by a relative error of at most 0.02.
Values may be sent and summed in bfloat16 or wider, within the bound.
No kernel may reach another device: no remote copies, remote signals or barrier semaphores. Data moves between devices by JAX's collectives and lax.ppermute only.
A program may use at most 512 MiB of HBM per device.

v0:
```python
import jax
import jax.numpy as jnp
from jax import lax
from jax.sharding import PartitionSpec as P

DH = 64
STRETCH = 128


epsilon = 1e-05
highest = lax.Precision.HIGHEST


def crop_layout(block_sizes, pad_sizes, block_total, stretch_rows):
    closing = jnp.cumsum(block_sizes)
    opening = closing - block_sizes
    position = jnp.arange(block_total, dtype=jnp.int32)
    member = jnp.logical_and(
        position[:, None] >= opening[None, :], position[:, None] < closing[None, :]
    ).astype(jnp.int32)
    first_block = jnp.sum(member * opening[None, :], axis=1)
    padding = jnp.sum(member * pad_sizes[None, :], axis=1)
    within = (position[:, None] - first_block[:, None]) * stretch_rows + jnp.arange(
        stretch_rows, dtype=jnp.int32
    )[None, :]
    validity = (within >= padding[:, None]).astype(jnp.float32).reshape(block_total * stretch_rows)
    crop_number = jnp.sum(member * jnp.arange(member.shape[1], dtype=jnp.int32)[None, :], axis=1)
    same_crop = (crop_number[:, None] == crop_number[None, :]).astype(jnp.float32)
    earlier = same_crop * (position[None, :] < position[:, None]).astype(jnp.float32)
    return (validity, earlier)


def layer_norm(values, gain, shift):
    average = jnp.mean(values, axis=-1, keepdims=True)
    centred = values - average
    spread = jnp.mean(centred * centred, axis=-1, keepdims=True)
    return centred * lax.rsqrt(spread + epsilon) * gain + shift


def feature(values):
    return jax.nn.elu(values) + 1.0


def slope(values):
    return jnp.where(values > 0, 1.0, jnp.exp(jnp.minimum(values, 0.0)))


def smooth_gate(values):
    return jax.nn.gelu(values, approximate=False)


def by_transpose(left, right):
    return lax.dot_general(
        left, right, (((1,), (1,)), ((), ())), preferred_element_type=jnp.float32
    )


def transpose_by(left, right):
    return lax.dot_general(
        left, right, (((0,), (0,)), ((), ())), preferred_element_type=jnp.float32
    )


def attention_maps(project, validity, heads_here):
    block_total = project.shape[0] // STRETCH
    shaped = project.reshape(block_total, STRETCH, heads_here, 3, DH)
    keep = validity.reshape(block_total, STRETCH, 1, 1)
    query_map = feature(shaped[:, :, :, 0]).astype(jnp.bfloat16)
    key_map = (keep * feature(shaped[:, :, :, 1])).astype(jnp.bfloat16)
    value_rows = shaped[:, :, :, 2].astype(jnp.bfloat16)
    products = jnp.einsum(
        "cjhd,cjhe->chde", key_map, value_rows, preferred_element_type=jnp.float32
    )
    key_sums = jnp.sum(key_map.astype(jnp.float32), axis=1)
    return (shaped, keep, query_map, key_map, value_rows, products, key_sums)


def attention_mix(feature_maps, states, key_totals):
    shaped, keep, query_map, key_map, value_rows = feature_maps[:5]
    lower = jnp.tril(jnp.ones((STRETCH, STRETCH), jnp.float32))
    scores = (
        jnp.einsum("cihd,cjhd->chij", query_map, key_map, preferred_element_type=jnp.float32)
        * lower
    )
    low_scores = scores.astype(jnp.bfloat16)
    low_states = states.astype(jnp.bfloat16)
    numerator = jnp.einsum(
        "chij,cjhe->cihe", low_scores, value_rows, preferred_element_type=jnp.float32
    ) + jnp.einsum("cihd,chde->cihe", query_map, low_states, preferred_element_type=jnp.float32)
    denominator = jnp.sum(scores, axis=3).transpose(0, 2, 1) + jnp.einsum(
        "cihd,chd->cih", query_map.astype(jnp.float32), key_totals, precision=highest
    )
    return (lower, low_scores, low_states, numerator, denominator, key_totals)


def attention_start(grad_attended, feature_maps, mixture):
    keep, query_map, value_rows = (feature_maps[1], feature_maps[2], feature_maps[4])
    lower, numerator, denominator = (mixture[0], mixture[3], mixture[4])
    floor = jnp.maximum(denominator, 1.0)
    grad_numer = (keep * grad_attended / floor[..., None]).astype(jnp.bfloat16)
    passing = (denominator > 1.0).astype(jnp.float32)
    grad_denom = -jnp.sum(keep * grad_attended * numerator, axis=3) * passing / (floor * floor)
    grad_low = jnp.einsum(
        "cihe,cjhe->chij", grad_numer, value_rows, preferred_element_type=jnp.float32
    )
    grad_scores = ((grad_low + grad_denom.transpose(0, 2, 1)[..., None]) * lower).astype(
        jnp.bfloat16
    )
    grad_states = jnp.einsum(
        "cihd,cihe->chde", query_map, grad_numer, preferred_element_type=jnp.float32
    )
    grad_totals = jnp.einsum(
        "cih,cihd->chd", grad_denom, query_map.astype(jnp.float32), precision=highest
    )
    return (grad_numer, grad_denom, grad_scores, grad_states, grad_totals)


def attention_finish(feature_maps, mixture, starts, grad_products, grad_key_sums):
    shaped, keep, query_map, key_map, value_rows = feature_maps[:5]
    low_scores, low_states, key_totals = (mixture[1], mixture[2], mixture[5])
    grad_numer, grad_denom, grad_scores = (starts[0], starts[1], starts[2])
    grad_query = (
        jnp.einsum("cihe,chde->cihd", grad_numer, low_states, preferred_element_type=jnp.float32)
        + jnp.einsum("chij,cjhd->cihd", grad_scores, key_map, preferred_element_type=jnp.float32)
        + grad_denom[..., None] * key_totals[:, None]
    )
    grad_keys = (
        jnp.einsum("chij,cihd->cjhd", grad_scores, query_map, preferred_element_type=jnp.float32)
        + jnp.einsum(
            "cjhe,chde->cjhd", value_rows, grad_products, preferred_element_type=jnp.float32
        )
        + grad_key_sums[:, None]
    )
    grad_values = jnp.einsum(
        "chij,cihe->cjhe", low_scores, grad_numer, preferred_element_type=jnp.float32
    ) + jnp.einsum("cjhd,chde->cjhe", key_map, grad_products, preferred_element_type=jnp.float32)
    grad_query = grad_query * slope(shaped[:, :, :, 0])
    grad_keys = grad_keys * keep * slope(shaped[:, :, :, 1])
    stacked = jnp.stack([grad_query, grad_keys, grad_values], axis=3)
    return stacked.reshape(shaped.shape[0] * STRETCH, shaped.shape[2] * 3 * DH).astype(jnp.bfloat16)


def on_device(
    layer_input,
    cotangent,
    crop_blocks,
    crop_padding,
    first_gain,
    first_shift,
    attend_weight,
    attend_bias,
    output_weight,
    output_bias,
    second_gain,
    second_shift,
    expand_weight,
    expand_bias,
    reduce_weight,
    reduce_bias,
):
    local_rows = layer_input.shape[0]
    group_rows = local_rows * lax.axis_size("head")
    group_blocks = group_rows // STRETCH
    inputs = layer_input.astype(jnp.float32)
    cot_local = cotangent.astype(jnp.float32)
    normed_local, first_pull = jax.vjp(layer_norm, inputs, first_gain, first_shift)
    normed_low = normed_local.astype(jnp.bfloat16)
    validity, earlier = crop_layout(crop_blocks[0], crop_padding[0], group_blocks, STRETCH)
    normed = lax.all_gather(normed_low, "head", axis=0, tiled=True)
    heads_here = attend_weight.shape[1] // (3 * DH)
    project = jnp.dot(normed, attend_weight, preferred_element_type=jnp.float32) + attend_bias
    feature_maps = attention_maps(project, validity, heads_here)
    states = jnp.einsum("ab,bhde->ahde", earlier, feature_maps[5], precision=highest)
    key_totals = jnp.einsum("ab,bhd->ahd", earlier, feature_maps[6], precision=highest)
    mixture = attention_mix(feature_maps, states, key_totals)
    attended_full = feature_maps[1] * mixture[3] / jnp.maximum(mixture[4], 1.0)[..., None]
    attended = attended_full.astype(jnp.bfloat16).reshape(group_rows, heads_here * DH)
    block_rows = attended
    middle = (
        inputs
        + lax.psum_scatter(
            jnp.dot(block_rows, output_weight, preferred_element_type=jnp.float32).astype(
                jnp.bfloat16
            ),
            "head",
            scatter_dimension=0,
            tiled=True,
        ).astype(jnp.float32)
        + output_bias
    )
    second_local, second_pull = jax.vjp(layer_norm, middle, second_gain, second_shift)
    second_low = second_local.astype(jnp.bfloat16)
    second_rows = lax.all_gather(second_low, "head", axis=0, tiled=True)
    hidden = jnp.dot(second_rows, expand_weight, preferred_element_type=jnp.float32) + expand_bias
    activated_full, gate_pull = jax.vjp(smooth_gate, hidden)
    activated = activated_full.astype(jnp.bfloat16)
    block_rows = activated
    reduced = lax.psum_scatter(
        jnp.dot(block_rows, reduce_weight, preferred_element_type=jnp.float32).astype(jnp.bfloat16),
        "head",
        scatter_dimension=0,
        tiled=True,
    ).astype(jnp.float32)
    layer_output = (middle + reduced + reduce_bias).astype(jnp.bfloat16)
    cot_rows = lax.all_gather(cotangent, "head", axis=0, tiled=True)
    grad_act = by_transpose(cot_rows, reduce_weight)
    grad_hidden = gate_pull(grad_act)[0].astype(jnp.bfloat16)
    reduce_weight_grad = transpose_by(activated, cot_rows)
    expand_bias_grad = jnp.sum(grad_hidden.astype(jnp.float32), axis=0)
    expand_weight_grad = transpose_by(second_rows, grad_hidden)
    block_rows = grad_hidden
    grad_second = lax.psum_scatter(
        by_transpose(block_rows, expand_weight).astype(jnp.bfloat16),
        "head",
        scatter_dimension=0,
        tiled=True,
    ).astype(jnp.float32)
    grad_middle_norm, second_gain_grad, second_shift_grad = second_pull(grad_second)
    grad_middle = cot_local + grad_middle_norm
    branch_low = grad_middle.astype(jnp.bfloat16)
    output_bias_grad = jnp.sum(branch_low.astype(jnp.float32), axis=0)
    branch_rows = lax.all_gather(branch_low, "head", axis=0, tiled=True)
    output_weight_grad = transpose_by(attended, branch_rows)
    grad_attended = by_transpose(branch_rows, output_weight).astype(jnp.bfloat16)
    grad_attended = grad_attended.reshape(group_blocks, STRETCH, heads_here, DH)
    starts = attention_start(grad_attended, feature_maps, mixture)
    grad_products = jnp.einsum("ab,ahde->bhde", earlier, starts[3], precision=highest).astype(
        jnp.bfloat16
    )
    grad_key_sums = jnp.einsum("ab,ahd->bhd", earlier, starts[4], precision=highest)
    grad_project = attention_finish(feature_maps, mixture, starts, grad_products, grad_key_sums)
    attend_weight_grad = transpose_by(normed, grad_project)
    attend_bias_grad = jnp.sum(grad_project.astype(jnp.float32), axis=0)
    block_rows = grad_project
    grad_first = lax.psum_scatter(
        by_transpose(block_rows, attend_weight).astype(jnp.bfloat16),
        "head",
        scatter_dimension=0,
        tiled=True,
    ).astype(jnp.float32)
    reduce_bias_grad = jnp.sum(cot_local, axis=0)
    grad_input_norm, first_gain_grad, first_shift_grad = first_pull(grad_first)
    input_grad = grad_middle + grad_input_norm
    (
        first_gain_grad,
        first_shift_grad,
        output_bias_grad,
        second_gain_grad,
        second_shift_grad,
        reduce_bias_grad,
    ) = lax.psum(
        (
            first_gain_grad,
            first_shift_grad,
            output_bias_grad,
            second_gain_grad,
            second_shift_grad,
            reduce_bias_grad,
        ),
        ("dp", "head"),
    )
    (
        attend_weight_grad,
        attend_bias_grad,
        output_weight_grad,
        expand_weight_grad,
        expand_bias_grad,
        reduce_weight_grad,
    ) = (
        lax.psum(attend_weight_grad.astype(jnp.bfloat16), "dp").astype(jnp.float32),
        lax.psum(attend_bias_grad.astype(jnp.bfloat16), "dp").astype(jnp.float32),
        lax.psum(output_weight_grad.astype(jnp.bfloat16), "dp").astype(jnp.float32),
        lax.psum(expand_weight_grad.astype(jnp.bfloat16), "dp").astype(jnp.float32),
        lax.psum(expand_bias_grad.astype(jnp.bfloat16), "dp").astype(jnp.float32),
        lax.psum(reduce_weight_grad.astype(jnp.bfloat16), "dp").astype(jnp.float32),
    )
    return (
        layer_output,
        input_grad,
        first_gain_grad,
        first_shift_grad,
        attend_weight_grad,
        attend_bias_grad,
        output_weight_grad,
        output_bias_grad,
        second_gain_grad,
        second_shift_grad,
        expand_weight_grad,
        expand_bias_grad,
        reduce_weight_grad,
        reduce_bias_grad,
    )


def solution(mesh):
    in_specs = (
        P(("dp", "head"), None),
        P(("dp", "head"), None),
        P("dp", None),
        P("dp", None),
        P(),
        P(),
        P(None, "head"),
        P("head"),
        P("head", None),
        P(),
        P(),
        P(),
        P(None, "head"),
        P("head"),
        P("head", None),
        P(),
    )
    out_specs = (
        P(("dp", "head"), None),
        P(("dp", "head"), None),
        P(),
        P(),
        P(None, "head"),
        P("head"),
        P("head", None),
        P(),
        P(),
        P(),
        P(None, "head"),
        P("head"),
        P("head", None),
        P(),
    )
    return jax.shard_map(
        on_device, mesh=mesh, in_specs=in_specs, out_specs=out_specs, check_vma=False
    )
```

profile of v0, /device:TPU:8, one launch (start us, length us, event | category | flops | bytes accessed | tf_op | source)
XLA Modules:
  0.0 2181.0 jit_solution(10112209222913035576)
XLA Ops:
  20.7 132.3 %all-gather.5.cloned.1.call-done = bf16[10240,1024]{1,0:T(8,128)(2,1)} async-done(((bf16[2560,1024]{1,0:T(8,128)(2,1)}), bf16[10240,1024]{1,0:T(8,128)(2,1)}) %all-gather.5.cloned.1.call-update) | async-done | bytes 20971536 | tf_op jit(solution)/shard_map/all_gather | solution.py:169
  152.9 25.6 %convolution_add_fusion = f32[10240,768]{1,0:T(8,128)} fusion(bf16[10240,1024]{1,0:T(8,128)(2,1)} %all-gather.5.cloned.1.call-done, bf16[1024,768]{1,0:T(8,128)(2,1)} %param.22, f32[768]{0:T(1024)S(1)} %copy-done.55), kind=kOutput, calls=%fused_computation.21 | convolution fusion | flops 16113991680 | bytes 54004736 | tf_op jit(solution)/shard_map/dot_general | solution.py:171
  178.5 30.8 %copy.86 = f32[10240,768]{0,1:T(8,128)} copy(f32[10240,768]{1,0:T(8,128)} %convolution_add_fusion) | data formatting | bytes 62914560 | tf_op jit(solution)/shard_map/add | solution.py:171
  209.3 26.4 %copy.123 = f32[96,8,80,128]{3,2,1,0:T(8,128)} copy(f32[96,8,80,128]{3,1,2,0:T(8,128)} %bitcast.157) | data formatting | bytes 62914560
  344.8 19.6 fusion.40
  385.7 153.2 %reduce-scatter.5.cloned.1.call-done = bf16[2560,1024]{1,0:T(8,128)(2,1)} async-done(((bf16[10240,1024]{1,0:T(8,128)(2,1)}), bf16[2560,1024]{1,0:T(8,128)(2,1)}) %reduce-scatter.5.cloned.1.call-update) | async-done | bytes 5242896 | tf_op jit(solution)/shard_map/reduce_scatter | solution.py:181
  556.6 131.1 %all-gather.7.cloned.1.call-done = bf16[10240,1024]{1,0:T(8,128)(2,1)} async-done(((bf16[2560,1024]{1,0:T(8,128)(2,1)}), bf16[10240,1024]{1,0:T(8,128)(2,1)}) %all-gather.7.cloned.1.call-update) | async-done | bytes 20971536 | tf_op jit(solution)/shard_map/all_gather | solution.py:193
  687.7 32.2 %fusion.105 = f32[10240,1024]{1,0:T(8,128)} fusion(bf16[10240,1024]{1,0:T(8,128)(2,1)} %all-gather.7.cloned.1.call-done, bf16[1024,1024]{1,0:T(8,128)(2,1)} %param.28), kind=kOutput, calls=%fused_computation.173 | convolution fusion | flops 21474836480 | bytes 65011712 | tf_op jit(solution)/shard_map/dot_general | solution.py:194
  719.9 101.0 %all-gather.9.cloned.1.call-done = bf16[10240,1024]{1,0:T(8,128)(2,1)} async-done(((bf16[2560,1024]{1,0:T(8,128)(2,1)}), bf16[10240,1024]{1,0:T(8,128)(2,1)}) %all-gather.9.cloned.1.call-update) | async-done | bytes 20971536 | tf_op jit(solution)/shard_map/all_gather | solution.py:205
  820.9 124.3 %fusion.91 = (bf16[1024]{0:T(1024)(128)(2,1)}, bf16[10240,1024]{1,0:T(8,128)(2,1)}, f32[10240,1024]{1,0:T(8,128)}) fusion(f32[10240,1024]{1,0:T(8,128)} %fusion.105, f32[1024]{0:T(1024)S(1)} %copy-done.50, bf16[10240,1024]{1,0:T(8,128)(2,1)} %all-gather.9.cloned.1.call-done, bf16[1024,1024]{1,0:T(8,128)(2,1)S(1)} %copy-done), kind=kOutput, calls=%fused_computation.166 | convolution fusion | flops 22250782720 | bytes 127932416 | tf_op jit(solution)/shard_map/dot_general | solution.py:53
  945.2 32.2 %convolution_convert_fusion.2 = bf16[10240,1024]{1,0:T(8,128)(2,1)} fusion(bf16[10240,1024]{1,0:T(8,128)(2,1)} %get-tuple-element.37, bf16[1024,1024]{1,0:T(8,128)(2,1)S(1)} %copy-done.54), kind=kOutput, calls=%fused_computation.24 | convolution fusion | flops 21485322240 | bytes 44040192 | tf_op jit(solution)/shard_map/dot_general | solution.py:53
  977.5 44.0 %multiply_convert_fusion = bf16[10240,1024]{1,0:T(8,128)(2,1)} fusion(f32[10240,1024]{1,0:T(8,128)} %get-tuple-element.38, f32[10240,1024]{1,0:T(8,128)} %fusion.105, f32[1024]{0:T(1024)S(1)} %copy-done.50), kind=kLoop, calls=%fused_computation.3 | loop fusion | flops 41943040 | bytes 104861696 | tf_op jit(solution)/shard_map/convert_element_type | solution.py:196
  1021.5 32.5 %convolution_convert_fusion.3 = bf16[10240,1024]{1,0:T(8,128)(2,1)} fusion(bf16[10240,1024]{1,0:T(8,128)(2,1)} %multiply_convert_fusion, bf16[1024,1024]{1,0:T(8,128)(2,1)S(1)} %copy-done), kind=kOutput, calls=%fused_computation.25 | convolution fusion | flops 21485322240 | bytes 44040192 | tf_op jit(solution)/shard_map/dot_general | solution.py:199
  1054.1 76.7 %reduce-scatter.9.cloned.1.call-done = bf16[2560,1024]{1,0:T(8,128)(2,1)} async-done(((bf16[10240,1024]{1,0:T(8,128)(2,1)}), bf16[2560,1024]{1,0:T(8,128)(2,1)}) %reduce-scatter.9.cloned.1.call-update) | async-done | bytes 5242896 | tf_op jit(solution)/shard_map/reduce_scatter | solution.py:212
  1140.4 146.0 %reduce-scatter.7.cloned.1.call-done = bf16[2560,1024]{1,0:T(8,128)(2,1)} async-done(((bf16[10240,1024]{1,0:T(8,128)(2,1)}), bf16[2560,1024]{1,0:T(8,128)(2,1)}) %reduce-scatter.7.cloned.1.call-update) | async-done | bytes 5242896 | tf_op jit(solution)/shard_map/reduce_scatter | solution.py:198
  1308.5 29.1 %convolution_convert_fusion.6 = bf16[1024,1024]{1,0:T(8,128)(2,1)} fusion(bf16[10240,1024]{1,0:T(8,128)(2,1)} %all-gather.7.cloned.1.call-done, bf16[10240,1024]{1,0:T(8,128)(2,1)} %get-tuple-element.37), kind=kOutput, calls=%fused_computation.109 | convolution fusion | flops 21475885056 | bytes 44040192 | tf_op jit(solution)/shard_map/dot_general | solution.py:59
  1337.6 28.3 %convolution_convert_fusion.5 = bf16[1024,1024]{1,0:T(8,128)(2,1)} fusion(bf16[10240,1024]{1,0:T(8,128)(2,1)} %multiply_convert_fusion, bf16[10240,1024]{1,0:T(8,128)(2,1)} %all-gather.9.cloned.1.call-done), kind=kOutput, calls=%fused_computation.108 | convolution fusion | flops 21475885056 | bytes 44040192 | tf_op jit(solution)/shard_map/dot_general | solution.py:59
  1365.9 73.6 %all-gather.11.cloned.1.call-done = bf16[10240,1024]{1,0:T(8,128)(2,1)} async-done(((bf16[2560,1024]{1,0:T(8,128)(2,1)}), bf16[10240,1024]{1,0:T(8,128)(2,1)}) %all-gather.11.cloned.1.call-update) | async-done | bytes 20971536 | tf_op jit(solution)/shard_map/all_gather | solution.py:222
  1664.9 34.0 %copy.107 = bf16[80,128,4,3,64]{1,0,4,3,2:T(8,128)(2,1)} copy(bf16[80,128,4,3,64]{1,4,2,0,3:T(8,128)(2,1)S(1)} %get-tuple-element.40) | data formatting | bytes 31457280 | tf_op jit(solution)/shard_map/convert_element_type | solution.py:140
  1711.2 26.1 %fusion.54 = bf16[1024,768]{1,0:T(8,128)(2,1)} fusion(bf16[10240,1024]{1,0:T(8,128)(2,1)} %all-gather.5.cloned.1.call-done, bf16[96,8,80,128]{3,2,1,0:T(8,128)(2,1)} %bitcast.168), kind=kOutput, calls=%fused_computation.110 | convolution fusion | flops 16106913792 | bytes 38273024 | tf_op jit(solution)/shard_map/dot_general | solution.py:59
  1737.4 37.8 %convolution_convert_fusion.1 = bf16[10240,1024]{1,0:T(8,128)(2,1)} fusion(bf16[1024,768]{1,0:T(8,128)(2,1)} %param.22, bf16[96,8,80,128]{3,2,1,0:T(8,128)(2,1)} %bitcast.169), kind=kOutput, calls=%fused_computation.23 | convolution fusion | flops 16116613120 | bytes 38273024 | tf_op jit(solution)/shard_map/dot_general | solution.py:53
  1796.5 154.3 %all-reduce.5.cloned.1.call-done = (bf16[1024,768]{1,0:T(8,128)(2,1)}, bf16[256,1024]{1,0:T(8,128)(2,1)}, bf16[1024,1024]{1,0:T(8,128)(2,1)}, bf16[1024,1024]{1,0:T(8,128)(2,1)}) async-done(((bf16[1024,768]{1,0:T(8,128)(2,1)}, bf16[256,1024]{1,0:T(8,128)(2,1)}, bf16[1024,1024]{1,0:T(8,128)(2,1)}, bf16[1024,1024]{1,0:T(8,128)(2,1)}), (bf16[1024,768]{1,0:T(8,128)(2,1)}, bf16[256,1024]{1,0:T(8,128)(2,1)}, ...) | async-done | bytes 6291472 | tf_op jit(solution)/shard_map/psum | solution.py:270
  1963.8 143.0 %reduce-scatter.11.cloned.1.call-done = bf16[2560,1024]{1,0:T(8,128)(2,1)} async-done(((bf16[10240,1024]{1,0:T(8,128)(2,1)}), bf16[2560,1024]{1,0:T(8,128)(2,1)}) %reduce-scatter.11.cloned.1.call-update) | async-done | bytes 5242896 | tf_op jit(solution)/shard_map/reduce_scatter | solution.py:235
  2134.2 40.0 %all-reduce = (f32[1024]{0:T(1024)}, f32[1024]{0:T(1024)}, f32[1024]{0:T(1024)}, f32[1024]{0:T(1024)}, f32[1024]{0:T(1024)}, /*index=5*/f32[1024]{0:T(1024)}) all-reduce(f32[1024]{0:T(1024)S(1)} %get-tuple-element.16, f32[1024]{0:T(1024)S(1)} %get-tuple-element.19, ...), channel_id=1, replica_groups=mesh['dp'=8,'head'=4] {'dp','head'}, use_global_device_ids=true, to_apply=%region_20.21 | all-reduce | flops 6144 | bytes 49152 | tf_op jit(solution)/shard_map/psum | solution.py:251
  (229 shorter events, 492.2 us)
Async XLA Ops:
  7.2 813.7 %copy-start = (bf16[1024,1024]{1,0:T(8,128)(2,1)S(1)}, bf16[1024,1024]{1,0:T(8,128)(2,1)}, u32[]{:S(2)}) copy-start(bf16[1024,1024]{1,0:T(8,128)(2,1)} %param.30) | copy-start | bytes 6291460
  7.2 145.7 %all-gather.5.cloned.1.call-start = ((), (), s32[]{:S(2)}) async-start(), calls=%async_computation.4 | async-start | bytes 26214400 | tf_op jit(solution)/shard_map/all_gather | solution.py:169
  20.0 518.9 %reduce-scatter.5.cloned.1.call-start = ((), (), s32[]{:S(2)}) async-start(), calls=%async_computation.5 | async-start | bytes 26214400 | tf_op jit(solution)/shard_map/reduce_scatter | solution.py:181
  20.4 324.4 %copy-start.19 = (f32[128,128]{0,1:T(8,128)}, f32[128,128]{0,1:T(8,128)S(1)}, u32[]{:S(2)}) copy-start(f32[128,128]{0,1:T(8,128)S(1)} %fusion.61) | copy-start | bytes 196612
  20.6 270.0 %copy-start.41 = (s32[80]{0:T(128)}, s32[80]{0:T(128)S(1)}, u32[]{:S(2)}) copy-start(s32[80]{0:T(128)S(1)} %get-tuple-element.21) | copy-start | bytes 964
  20.7 324.2 %copy-start.14 = (f32[80,128]{1,0:T(8,128)}, f32[80,128]{1,0:T(8,128)S(1)}, u32[]{:S(2)}) copy-start(f32[80,128]{1,0:T(8,128)S(1)} %fusion.70) | copy-start | bytes 122884
  385.6 165.6 %slice-start = ((s8[5242880]{0:T(1024)(128)(4,1)}), s8[1048576]{0:T(1024)(128)(4,1)S(1)}, s32[]{:S(2)}) async-start(s8[5242880]{0:T(1024)(128)(4,1)} %bitcast.151), calls=%async_computation.13 | async-start | bytes 2097152
  385.6 165.6 %copy-start.43 = (f32[1024]{0:T(1024)S(1)}, f32[1024]{0:T(1024)}, u32[]{:S(2)}) copy-start(f32[1024]{0:T(1024)} %param.26) | copy-start | bytes 12292
  385.7 165.6 %copy-start.49 = (f32[1024]{0:T(1024)S(1)}, f32[1024]{0:T(1024)}, u32[]{:S(2)}) copy-start(f32[1024]{0:T(1024)} %param.27) | copy-start | bytes 12292
  385.7 302.0 %all-gather.7.cloned.1.call-start = ((), (), s32[]{:S(2)}) async-start(), calls=%async_computation.6 | async-start | bytes 26214400 | tf_op jit(solution)/shard_map/all_gather | solution.py:193
  555.9 264.9 %all-gather.9.cloned.1.call-start = ((), (), s32[]{:S(2)}) async-start(), calls=%async_computation.8 | async-start | bytes 26214400 | tf_op jit(solution)/shard_map/all_gather | solution.py:205
  556.5 264.4 %copy-start.50 = (f32[1024]{0:T(1024)S(1)}, f32[1024]{0:T(1024)}, u32[]{:S(2)}) copy-start(f32[1024]{0:T(1024)} %param.29) | copy-start | bytes 12292
  556.5 574.2 %reduce-scatter.9.cloned.1.call-start = ((), (), s32[]{:S(2)}) async-start(), calls=%async_computation.9 | async-start | bytes 26214400 | tf_op jit(solution)/shard_map/reduce_scatter | solution.py:212
  977.4 308.9 %reduce-scatter.7.cloned.1.call-start = ((), (), s32[]{:S(2)}) async-start(), calls=%async_computation.7 | async-start | bytes 26214400 | tf_op jit(solution)/shard_map/reduce_scatter | solution.py:198
  1054.0 232.4 %copy-start.51 = (f32[1024]{0:T(1024)S(1)}, f32[1024]{0:T(1024)}, u32[]{:S(2)}) copy-start(f32[1024]{0:T(1024)} %param.31) | copy-start | bytes 12292
  1054.0 385.5 %all-gather.11.cloned.1.call-start = ((), (), s32[]{:S(2)}) async-start(), calls=%async_computation.10 | async-start | bytes 26214400 | tf_op jit(solution)/shard_map/all_gather | solution.py:222
  1307.7 643.1 %all-reduce.5.cloned.1.call-start = ((), (), s32[]{:S(2)}) async-start(), calls=%async_computation.12 | async-start | bytes 12582912 | tf_op jit(solution)/shard_map/psum | solution.py:270
  1737.4 369.5 %reduce-scatter.11.cloned.1.call-start = ((), (), s32[]{:S(2)}) async-start(), calls=%async_computation.11 | async-start | bytes 26214400 | tf_op jit(solution)/shard_map/reduce_scatter | solution.py:235
  1775.2 331.7 %copy-start.24 = (f32[2560]{0:T(1024)S(1)}, f32[2560]{0:T(1024)}, u32[]{:S(2)}) copy-start(f32[2560]{0:T(1024)} %copy-done.23) | copy-start | bytes 30724
  1775.2 331.7 %copy-start.40 = (f32[1024]{0:T(1024)S(1)}, f32[1024]{0:T(1024)}, u32[]{:S(2)}) copy-start(f32[1024]{0:T(1024)} %param.20) | copy-start | bytes 12292
  1956.3 157.9 %copy-start.34 = (f32[2560]{0:T(1024)S(1)}, f32[2560]{0:T(1024)}, u32[]{:S(2)}) copy-start(f32[2560]{0:T(1024)} %copy-done.33) | copy-start | bytes 30724
  1956.4 157.9 %copy-start.28 = (f32[2560]{0:T(1024)S(1)}, f32[2560]{0:T(1024)}, u32[]{:S(2)}) copy-start(f32[2560]{0:T(1024)} %copy-done.27) | copy-start | bytes 30724
  1963.8 158.6 %slice-start.2 = ((s8[5242880]{0:T(1024)(128)(4,1)}), s8[1048576]{0:T(1024)(128)(4,1)S(1)}, s32[]{:S(2)}) async-start(s8[5242880]{0:T(1024)(128)(4,1)} %bitcast.153), calls=%async_computation.15 | async-start | bytes 2097152
  1963.8 158.6 %copy-start.32 = (f32[2560]{0:T(1024)S(1)}, f32[2560]{0:T(1024)}, u32[]{:S(2)}) copy-start(f32[2560]{0:T(1024)} %copy-done.31) | copy-start | bytes 30724
  (50 other events, 1447.1 us)
Sparse Core Ops, SparseCore 0:
  20.1 132.7 all-gather.4
  385.8 153.1 reduce-scatter.4
  556.1 131.6 all-gather.6
  689.2 131.6 all-gather.8
  977.6 153.1 reduce-scatter.8
  1133.2 153.1 reduce-scatter.6
  1307.8 131.6 all-gather.10
  1737.5 213.2 all-reduce.4
  1953.4 153.4 reduce-scatter.10
where the time goes:
time: 2190 us; the launch traced here: 2180 us
  waiting for transfers between devices  1110 us (51%)
  matrix products  600 us (27%)
  local copies, waits for them, and re-layouts  202 us (9%)
  other arithmetic  192 us (9%)
  blocking collectives  59.4 us (3%)
    dot_general x4, matrix products, by_transpose(): lax.dot_general(left, right, (((1,), (1,)), ((), ())), preferred_element_...  206 us
    psum x1, waiting for transfers between devices, on_device(): lax.psum(attend_weight_grad.astype(jnp.bfloat16), 'dp').astype(jnp.float32)  154 us
    reduce_scatter x1, waiting for transfers between devices, on_device(): lax.psum_scatter(jnp.dot(block_rows, output_weight, preferred_element_typ...  153 us
    reduce_scatter x1, waiting for transfers between devices, on_device(): lax.psum_scatter(jnp.dot(block_rows, reduce_weight, preferred_element_typ...  146 us
    reduce_scatter x1, waiting for transfers between devices, on_device(): lax.psum_scatter(by_transpose(block_rows, attend_weight).astype(jnp.bfloa...  143 us
    all_gather x1, waiting for transfers between devices, on_device(): normed = lax.all_gather(normed_low, 'head', axis=0, tiled=True)  132 us
    all_gather x1, waiting for transfers between devices, on_device(): second_rows = lax.all_gather(second_low, 'head', axis=0, tiled=True)  131 us
    all_gather x1, waiting for transfers between devices, on_device(): cot_rows = lax.all_gather(cotangent, 'head', axis=0, tiled=True)  101 us
  transfers between devices with their start and end apart: 9, of which 9 were waited for; matrix products, arithmetic and copies ran while one was open for 10% of the time, Pallas kernels for 0%

commit v1 on v0

v1 whole, which is shorter than its diff:
```python
import functools

import jax
import jax.numpy as jnp
from jax import lax
from jax.experimental import pallas as pl
from jax.experimental.pallas import tpu as pltpu
from jax.sharding import PartitionSpec as P

DH = 64
STRETCH = 128
D = 1024
QUADS = 4
QW = D // QUADS
PW = 3 * QW
EPS = 1e-05
VMEM = 60 * 1024 * 1024

f32 = jnp.float32
bf16 = jnp.bfloat16


def nn(a, b):
    return lax.dot_general(a, b, (((1,), (0,)), ((), ())), preferred_element_type=f32)


def nt(a, b):
    return lax.dot_general(a, b, (((1,), (1,)), ((), ())), preferred_element_type=f32)


def tn(a, b):
    return lax.dot_general(a, b, (((0,), (0,)), ((), ())), preferred_element_type=f32)


def params():
    return pltpu.CompilerParams(vmem_limit_bytes=VMEM)


def cost(flops, bytes_accessed):
    return pl.CostEstimate(flops=flops, bytes_accessed=bytes_accessed, transcendentals=0)


def head_rows():
    lane = lax.broadcasted_iota(jnp.int32, (1, QW), 1) // DH
    return [(lane == h).astype(f32) for h in range(4)]


def spread_heads(block, picks):
    return jnp.concatenate([block * pick for pick in picks], axis=0)


def spread_state(state, picks):
    return jnp.concatenate([state * pick for pick in picks], axis=0)


def gather_state(square, picks):
    total = square[0:DH] * picks[0]
    for h in range(1, 4):
        total = total + square[h * DH : (h + 1) * DH] * picks[h]
    return total


def centre(values):
    average = jnp.mean(values, axis=-1, keepdims=True)
    centred = values - average
    spread = jnp.mean(centred * centred, axis=-1, keepdims=True)
    inverse = lax.rsqrt(spread + EPS)
    return centred * inverse, inverse


def norm_back(xhat, inverse, grad, gain):
    w = grad * gain
    return inverse * (
        w
        - jnp.mean(w, axis=-1, keepdims=True)
        - xhat * jnp.mean(w * xhat, axis=-1, keepdims=True)
    )


def fold_rows(values):
    rows, columns = values.shape
    return jnp.sum(values.reshape(rows // 8, 8, columns), axis=0)


def normal_parts(v):
    size = jnp.abs(v) * 0.7071067811865476
    t = 1.0 / (1.0 + 0.3275911 * size)
    bell = jnp.exp(-0.5 * v * v)
    poly = t * (
        0.254829592
        + t * (-0.284496736 + t * (1.421413741 + t * (-1.453152027 + t * 1.061405429)))
    )
    tail = 0.5 * poly * bell
    return jnp.where(v < 0, tail, 1.0 - tail), bell


def qkv_kernel(blocks, thr, last, x, gain, shift, *refs):
    wa, ba = refs[0:4], refs[4]
    q_out, k_out, v_out, n_out, t_out = refs[5:10]
    step = pl.program_id(0)
    rows = blocks * STRETCH

    @pl.when(step == 0)
    def _():
        t_out[...] = jnp.zeros_like(t_out)

    xhat, _ = centre(x[...].astype(f32))
    normed = (xhat * gain[...] + shift[...]).astype(bf16)
    n_out[...] = normed
    place = lax.broadcasted_iota(jnp.int32, (STRETCH, 128), 0)
    valid = jnp.concatenate(
        [(place >= thr[step * blocks + b]).astype(f32) for b in range(blocks)], axis=0
    )
    low = lax.broadcasted_iota(jnp.int32, (rows, 128), 1) < DH

    def feature(values):
        return jnp.where(values > 0, values + 1.0, jnp.exp(jnp.minimum(values, 0.0)))

    for g in range(QUADS):
        project = nn(normed, wa[g][...]) + ba[:, g * PW : (g + 1) * PW]
        for pair in range(2):
            c0, c1, c2 = (
                project[:, pair * 384 + j * 128 : pair * 384 + (j + 1) * 128] for j in range(3)
            )
            at = slice(g * QW + pair * 128, g * QW + (pair + 1) * 128)
            q_out[:, at] = feature(jnp.where(low, c0, c1)).astype(bf16)
            key = pltpu.roll(jnp.where(low, c2, c0), DH, 1)
            k_out[:, at] = (valid * feature(key)).astype(bf16)
            v_out[:, at] = jnp.where(low, c1, c2).astype(bf16)
    picks = head_rows()
    for b in range(blocks):

        @pl.when(last[step * blocks + b] == 1)
        def _(b=b):
            here = slice(b * STRETCH, (b + 1) * STRETCH)
            for g in range(QUADS):
                at = slice(g * QW, (g + 1) * QW)
                key = k_out[here, at]
                t_out[0:DH, at] += gather_state(tn(key, v_out[here, at]), picks)
                t_out[DH : DH + 8, at] += fold_rows(key.astype(f32))


def attend_kernel(blocks, cont, q, k, v, x, s_in, ones, bo, gain, shift, *refs):
    wo = refs[0:4]
    att_out, rec_out, st_out, kt_out, mid_out, n_out = refs[4:10]
    state, total = refs[10:12]
    step = pl.program_id(0)

    @pl.when(step == 0)
    def _():
        state[...] = s_in[0:DH]
        total[...] = jnp.broadcast_to(
            jnp.sum(s_in[DH : DH + 8], axis=0, keepdims=True), total.shape
        )

    picks = head_rows()
    low_picks = [p.astype(bf16) for p in picks]
    row = lax.broadcasted_iota(jnp.int32, (STRETCH, 512), 0)
    lane = lax.broadcasted_iota(jnp.int32, (STRETCH, 512), 1) % STRETCH
    lower = lane <= row
    for b in range(blocks):
        keep = cont[step * blocks + b].astype(f32)
        here = slice(b * STRETCH, (b + 1) * STRETCH)
        state[...] = state[...] * keep
        total[...] = total[...] * keep
        low_state = state[...].astype(bf16)
        st_out[b * DH : (b + 1) * DH, :] = low_state
        kt_out[b * 8 : (b + 1) * 8, :] = total[...]
        for g in range(QUADS):
            at = slice(g * QW, (g + 1) * QW)
            qb, kb, vb = q[here, at], k[here, at], v[here, at]
            scores = nt(qb, spread_heads(kb, low_picks))
            scores = jnp.where(lower, scores, 0.0).astype(bf16)
            numer = nn(scores, spread_heads(vb, low_picks)) + nn(
                qb, spread_state(low_state[:, at], low_picks)
            )
            weighted = (qb.astype(f32) * total[0:1, at]).astype(bf16)
            denom = nn(scores, ones[0:512]) + nn(weighted, ones[512:768])
            rec = 1.0 / jnp.maximum(denom, 1.0)
            rec_out[here, at] = rec
            att_out[here, at] = (numer * rec).astype(bf16)
            state[:, at] += gather_state(tn(kb, vb), picks)
            total[:, at] += jnp.sum(kb.astype(f32), axis=0, keepdims=True)
    return picks


def attend_tile(blocks, cont, thr, *refs):
    q, k, v, x, s_in, ones, bo, gain, shift = refs[0:9]
    wo = refs[9:13]
    att_out, rec_out, st_out, kt_out, mid_out, n_out = refs[13:19]
    attend_kernel(blocks, cont, q, k, v, x, s_in, ones, bo, gain, shift, *refs[9:])
    step = pl.program_id(0)
    place = lax.broadcasted_iota(jnp.int32, (STRETCH, D), 0)
    for b in range(blocks):
        here = slice(b * STRETCH, (b + 1) * STRETCH)

        @pl.when(thr[step * blocks + b] > 0)
        def _(b=b, here=here):
            valid = (place >= thr[step * blocks + b]).astype(f32)
            rec = rec_out[here, :] * valid
            rec_out[here, :] = rec
            att_out[here, :] = (att_out[here, :].astype(f32) * valid).astype(bf16)

    middle = x[...].astype(f32) + bo[...]
    for g in range(QUADS):
        middle = middle + nn(att_out[:, g * QW : (g + 1) * QW], wo[g][...])
    mid_out[...] = middle
    xhat, _ = centre(middle)
    n_out[...] = (xhat * gain[...] + shift[...]).astype(bf16)


def ffn_kernel(blocks, first, n2, cot, mid, att, rec, q, gain, be, br, ones, *refs):
    we, wr, wo = refs[0:4], refs[4:8], refs[8:12]
    act, gh = refs[12:16], refs[16:20]
    out, gm_out, gb_out, gn_out, t_out, l_out, sums, be_sum = refs[20:28]
    step = pl.program_id(0)

    @pl.when(step == 0)
    def _():
        l_out[...] = jnp.zeros_like(l_out)
        sums[...] = jnp.zeros_like(sums)
        be_sum[...] = jnp.zeros_like(be_sum)

    normed = n2[...]
    cotangent = cot[...]
    reduced = None
    grad = None
    for g in range(QUADS):
        at = slice(g * D, (g + 1) * D)
        hidden = nn(normed, we[g][...]) + be[:, at]
        grad_act = nt(cotangent, wr[g][...])
        phi, bell = normal_parts(hidden)
        active = (hidden * phi).astype(bf16)
        back = (grad_act * (phi + hidden * (0.3989422804014327 * bell))).astype(bf16)
        act[g][...] = active
        gh[g][...] = back
        be_sum[:, at] += fold_rows(back.astype(f32))
        part = nn(active, wr[g][...])
        reduced = part if reduced is None else reduced + part
        part = nt(back, we[g][...])
        grad = part if grad is None else grad + part
    middle = mid[...]
    out[...] = (middle + reduced + br[...]).astype(bf16)
    xhat, inverse = centre(middle)
    cot_wide = cotangent.astype(f32)
    grad_middle = cot_wide + norm_back(xhat, inverse, grad, gain[...])
    gm_out[...] = grad_middle
    branch = grad_middle.astype(bf16)
    gb_out[...] = branch
    sums[0:8, :] += fold_rows(branch.astype(f32))
    sums[8:16, :] += fold_rows(grad * xhat)
    sums[16:24, :] += fold_rows(grad)
    sums[24:32, :] += fold_rows(cot_wide)
    for g in range(QUADS):
        at = slice(g * QW, (g + 1) * QW)
        grad_att = nt(branch, wo[g][...]).astype(bf16).astype(f32)
        share = rec[:, at]
        numer = grad_att * share
        gn_out[:, at] = numer.astype(bf16)
        t_out[:, at] = jnp.where(
            share < 1.0, -(numer * att[:, at].astype(f32)), 0.0
        ).astype(bf16)
    picks = head_rows()
    for b in range(blocks):

        @pl.when(first[step * blocks + b] == 1)
        def _(b=b):
            here = slice(b * STRETCH, (b + 1) * STRETCH)
            for g in range(QUADS):
                at = slice(g * QW, (g + 1) * QW)
                query = q[here, at]
                l_out[0:DH, at] += gather_state(tn(query, gn_out[here, at]), picks)
                grad_denom = nn(t_out[here, at], ones[512:768])
                l_out[DH : DH + 8, at] += fold_rows(grad_denom * query.astype(f32))


def back_kernel(blocks, tiles, cont, q, k, v, gn, t, st, kt, g_in, ones, *refs):
    gp_out, ba_sum = refs[0:4], refs[4]
    state, total = refs[5:7]
    step = pl.program_id(0)
    tile = tiles - 1 - step

    @pl.when(step == 0)
    def _():
        state[...] = g_in[0:DH]
        total[...] = jnp.broadcast_to(
            jnp.sum(g_in[DH : DH + 8], axis=0, keepdims=True), total.shape
        )
        ba_sum[...] = jnp.zeros_like(ba_sum)

    picks = head_rows()
    low_picks = [p.astype(bf16) for p in picks]
    row = lax.broadcasted_iota(jnp.int32, (STRETCH, 512), 0)
    lane = lax.broadcasted_iota(jnp.int32, (STRETCH, 512), 1) % STRETCH
    lower = lane <= row
    upper = lane >= row
    low_lane = lax.broadcasted_iota(jnp.int32, (STRETCH, 128), 1) < DH
    all_ones = jnp.ones((STRETCH, QW), bf16)
    for b in reversed(range(blocks)):
        keep = cont[tile * blocks + b + 1].astype(f32)
        here = slice(b * STRETCH, (b + 1) * STRETCH)
        state[...] = state[...] * keep
        total[...] = total[...] * keep
        low_state = state[...].astype(bf16)
        for g in range(QUADS):
            at = slice(g * QW, (g + 1) * QW)
            qb, kb, vb, gb, tb = q[here, at], k[here, at], v[here, at], gn[here, at], t[here, at]
            q_wide = qb.astype(f32)
            spread_q = spread_heads(qb, low_picks)
            spread_g = spread_heads(gb, low_picks)
            forward = spread_state(st[b * DH : (b + 1) * DH, at], low_picks)
            behind = spread_state(low_state[:, at], low_picks)
            scores = nt(gb, spread_heads(vb, low_picks)) + nt(tb, ones[0:512])
            scores = jnp.where(lower, scores, 0.0).astype(bf16)
            turned = nt(vb, spread_g) + nt(all_ones, spread_heads(tb, low_picks))
            turned = jnp.where(upper, turned, 0.0).astype(bf16)
            mixed = jnp.where(upper, nt(kb, spread_q), 0.0).astype(bf16)
            grad_denom = nn(tb, ones[512:768])
            grad_q = (
                nn(scores, spread_heads(kb, low_picks))
                + nt(gb, forward)
                + grad_denom * kt[b * 8 : b * 8 + 1, at]
            )
            grad_k = nn(turned, spread_q) + nt(vb, behind) + total[0:1, at]
            grad_v = nn(mixed, spread_g) + nn(kb, behind)
            grad_q = grad_q * jnp.minimum(q_wide, 1.0)
            grad_k = grad_k * jnp.minimum(kb.astype(f32), 1.0)
            for pair in range(2):
                two = slice(pair * 128, (pair + 1) * 128)
                swapped = pltpu.roll(grad_k[:, two], DH, 1)
                for j, piece in enumerate(
                    (
                        jnp.where(low_lane, grad_q[:, two], swapped),
                        jnp.where(low_lane, grad_v[:, two], grad_q[:, two]),
                        jnp.where(low_lane, swapped, grad_v[:, two]),
                    )
                ):
                    piece = piece.astype(bf16)
                    start = pair * 384 + j * 128
                    gp_out[g][here, start : start + 128] = piece
                    ba_sum[:, g * PW + start : g * PW + start + 128] += fold_rows(
                        piece.astype(f32)
                    )
            state[:, at] += gather_state(tn(qb, gb), picks)
            total[:, at] += jnp.sum(grad_denom * q_wide, axis=0, keepdims=True)


def input_kernel(x, gm, gain, *refs):
    gp, wa = refs[0:4], refs[4:8]
    out, sums = refs[8:10]

    @pl.when(pl.program_id(0) == 0)
    def _():
        sums[...] = jnp.zeros_like(sums)

    grad = nt(gp[0][...], wa[0][...])
    for g in range(1, QUADS):
        grad = grad + nt(gp[g][...], wa[g][...])
    xhat, inverse = centre(x[...].astype(f32))
    out[...] = gm[...] + norm_back(xhat, inverse, grad, gain[...])
    sums[0:8, :] += fold_rows(grad * xhat)
    sums[8:16, :] += fold_rows(grad)


def rows_spec(rows, columns):
    return pl.BlockSpec((rows, columns), lambda i, *_: (i, 0))


def back_spec(rows, columns, tiles):
    return pl.BlockSpec((rows, columns), lambda i, *_: (tiles - 1 - i, 0))


def whole_spec(shape):
    return pl.BlockSpec(shape, lambda i, *_: (0,) * len(shape), pipeline_mode=pl.Buffered(1))


def sum_spec(shape):
    return pl.BlockSpec(shape, lambda i, *_: (0,) * len(shape))


def grid_spec(scalars, tiles, in_specs, out_specs, scratch=()):
    return pltpu.PrefetchScalarGridSpec(
        num_scalar_prefetch=scalars,
        grid=(tiles,),
        in_specs=in_specs,
        out_specs=out_specs,
        scratch_shapes=list(scratch),
    )


def swap(value, axis, bit):
    size = lax.axis_size(axis)
    return lax.ppermute(value, axis, [(i, i ^ bit) for i in range(size)])


def bits_of(size):
    bit, bits = 1, []
    while bit < size:
        bits.append(bit)
        bit *= 2
    return bits


def gather_shards(own):
    size = lax.axis_size("head")
    held = {0: own}
    for bit in reversed(bits_of(size)):
        for k in list(held):
            held[k ^ bit] = swap(held[k], "head", bit)
    return [held[k] for k in range(size)]


def regroup(parts, count, axis):
    if len(parts) == count:
        return parts
    whole = jnp.concatenate(parts, axis=axis)
    width = whole.shape[axis] // count
    return [
        lax.slice_in_dim(whole, k * width, (k + 1) * width, axis=axis) for k in range(count)
    ]


def swap_state(mine, weights):
    size = lax.axis_size("head")
    sent = mine.astype(bf16)
    total = None
    for j in range(1, size):
        got = swap(sent, "head", j)
        slots = jnp.split(got, size, axis=1)
        got = jnp.concatenate([slots[k ^ j] for k in range(size)], axis=1).astype(f32)
        got = got * weights[j]
        total = got if total is None else total + got
    return total


def scatter_head(parts):
    held = dict(enumerate(parts))
    for bit in bits_of(len(parts)):
        for k in [k for k in held if k & bit]:
            got = swap(held.pop(k).astype(bf16), "head", bit)
            held[k ^ bit] = held[k ^ bit].astype(f32) + got.astype(f32)
    return held[0]


def sum_groups(value):
    size = lax.axis_size("dp")
    me = lax.axis_index("dp")
    bits = bits_of(size)
    value = value.astype(bf16)
    for bit in bits:
        half = value.shape[0] // 2
        mine = jnp.where((me & bit) != 0, 1, 0)
        sent = lax.dynamic_slice_in_dim(value, (1 - mine) * half, half, 0)
        kept = lax.dynamic_slice_in_dim(value, mine * half, half, 0)
        got = swap(sent, "dp", bit)
        value = (kept.astype(f32) + got.astype(f32)).astype(bf16)
    for bit in reversed(bits):
        got = swap(value, "dp", bit)
        upper = (me & bit) != 0
        value = jnp.concatenate(
            [jnp.where(upper, got, value), jnp.where(upper, value, got)], axis=0
        )
    return value.astype(f32)


def sum_small(shared, split):
    size = len(split)
    held = dict(enumerate(split))
    flat = shared.reshape(-1)
    for bit in bits_of(size):
        gone = [k for k in held if k & bit]
        sent = jnp.concatenate([flat] + [held[k] for k in gone])
        got = swap(sent, "head", bit)
        flat = flat + got[: flat.shape[0]]
        at = flat.shape[0]
        for k in gone:
            width = held[k].shape[0]
            held[k ^ bit] = held[k ^ bit] + got[at : at + width]
            del held[k]
            at += width
    both = jnp.concatenate([flat, held[0]])
    for bit in bits_of(lax.axis_size("dp")):
        both = both + swap(both, "dp", bit)
    return both[: flat.shape[0]].reshape(shared.shape), both[flat.shape[0] :]


def on_device(
    layer_input,
    cotangent,
    crop_blocks,
    crop_padding,
    first_gain,
    first_shift,
    attend_weight,
    attend_bias,
    output_weight,
    output_bias,
    second_gain,
    second_shift,
    expand_weight,
    expand_bias,
    reduce_weight,
    reduce_bias,
):
    R = layer_input.shape[0]
    n = lax.axis_size("head")
    me = lax.axis_index("head")
    nb = R // STRETCH
    FF = expand_weight.shape[1] * n

    wa_all = gather_shards(attend_weight)
    ba_all = gather_shards(attend_bias)
    wo_all = gather_shards(output_weight)
    we_all = gather_shards(expand_weight)
    wr_all = gather_shards(reduce_weight)
    be_all = gather_shards(expand_bias)
    wa = regroup(wa_all, QUADS, 1)
    wo = regroup(wo_all, QUADS, 0)
    we = regroup(we_all, QUADS, 1)
    wr = regroup(wr_all, QUADS, 0)
    ba = jnp.concatenate(ba_all)[None, :]
    be = jnp.concatenate(be_all)[None, :]

    sizes, pads = crop_blocks[0], crop_padding[0]
    crops = sizes.shape[0]
    closing = jnp.sum(jnp.tril(jnp.ones((crops, crops), jnp.int32)) * sizes[None, :], axis=1)

    def crop_of(position):
        return jnp.sum((position[..., None] >= closing).astype(jnp.int32), axis=-1)

    spots = me * nb + jnp.arange(nb, dtype=jnp.int32)
    crop = crop_of(spots)
    belongs = crop[:, None] == jnp.arange(crops, dtype=jnp.int32)[None, :]
    opening = jnp.sum(jnp.where(belongs, (closing - sizes)[None, :], 0), axis=1)
    padding = jnp.sum(jnp.where(belongs, pads[None, :], 0), axis=1)
    thr = jnp.maximum(padding - (spots - opening) * STRETCH, 0).astype(jnp.int32)
    first = (crop == crop[0]).astype(jnp.int32)
    last = (crop == crop[nb - 1]).astype(jnp.int32)
    one = jnp.ones((1,), jnp.int32)
    cont = jnp.concatenate([one, (crop[1:] == crop[:-1]).astype(jnp.int32), one])
    others = me ^ jnp.arange(n, dtype=jnp.int32)
    opens = crop_of(others * nb)
    closes = crop_of(others * nb + nb - 1)
    before = jnp.logical_and(others < me, closes == crop[0]).astype(f32)
    after = jnp.logical_and(others > me, opens == crop[nb - 1]).astype(f32)

    line = lax.broadcasted_iota(jnp.int32, (768, QW), 0)
    lane_head = lax.broadcasted_iota(jnp.int32, (768, QW), 1) // DH
    ones = (jnp.where(line < 512, line // STRETCH, (line - 512) // DH) == lane_head).astype(bf16)

    blocks = 2 if nb % 2 == 0 else 1
    rows = blocks * STRETCH
    tiles = R // rows
    vec = whole_spec((1, D))
    gain1, shift1 = first_gain[None, :], first_shift[None, :]
    gain2, shift2 = second_gain[None, :], second_shift[None, :]
    like = jax.ShapeDtypeStruct
    low = like((R, D), bf16)
    wide = like((R, D), f32)
    state_shape = (DH + 8, D)

    q, k, v, normed, trailing = pl.pallas_call(
        functools.partial(qkv_kernel, blocks),
        grid_spec=grid_spec(
            2,
            tiles,
            [rows_spec(rows, D), vec, vec]
            + [whole_spec((D, PW))] * 4
            + [whole_spec((1, 3 * D))],
            [rows_spec(rows, D)] * 4 + [sum_spec(state_shape)],
        ),
        out_shape=[low] * 4 + [like(state_shape, f32)],
        compiler_params=params(),
        cost_estimate=cost(2 * R * D * 3 * D, 10 * R * D + 6 * D * D),
        name="qkv",
    )(thr, last, layer_input, gain1, shift1, *wa, ba)

    s_in = swap_state(trailing, before)

    att, rec, st, kt, middle, n2 = pl.pallas_call(
        functools.partial(attend_tile, blocks),
        grid_spec=grid_spec(
            2,
            tiles,
            [rows_spec(rows, D)] * 4
            + [whole_spec(state_shape), whole_spec((768, QW)), vec, vec, vec]
            + [whole_spec((QW, D))] * 4,
            [
                rows_spec(rows, D),
                rows_spec(rows, D),
                rows_spec(blocks * DH, D),
                rows_spec(blocks * 8, D),
                rows_spec(rows, D),
                rows_spec(rows, D),
            ],
            [pltpu.VMEM((DH, D), f32), pltpu.VMEM((8, D), f32)],
        ),
        out_shape=[low, wide, like((nb * DH, D), bf16), like((nb * 8, D), f32), wide, low],
        compiler_params=params(),
        cost_estimate=cost(6 * R * D * D, 20 * R * D),
        name="attend",
    )(cont, thr, q, k, v, layer_input, s_in, ones, output_bias[None, :], gain2, shift2, *wo)

    results = pl.pallas_call(
        functools.partial(ffn_kernel, blocks),
        grid_spec=grid_spec(
            1,
            tiles,
            [rows_spec(rows, D)] * 6
            + [vec, whole_spec((1, FF)), vec, whole_spec((768, QW))]
            + [whole_spec((D, FF // 4))] * 4
            + [whole_spec((FF // 4, D))] * 4
            + [whole_spec((QW, D))] * 4,
            [rows_spec(rows, FF // 4)] * 8
            + [rows_spec(rows, D)] * 5
            + [sum_spec(state_shape), sum_spec((32, D)), sum_spec((8, FF))],
        ),
        out_shape=[like((R, FF // 4), bf16)] * 8
        + [low, wide, low, low, low]
        + [like(state_shape, f32), like((32, D), f32), like((8, FF), f32)],
        compiler_params=params(),
        cost_estimate=cost(8 * R * D * FF + 2 * R * D * D, 40 * R * D),
        name="ffn",
    )(
        first, n2, cotangent, middle, att, rec, q, gain2, be, reduce_bias[None, :], ones,
        *we, *wr, *wo,
    )
    act, gh = results[0:4], results[4:8]
    layer_output, grad_middle, branch, gn, t, leading, sums2, be_sum = results[8:]

    g_in = swap_state(leading, after)

    reduce_grads = regroup([tn(a, cotangent) for a in act], n, 0)
    expand_grads = regroup([tn(n2, g) for g in gh], n, 1)
    reduce_weight_grad = sum_groups(scatter_head(reduce_grads))
    expand_weight_grad = sum_groups(scatter_head(expand_grads))

    gp_and_sum = pl.pallas_call(
        functools.partial(back_kernel, blocks, tiles),
        grid_spec=grid_spec(
            1,
            tiles,
            [back_spec(rows, D, tiles)] * 5
            + [back_spec(blocks * DH, D, tiles), back_spec(blocks * 8, D, tiles)]
            + [whole_spec(state_shape), whole_spec((768, QW))],
            [back_spec(rows, PW, tiles)] * 4 + [sum_spec((8, 3 * D))],
            [pltpu.VMEM((DH, D), f32), pltpu.VMEM((8, D), f32)],
        ),
        out_shape=[like((R, PW), bf16)] * 4 + [like((8, 3 * D), f32)],
        compiler_params=params(),
        cost_estimate=cost(8 * R * D * D, 18 * R * D),
        name="attend_back",
    )(cont, q, k, v, gn, t, st, kt, g_in, ones)
    gp, ba_sum = gp_and_sum[0:4], gp_and_sum[4]

    out_grads = regroup([tn(att, branch)], n, 0)
    output_weight_grad = sum_groups(scatter_head(out_grads))
    attend_grads = regroup([tn(normed, g) for g in gp], n, 1)
    attend_weight_grad = sum_groups(scatter_head(attend_grads))

    input_grad, sums1 = pl.pallas_call(
        input_kernel,
        grid_spec=grid_spec(
            0,
            tiles,
            [rows_spec(rows, D)] * 2
            + [vec]
            + [rows_spec(rows, PW)] * 4
            + [whole_spec((D, PW))] * 4,
            [rows_spec(rows, D), sum_spec((16, D))],
        ),
        out_shape=[wide, like((16, D), f32)],
        compiler_params=params(),
        cost_estimate=cost(2 * R * D * 3 * D, 16 * R * D),
        name="input_grad",
    )(layer_input, grad_middle, gain1, *gp, *wa)

    shared2, expand_bias_grad = sum_small(
        jnp.sum(sums2.reshape(4, 8, D), axis=1), regroup([jnp.sum(be_sum, axis=0)], n, 0)
    )
    shared1, attend_bias_grad = sum_small(
        jnp.sum(sums1.reshape(2, 8, D), axis=1), regroup([jnp.sum(ba_sum, axis=0)], n, 0)
    )
    return (
        layer_output,
        input_grad,
        shared1[0],
        shared1[1],
        attend_weight_grad,
        attend_bias_grad,
        output_weight_grad,
        shared2[0],
        shared2[1],
        shared2[2],
        expand_weight_grad,
        expand_bias_grad,
        reduce_weight_grad,
        shared2[3],
    )


def solution(mesh):
    in_specs = (
        P(("dp", "head"), None),
        P(("dp", "head"), None),
        P("dp", None),
        P("dp", None),
        P(),
        P(),
        P(None, "head"),
        P("head"),
        P("head", None),
        P(),
        P(),
        P(),
        P(None, "head"),
        P("head"),
        P("head", None),
        P(),
    )
    out_specs = (
        P(("dp", "head"), None),
        P(("dp", "head"), None),
        P(),
        P(),
        P(None, "head"),
        P("head"),
        P("head", None),
        P(),
        P(),
        P(),
        P(None, "head"),
        P("head"),
        P("head", None),
        P(),
    )
    return jax.shard_map(
        on_device, mesh=mesh, in_specs=in_specs, out_specs=out_specs, check_vma=False
    )
```

time: 2190 us -> 855 us (0.39)
  waiting for transfers between devices: 1110 us -> 329 us
  matrix products: 600 us -> 100 us
  Pallas kernels: 0 us -> 296 us
  local copies, waits for them, and re-layouts: 202 us -> 5.82 us
  other arithmetic: 192 us -> 34.7 us
  starting transfers between devices: 0.54 us -> 79.4 us
  blocking collectives: 59.4 us -> 0 us
    reduce_scatter x4 -> x0, waiting for transfers between devices: 519 us -> none  [the longest x1 153 us: on_device(): lax.psum_scatter(jnp.dot(block_rows, output_weight, preferred_element_typ...]
    dot_general x26 -> x13, matrix products: 579 us -> 100 us  [tn(): lax.dot_general(a, b, (((0,), (0,)), ((), ())), preferred_element_type=f32)]
    all_gather x4 -> x0, waiting for transfers between devices: 438 us -> none  [the longest x1 132 us: on_device(): normed = lax.all_gather(normed_low, 'head', axis=0, tiled=True)]
    ppermute x0 -> x70, waiting for transfers between devices: none -> 329 us  [swap(): return lax.ppermute(value, axis, [(i, i ^ bit) for i in range(size)])]
    pallas_call x0 -> x5, Pallas kernels: none -> 296 us  [the longest x1 139 us: on_device(): pl.pallas_call(functools.partial(ffn_kernel, blocks), grid_spec=grid_spec...]
    psum x1 -> x0, waiting for transfers between devices: 154 us -> none  [on_device(): lax.psum(attend_weight_grad.astype(jnp.bfloat16), 'dp').astype(jnp.float32)]
    reduce_sum x14 -> x8, other arithmetic: 118 us -> 2.79 us  [the longest x1 0.87 us: on_device(): jnp.sum(sums1.reshape(2, 8, D), axis=1)]
    convert_element_type x6 -> x0, local copies, waits for them, and re-layouts: 103 us -> none  [the longest x2 38.3 us: attention_start(): grad_numer = (keep * grad_attended / floor[..., None]).astype(jnp.bfloat16)]
  transfers between devices with their start and end apart: 9 -> 70, of which waited for: 9 -> 26; matrix products, arithmetic and copies ran while one was open for 10% -> 16% of each run, Pallas kernels for 0% -> 19%
where the time goes in v1:
time: 855 us; the launch traced here: 847 us
  waiting for transfers between devices  329 us (38%)
  Pallas kernels  296 us (35%)
  matrix products  100 us (12%)
  starting transfers between devices  79.4 us (9%)
  other arithmetic  34.7 us (4%)
    ppermute x70, waiting for transfers between devices, swap(): return lax.ppermute(value, axis, [(i, i ^ bit) for i in range(size)])  329 us
    pallas_call x1, Pallas kernels, on_device(): pl.pallas_call(functools.partial(ffn_kernel, blocks), grid_spec=grid_spec...  139 us
    dot_general x13, matrix products, tn(): lax.dot_general(a, b, (((0,), (0,)), ((), ())), preferred_element_type=f32)  100 us
    ppermute x70, starting transfers between devices, swap(): return lax.ppermute(value, axis, [(i, i ^ bit) for i in range(size)])  79.4 us
    pallas_call x1, Pallas kernels, on_device(): pl.pallas_call(functools.partial(back_kernel, blocks, tiles), grid_spec=g...  59.3 us
    pallas_call x1, Pallas kernels, on_device(): pl.pallas_call(functools.partial(attend_tile, blocks), grid_spec=grid_spe...  37.6 us
    pallas_call x1, Pallas kernels, on_device(): pl.pallas_call(functools.partial(qkv_kernel, blocks), grid_spec=grid_spec...  33 us
    pallas_call x1, Pallas kernels, on_device(): pl.pallas_call(input_kernel, grid_spec=grid_spec(0, tiles, [rows_spec(row...  27.6 us
  transfers between devices with their start and end apart: 70, of which 26 were waited for; matrix products, arithmetic and copies ran while one was open for 16% of the time, Pallas kernels for 19%

profile of v1, /device:TPU:8, one launch (start us, length us, event | category | flops | bytes accessed | tf_op | source)
XLA Modules:
  0.0 847.4 jit_solution(15730392451573700522)
XLA Ops:
  7.6 32.0 %collective-permute-done.1.refs_2_.refs_6_ = bf16[1024,768]{1,0:T(8,128)(2,1)S(1)} collective-permute-done((bf16[1024,768]{1,0:T(8,128)(2,1)}, bf16[1024,768]{1,0:T(8,128)(2,1)S(1)}, u32[]{:S(2)}, u32[]{:S(2)}) %collective-permute-start.1) | collective-permute-done | bytes 1572896 | tf_op jit(solution)/shard_map/ppermute | solution.py:393
  48.1 81.1 %collective-permute-done.13 = f32[1024]{0:T(1024)S(1)} collective-permute-done((f32[1024]{0:T(1024)}, f32[1024]{0:T(1024)S(1)}, u32[]{:S(2)}, u32[]{:S(2)}) %collective-permute-start.13) | collective-permute-done | bytes 4128 | tf_op jit(solution)/shard_map/ppermute | solution.py:393
  133.6 33.0 %qkv.1 = (bf16[2560,1024]{1,0:T(8,128)(2,1)}, bf16[2560,1024]{1,0:T(8,128)(2,1)}, bf16[2560,1024]{1,0:T(8,128)(2,1)}, bf16[2560,1024]{1,0:T(8,128)(2,1)}, f32[72,1024]{1,0:T(8,128)}) custom-call(s32[20]{0:T(128)} %subtract_maximum_fusion.thr, s32[20]{0:T(128)} %get-tuple-element.149.last, bf16[2560,1024]{1,0:T(8,128)(2,1)} %x.3, f32[1,1024]{1,0:T(1,128)} %bitcast.83, ...), custom_call_target="tpu_custom_call" | custom-call | flops 16106127360 | bytes 32505856 | tf_op jit(solution)/shard_map/qkv/pallas_call | solution.py:562
  184.0 37.6 %attend.1 = (bf16[2560,1024]{1,0:T(8,128)(2,1)}, f32[2560,1024]{1,0:T(8,128)}, bf16[1280,1024]{1,0:T(8,128)(2,1)}, f32[160,1024]{1,0:T(8,128)}, f32[2560,1024]{1,0:T(8,128)}, /*index=5*/bf16[2560,1024]{1,0:T(8,128)(2,1)}) custom-call(s32[21]{0:T(128)} %add_convert_fusion.18.cont, s32[20]{0:T(128)} %subtract_maximum_fusion.thr, ...), custom_call_target="tpu_custom_call" | custom-call | flops 16106127360 | bytes 52428800 | tf_op jit(solution)/shard_map/attend/pallas_call | solution.py:580
  221.6 138.7 %ffn.1 = (bf16[2560,1024]{1,0:T(8,128)(2,1)}, bf16[2560,1024]{1,0:T(8,128)(2,1)}, bf16[2560,1024]{1,0:T(8,128)(2,1)}, bf16[2560,1024]{1,0:T(8,128)(2,1)}, bf16[2...) custom-call(s32[20]{0:T(128)} %get-tuple-element.150.first, ...), custom_call_target="tpu_custom_call" | custom-call | flops 91268055040 | bytes 104857600 | tf_op jit(solution)/shard_map/ffn/pallas_call | solution.py:604
  370.2 10.2 %convolution_convert_fusion = bf16[1024,1024]{1,0:T(8,128)(2,1)} fusion(bf16[2560,1024]{1,0:T(8,128)(2,1)} %get-tuple-element.81, bf16[2560,1024]{1,0:T(8,128)(2,1)} %cot.1), kind=kOutput, calls=%fused_computation.10 | convolution fusion | flops 5369757696 | bytes 12582912 | tf_op jit(solution)/shard_map/dot_general | solution.py:32
  381.1 10.3 %convolution_convert_fusion.1 = bf16[1024,1024]{1,0:T(8,128)(2,1)} fusion(bf16[2560,1024]{1,0:T(8,128)(2,1)} %get-tuple-element.79, bf16[2560,1024]{1,0:T(8,128)(2,1)} %cot.1), kind=kOutput, calls=%fused_computation.11 | convolution fusion | flops 5369757696 | bytes 12582912 | tf_op jit(solution)/shard_map/dot_general | solution.py:32
  393.2 9.6 %convolution_convert_fusion.2 = bf16[1024,1024]{1,0:T(8,128)(2,1)} fusion(bf16[2560,1024]{1,0:T(8,128)(2,1)} %get-tuple-element.52.n2, bf16[2560,1024]{1,0:T(8,128)(2,1)S(1)} %copy-done.15), kind=kOutput, calls=%fused_computation.12 | convolution fusion | flops 5369757696 | bytes 12582912 | tf_op jit(solution)/shard_map/dot_general | solution.py:32
  424.9 59.3 %attend_back.1 = (bf16[2560,768]{1,0:T(8,128)(2,1)}, bf16[2560,768]{1,0:T(8,128)(2,1)}, bf16[2560,768]{1,0:T(8,128)(2,1)}, bf16[2560,768]{1,0:T(8,128)(2,1)}, f32[8,3072]{1,0:T(8,128)}) custom-call(s32[21]{0:T(128)} %add_convert_fusion.18.cont, bf16[2560,1024]{1,0:T(8,128)(2,1)} %get-tuple-element.48.refs_0_.q, ...), custom_call_target="tpu_custom_call" | custom-call | flops 21474836480 | bytes 47185920 | tf_op jit(solution)/shard_map/attend_back/pallas_call | solution.py:638
  484.3 27.6 %input_grad.1 = (f32[2560,1024]{1,0:T(8,128)}, f32[16,1024]{1,0:T(8,128)}) custom-call(bf16[2560,1024]{1,0:T(8,128)(2,1)} %x.3, f32[2560,1024]{1,0:T(8,128)} %get-tuple-element.57.gm, f32[1,1024]{1,0:T(1,128)} %bitcast.84, bf16[2560,768]{1,0:T(8,128)(2,1)} %get-tuple-element.63.refs_0_, bf16[2560,768]{1,0:T(8,128)(2,1)} %get-tuple-element.64.refs_1_, ...), custom_call_target="tpu_custom_call" | custom-call | flops 16106127360 | bytes 41943040 | tf_op jit(solution)/shard_map/input_grad/pallas_call | solution.py:661
  518.9 11.8 %collective-permute-done.40 = bf16[256,1024]{1,0:T(8,128)(2,1)S(1)} collective-permute-done((bf16[256,1024]{1,0:T(8,128)(2,1)S(1)}, bf16[256,1024]{1,0:T(8,128)(2,1)S(1)}, u32[]{:S(2)}, u32[]{:S(2)}) %collective-permute-start.40) | collective-permute-done | bytes 524320 | tf_op jit(solution)/shard_map/ppermute | solution.py:393
  568.8 8.9 %add_convert_fusion.1 = bf16[1024,1024]{1,0:T(8,128)(2,1)S(1)} fusion(bf16[1024,1024]{1,0:T(8,128)(2,1)} %collective-permute-done.62, bf16[2560,1024]{1,0:T(8,128)(2,1)} %get-tuple-element.80, bf16[2560,1024]{1,0:T(8,128)(2,1)S(1)} %bitcast.76), kind=kOutput, calls=%fused_computation.1 | convolution fusion | flops 5371854848 | bytes 14680064 | tf_op jit(solution)/shard_map/dot_general | solution.py:32
  579.7 25.1 %collective-permute-done.31 = bf16[1024,768]{1,0:T(8,128)(2,1)S(1)} collective-permute-done((bf16[1024,768]{1,0:T(8,128)(2,1)S(1)}, bf16[1024,768]{1,0:T(8,128)(2,1)S(1)}, u32[]{:S(2)}, u32[]{:S(2)}) %collective-permute-start.31) | collective-permute-done | bytes 1572896 | tf_op jit(solution)/shard_map/ppermute | solution.py:393
  610.4 10.1 %add_convert_fusion.3 = bf16[1024,1024]{1,0:T(8,128)(2,1)S(1)} fusion(bf16[1024,1024]{1,0:T(8,128)(2,1)S(1)} %collective-permute-done.53, bf16[2560,1024]{1,0:T(8,128)(2,1)} %get-tuple-element.52.n2, bf16[2560,1024]{1,0:T(8,128)(2,1)} %get-tuple-element.76), kind=kOutput, calls=%fused_computation.3 | convolution fusion | flops 5371854848 | bytes 14680064 | tf_op jit(solution)/shard_map/dot_general | solution.py:32
  631.2 22.1 %collective-permute-done.63 = bf16[1024,1024]{1,0:T(8,128)(2,1)S(1)} collective-permute-done((bf16[1024,1024]{1,0:T(8,128)(2,1)S(1)}, bf16[1024,1024]{1,0:T(8,128)(2,1)S(1)}, u32[]{:S(2)}, u32[]{:S(2)}) %collective-permute-start.63) | collective-permute-done | bytes 2097184 | tf_op jit(solution)/shard_map/ppermute | solution.py:393
  653.3 8.9 %add_convert_fusion = bf16[1024,1024]{1,0:T(8,128)(2,1)S(1)} fusion(bf16[1024,1024]{1,0:T(8,128)(2,1)S(1)} %collective-permute-done.63, bf16[1024,1024]{1,0:T(8,128)(2,1)} %collective-permute-done.61, bf16[2560,1024]{1,0:T(8,128)(2,1)} %get-tuple-element.78, bf16[2560,1024]{1,0:T(8,128)(2,1)S(1)} %bitcast.76), kind=kOutput, calls=%fused_computation | convolution fusion | flops 5373952000 | bytes 16777216 | tf_op jit(solution)/shard_map/dot_general | solution.py:32
  662.8 33.6 %collective-permute-done.54 = bf16[1024,1024]{1,0:T(8,128)(2,1)S(1)} collective-permute-done((bf16[1024,1024]{1,0:T(8,128)(2,1)S(1)}, bf16[1024,1024]{1,0:T(8,128)(2,1)S(1)}, u32[]{:S(2)}, u32[]{:S(2)}) %collective-permute-start.54) | collective-permute-done | bytes 2097184 | tf_op jit(solution)/shard_map/ppermute | solution.py:393
  715.7 13.2 %collective-permute-done.55 = bf16[512,1024]{1,0:T(8,128)(2,1)S(1)} collective-permute-done((bf16[512,1024]{1,0:T(8,128)(2,1)S(1)}, bf16[512,1024]{1,0:T(8,128)(2,1)S(1)}, u32[]{:S(2)}, u32[]{:S(2)}) %collective-permute-start.55) | collective-permute-done | bytes 1048608 | tf_op jit(solution)/shard_map/ppermute | solution.py:393
  735.7 11.8 %collective-permute-done.56 = bf16[256,1024]{1,0:T(8,128)(2,1)S(1)} collective-permute-done((bf16[256,1024]{1,0:T(8,128)(2,1)S(1)}, bf16[256,1024]{1,0:T(8,128)(2,1)S(1)}, u32[]{:S(2)}, u32[]{:S(2)}) %collective-permute-start.56) | collective-permute-done | bytes 524320 | tf_op jit(solution)/shard_map/ppermute | solution.py:393
  753.4 12.1 %collective-permute-done.57 = bf16[128,1024]{1,0:T(8,128)(2,1)S(1)} collective-permute-done((bf16[128,1024]{1,0:T(8,128)(2,1)S(1)}, bf16[128,1024]{1,0:T(8,128)(2,1)S(1)}, u32[]{:S(2)}, u32[]{:S(2)}) %collective-permute-start.57) | collective-permute-done | bytes 262176 | tf_op jit(solution)/shard_map/ppermute | solution.py:393
  785.2 8.6 %collective-permute-done.68 = bf16[256,1024]{1,0:T(8,128)(2,1)S(1)} collective-permute-done((bf16[256,1024]{1,0:T(8,128)(2,1)S(1)}, bf16[256,1024]{1,0:T(8,128)(2,1)S(1)}, u32[]{:S(2)}, u32[]{:S(2)}) %collective-permute-start.68) | collective-permute-done | bytes 524320 | tf_op jit(solution)/shard_map/ppermute | solution.py:393
  796.3 8.6 %collective-permute-done.59 = bf16[256,1024]{1,0:T(8,128)(2,1)S(1)} collective-permute-done((bf16[256,1024]{1,0:T(8,128)(2,1)S(1)}, bf16[256,1024]{1,0:T(8,128)(2,1)S(1)}, u32[]{:S(2)}, u32[]{:S(2)}) %collective-permute-start.59) | collective-permute-done | bytes 524320 | tf_op jit(solution)/shard_map/ppermute | solution.py:393
  810.6 12.1 %collective-permute-done.69 = bf16[512,1024]{1,0:T(8,128)(2,1)S(1)} collective-permute-done((bf16[512,1024]{1,0:T(8,128)(2,1)S(1)}, bf16[512,1024]{1,0:T(8,128)(2,1)S(1)}, u32[]{:S(2)}, u32[]{:S(2)}) %collective-permute-start.69) | collective-permute-done | bytes 1048608 | tf_op jit(solution)/shard_map/ppermute | solution.py:393
  825.7 18.4 %collective-permute-done.60 = bf16[512,1024]{1,0:T(8,128)(2,1)S(1)} collective-permute-done((bf16[512,1024]{1,0:T(8,128)(2,1)S(1)}, bf16[512,1024]{1,0:T(8,128)(2,1)S(1)}, u32[]{:S(2)}, u32[]{:S(2)}) %collective-permute-start.60) | collective-permute-done | bytes 1048608 | tf_op jit(solution)/shard_map/ppermute | solution.py:393
  (323 shorter events, 200.5 us)
Async XLA Ops:
  0.6 44.8 %collective-permute-start.4 = (f32[768]{0:T(1024)}, f32[768]{0:T(1024)S(1)}, u32[]{:S(2)}, u32[]{:S(2)}) collective-permute-start(f32[768]{0:T(1024)} %param.23), channel_id=1, source_target_pairs={{0,2},{1,3},{2,0},{3,1},{4,6},{5,7},{6,4},{7,5},{8,10},{9,11},{10,... | collective-permute-start | bytes 9224 | tf_op jit(solution)/shard_map/ppermute | solution.py:393
  2.7 129.7 %collective-permute-start = (bf16[1024,768]{1,0:T(8,128)(2,1)}, bf16[1024,768]{1,0:T(8,128)(2,1)}, u32[]{:S(2)}, u32[]{:S(2)}) collective-permute-start(bf16[1024,768]{1,0:T(8,128)(2,1)} %refs_4_.3), channel_id=1, source_target_pairs={{0,1},{1,0},{2,3},{3,2},{4,5},{5,4},{6,7},{7,6},{8,9},{9,8},{10,11... | collective-permute-start | bytes 4718600 | tf_op jit(solution)/shard_map/ppermute | solution.py:393
  3.0 168.7 %collective-permute-start.16 = (bf16[1024,1024]{1,0:T(8,128)(2,1)}, bf16[1024,1024]{1,0:T(8,128)(2,1)}, u32[]{:S(2)}, u32[]{:S(2)}) collective-permute-start(bf16[1024,1024]{1,0:T(8,128)(2,1)} %refs_0_.3), channel_id=1, source_target_pairs={{0,2},{1,3},{2,0},{3,1},{4,6},{5,7},{6,4},{7,5},{8,10},{9,11},{10,... | collective-permute-start | bytes 6291464 | tf_op jit(solution)/shard_map/ppermute | solution.py:393
  39.6 92.9 %collective-permute-start.2 = (bf16[1024,768]{1,0:T(8,128)(2,1)S(1)}, bf16[1024,768]{1,0:T(8,128)(2,1)S(1)}, u32[]{:S(2)}, u32[]{:S(2)}) collective-permute-start(bf16[1024,768]{1,0:T(8,128)(2,1)S(1)} %collective-permute-done.1.refs_2_.refs_6_), channel_id=1, source_target_pairs={{0,1},{1,0},{2,3},{3,2},{4,5},{5,4},{6,7},{7,6},{8,9},{9,8},{10,11... | collective-permute-start | bytes 4718600 | tf_op jit(solution)/shard_map/ppermute | solution.py:393
  45.4 126.6 %collective-permute-start.19 = (bf16[1024,1024]{1,0:T(8,128)(2,1)}, bf16[1024,1024]{1,0:T(8,128)(2,1)}, u32[]{:S(2)}, u32[]{:S(2)}) collective-permute-start(bf16[1024,1024]{1,0:T(8,128)(2,1)} %refs_4_.2), channel_id=1, source_target_pairs={{0,2},{1,3},{2,0},{3,1},{4,6},{5,7},{6,4},{7,5},{8,10},{9,11},{10,... | collective-permute-start | bytes 6291464 | tf_op jit(solution)/shard_map/ppermute | solution.py:393
  46.0 83.3 %collective-permute-start.13 = (f32[1024]{0:T(1024)}, f32[1024]{0:T(1024)S(1)}, u32[]{:S(2)}, u32[]{:S(2)}) collective-permute-start(f32[1024]{0:T(1024)} %param.29), channel_id=1, source_target_pairs={{0,2},{1,3},{2,0},{3,1},{4,6},{5,7},{6,4},{7,5},{8,10},{9,11},{10,... | collective-permute-start | bytes 12296 | tf_op jit(solution)/shard_map/ppermute | solution.py:393
  171.5 50.0 %collective-permute-start.15 = (bf16[1024,1024]{1,0:T(8,128)(2,1)S(1)}, bf16[1024,1024]{1,0:T(8,128)(2,1)}, u32[]{:S(2)}, u32[]{:S(2)}) collective-permute-start(bf16[1024,1024]{1,0:T(8,128)(2,1)S(1)} %copy-done.4), channel_id=1, source_target_pairs={{0,1},{1,0},{2,3},{3,2},{4,5},{5,4},{6,7},{7,6},{8,9},{9,8},{10,11... | collective-permute-start | bytes 6291464 | tf_op jit(solution)/shard_map/ppermute | solution.py:393
  171.6 49.9 %collective-permute-start.18 = (bf16[1024,1024]{1,0:T(8,128)(2,1)}, bf16[1024,1024]{1,0:T(8,128)(2,1)}, u32[]{:S(2)}, u32[]{:S(2)}) collective-permute-start(bf16[1024,1024]{1,0:T(8,128)(2,1)} %refs_4_.2), channel_id=1, source_target_pairs={{0,1},{1,0},{2,3},{3,2},{4,5},{5,4},{6,7},{7,6},{8,9},{9,8},{10,11... | collective-permute-start | bytes 6291464 | tf_op jit(solution)/shard_map/ppermute | solution.py:393
  172.1 49.5 %collective-permute-start.17 = (bf16[1024,1024]{1,0:T(8,128)(2,1)}, bf16[1024,1024]{1,0:T(8,128)(2,1)}, u32[]{:S(2)}, u32[]{:S(2)}) collective-permute-start(bf16[1024,1024]{1,0:T(8,128)(2,1)} %collective-permute-done.16.refs_2_), channel_id=1, source_target_pairs={{0,1},{1,0},{2,3},{3,2},{4,5},{5,4},{6,7},{7,6},{8,9},{9,8},{10,11... | collective-permute-start | bytes 6291464 | tf_op jit(solution)/shard_map/ppermute | solution.py:393
  172.9 48.7 %collective-permute-start.20 = (bf16[1024,1024]{1,0:T(8,128)(2,1)}, bf16[1024,1024]{1,0:T(8,128)(2,1)}, u32[]{:S(2)}, u32[]{:S(2)}) collective-permute-start(bf16[1024,1024]{1,0:T(8,128)(2,1)} %collective-permute-done.19.refs_6_), channel_id=1, source_target_pairs={{0,1},{1,0},{2,3},{3,2},{4,5},{5,4},{6,7},{7,6},{8,9},{9,8},{10,11... | collective-permute-start | bytes 6291464 | tf_op jit(solution)/shard_map/ppermute | solution.py:393
  361.3 60.9 %collective-permute-start.23 = (bf16[72,1024]{1,0:T(8,128)(2,1)S(1)}, bf16[72,1024]{1,0:T(8,128)(2,1)S(1)}, u32[]{:S(2)}, u32[]{:S(2)}) collective-permute-start(bf16[72,1024]{1,0:T(8,128)(2,1)S(1)} %convert_element_type.263), channel_id=1, source_target_pairs={{0,3},{1,2},{2,1},{3,0},{4,7},{5,6},{6,5},{7,4},{8,11},{9,10},{10,... | collective-permute-start | bytes 442376 | tf_op jit(solution)/shard_map/ppermute | solution.py:393
  368.3 50.9 %collective-permute-start.22 = (bf16[72,1024]{1,0:T(8,128)(2,1)S(1)}, bf16[72,1024]{1,0:T(8,128)(2,1)S(1)}, u32[]{:S(2)}, u32[]{:S(2)}) collective-permute-start(bf16[72,1024]{1,0:T(8,128)(2,1)S(1)} %convert_element_type.263), channel_id=1, source_target_pairs={{0,2},{1,3},{2,0},{3,1},{4,6},{5,7},{6,4},{7,5},{8,10},{9,11},{10,... | collective-permute-start | bytes 442376 | tf_op jit(solution)/shard_map/ppermute | solution.py:393
  370.1 52.2 %collective-permute-start.21 = (bf16[72,1024]{1,0:T(8,128)(2,1)S(1)}, bf16[72,1024]{1,0:T(8,128)(2,1)S(1)}, u32[]{:S(2)}, u32[]{:S(2)}) collective-permute-start(bf16[72,1024]{1,0:T(8,128)(2,1)S(1)} %convert_element_type.263), channel_id=1, source_target_pairs={{0,1},{1,0},{2,3},{3,2},{4,5},{5,4},{6,7},{7,6},{8,9},{9,8},{10,11... | collective-permute-start | bytes 442376 | tf_op jit(solution)/shard_map/ppermute | solution.py:393
  380.3 188.0 %collective-permute-start.62 = (bf16[1024,1024]{1,0:T(8,128)(2,1)}, bf16[1024,1024]{1,0:T(8,128)(2,1)}, u32[]{:S(2)}, u32[]{:S(2)}) collective-permute-start(bf16[1024,1024]{1,0:T(8,128)(2,1)} %convolution_convert_fusion), channel_id=1, source_target_pairs={{0,1},{1,0},{2,3},{3,2},{4,5},{5,4},{6,7},{7,6},{8,9},{9,8},{10,11... | collective-permute-start | bytes 6291464 | tf_op jit(solution)/shard_map/ppermute | solution.py:393
  419.1 211.2 %collective-permute-start.61 = (bf16[1024,1024]{1,0:T(8,128)(2,1)}, bf16[1024,1024]{1,0:T(8,128)(2,1)}, u32[]{:S(2)}, u32[]{:S(2)}) collective-permute-start(bf16[1024,1024]{1,0:T(8,128)(2,1)} %convolution_convert_fusion.1), channel_id=1, source_target_pairs={{0,1},{1,0},{2,3},{3,2},{4,5},{5,4},{6,7},{7,6},{8,9},{9,8},{10,11... | collective-permute-start | bytes 6291464 | tf_op jit(solution)/shard_map/ppermute | solution.py:393
  419.2 94.4 %collective-permute-start.51 = (f32[5120]{0:T(1024)S(1)}, f32[5120]{0:T(1024)S(1)}, u32[]{:S(2)}, u32[]{:S(2)}) collective-permute-start(f32[5120]{0:T(1024)S(1)} %add.250), channel_id=1, source_target_pairs={{0,16},{4,20},{8,24},{12,28},{16,0},{20,4},{24,8},{28,12},{1,17},{... | collective-permute-start | bytes 61448 | tf_op jit(solution)/shard_map/ppermute | solution.py:393
  557.3 52.6 %collective-permute-start.53 = (bf16[1024,1024]{1,0:T(8,128)(2,1)S(1)}, bf16[1024,1024]{1,0:T(8,128)(2,1)S(1)}, u32[]{:S(2)}, u32[]{:S(2)}) collective-permute-start(bf16[1024,1024]{1,0:T(8,128)(2,1)S(1)} %copy-done.6), channel_id=1, source_target_pairs={{0,1},{1,0},{2,3},{3,2},{4,5},{5,4},{6,7},{7,6},{8,9},{9,8},{10,11... | collective-permute-start | bytes 6291464 | tf_op jit(solution)/shard_map/ppermute | solution.py:393
  562.9 99.9 %collective-permute-start.52 = (bf16[1024,1024]{1,0:T(8,128)(2,1)S(1)}, bf16[1024,1024]{1,0:T(8,128)(2,1)S(1)}, u32[]{:S(2)}, u32[]{:S(2)}) collective-permute-start(bf16[1024,1024]{1,0:T(8,128)(2,1)S(1)} %copy-done.5), channel_id=1, source_target_pairs={{0,1},{1,0},{2,3},{3,2},{4,5},{5,4},{6,7},{7,6},{8,9},{9,8},{10,11... | collective-permute-start | bytes 6291464 | tf_op jit(solution)/shard_map/ppermute | solution.py:393
  577.7 127.5 %collective-permute-start.45 = (bf16[64,1024]{1,0:T(8,128)(2,1)S(1)}, bf16[64,1024]{1,0:T(8,128)(2,1)S(1)}, u32[]{:S(2)}, u32[]{:S(2)}) collective-permute-start(bf16[64,1024]{1,0:T(8,128)(2,1)S(1)} %pad_maximum_fusion.7), channel_id=1, source_target_pairs={{0,8},{4,12},{8,0},{12,4},{16,24},{20,28},{24,16},{28,20},{1,9},{5... | collective-permute-start | bytes 393224 | tf_op jit(solution)/shard_map/ppermute | solution.py:393
  604.8 48.6 %collective-permute-start.63 = (bf16[1024,1024]{1,0:T(8,128)(2,1)S(1)}, bf16[1024,1024]{1,0:T(8,128)(2,1)S(1)}, u32[]{:S(2)}, u32[]{:S(2)}) collective-permute-start(bf16[1024,1024]{1,0:T(8,128)(2,1)S(1)} %add_convert_fusion.1), channel_id=1, source_target_pairs={{0,2},{1,3},{2,0},{3,1},{4,6},{5,7},{6,4},{7,5},{8,10},{9,11},{10,... | collective-permute-start | bytes 6291464 | tf_op jit(solution)/shard_map/ppermute | solution.py:393
  628.3 68.1 %collective-permute-start.54 = (bf16[1024,1024]{1,0:T(8,128)(2,1)S(1)}, bf16[1024,1024]{1,0:T(8,128)(2,1)S(1)}, u32[]{:S(2)}, u32[]{:S(2)}) collective-permute-start(bf16[1024,1024]{1,0:T(8,128)(2,1)S(1)} %add_convert_fusion.3), channel_id=1, source_target_pairs={{0,2},{1,3},{2,0},{3,1},{4,6},{5,7},{6,4},{7,5},{8,10},{9,11},{10,... | collective-permute-start | bytes 6291464 | tf_op jit(solution)/shard_map/ppermute | solution.py:393
  630.4 72.9 %collective-permute-start.33 = (bf16[256,768]{1,0:T(8,128)(2,1)S(1)}, bf16[256,768]{1,0:T(8,128)(2,1)S(1)}, u32[]{:S(2)}, u32[]{:S(2)}) collective-permute-start(bf16[256,768]{1,0:T(8,128)(2,1)S(1)} %constant_dynamic-slice_fusion.10), channel_id=1, source_target_pairs={{0,8},{4,12},{8,0},{12,4},{16,24},{20,28},{24,16},{28,20},{1,9},{5... | collective-permute-start | bytes 1179656 | tf_op jit(solution)/shard_map/ppermute | solution.py:393
  662.4 52.8 %collective-permute-start.64 = (bf16[512,1024]{1,0:T(8,128)(2,1)S(1)}, bf16[512,1024]{1,0:T(8,128)(2,1)S(1)}, u32[]{:S(2)}, u32[]{:S(2)}) collective-permute-start(bf16[512,1024]{1,0:T(8,128)(2,1)S(1)} %constant_dynamic-slice_fusion.2), channel_id=1, source_target_pairs={{0,4},{4,0},{8,12},{12,8},{16,20},{20,16},{24,28},{28,24},{1,5},{5... | collective-permute-start | bytes 3145736 | tf_op jit(solution)/shard_map/ppermute | solution.py:393
  705.3 90.9 %collective-permute-start.46 = (bf16[128,1024]{1,0:T(8,128)(2,1)S(1)}, bf16[128,1024]{1,0:T(8,128)(2,1)S(1)}, u32[]{:S(2)}, u32[]{:S(2)}) collective-permute-start(bf16[128,1024]{1,0:T(8,128)(2,1)S(1)} %pad_maximum_fusion.6), channel_id=1, source_target_pairs={{0,4},{4,0},{8,12},{12,8},{16,20},{20,16},{24,28},{28,24},{1,5},{5... | collective-permute-start | bytes 786440 | tf_op jit(solution)/shard_map/ppermute | solution.py:393
  (78 other events, 1611.7 us)

commit v2 on v1

--- a/solution.py
+++ b/solution.py
@@ -30,14 +30,6 @@
 
 def tn(a, b):
     return lax.dot_general(a, b, (((0,), (0,)), ((), ())), preferred_element_type=f32)
-
-
-def params():
-    return pltpu.CompilerParams(vmem_limit_bytes=VMEM)
-
-
-def cost(flops, bytes_accessed):
-    return pl.CostEstimate(flops=flops, bytes_accessed=bytes_accessed, transcendentals=0)
 
 
 def head_rows():
@@ -94,9 +86,17 @@
     return jnp.where(v < 0, tail, 1.0 - tail), bell
 
 
-def qkv_kernel(blocks, thr, last, x, gain, shift, *refs):
-    wa, ba = refs[0:4], refs[4]
-    q_out, k_out, v_out, n_out, t_out = refs[5:10]
+def qkv_kernel(blocks, fresh, thr, last, *refs):
+    if fresh:
+        x, gain, shift, n_out = refs[0], refs[1], refs[2], refs[9]
+        wa, ba = refs[3:5], refs[5]
+        q_out, k_out, v_out = refs[6:9]
+        t_out = refs[10]
+    else:
+        n_in = refs[0]
+        wa, ba = refs[1:3], refs[3]
+        q_out, k_out, v_out = refs[4:7]
+        t_out = refs[7]
     step = pl.program_id(0)
     rows = blocks * STRETCH
 
@@ -104,9 +104,12 @@
     def _():
         t_out[...] = jnp.zeros_like(t_out)
 
-    xhat, _ = centre(x[...].astype(f32))
-    normed = (xhat * gain[...] + shift[...]).astype(bf16)
-    n_out[...] = normed
+    if fresh:
+        xhat, _ = centre(x[...].astype(f32))
+        normed = (xhat * gain[...] + shift[...]).astype(bf16)
+        n_out[...] = normed
+    else:
+        normed = n_in[...]
     place = lax.broadcasted_iota(jnp.int32, (STRETCH, 128), 0)
     valid = jnp.concatenate(
         [(place >= thr[step * blocks + b]).astype(f32) for b in range(blocks)], axis=0
@@ -116,7 +119,7 @@
     def feature(values):
         return jnp.where(values > 0, values + 1.0, jnp.exp(jnp.minimum(values, 0.0)))
 
-    for g in range(QUADS):
+    for g in range(2):
         project = nn(normed, wa[g][...]) + ba[:, g * PW : (g + 1) * PW]
         for pair in range(2):
             c0, c1, c2 = (
@@ -133,17 +136,19 @@
         @pl.when(last[step * blocks + b] == 1)
         def _(b=b):
             here = slice(b * STRETCH, (b + 1) * STRETCH)
-            for g in range(QUADS):
+            for g in range(2):
                 at = slice(g * QW, (g + 1) * QW)
                 key = k_out[here, at]
                 t_out[0:DH, at] += gather_state(tn(key, v_out[here, at]), picks)
                 t_out[DH : DH + 8, at] += fold_rows(key.astype(f32))
 
 
-def attend_kernel(blocks, cont, q, k, v, x, s_in, ones, bo, gain, shift, *refs):
-    wo = refs[0:4]
-    att_out, rec_out, st_out, kt_out, mid_out, n_out = refs[4:10]
-    state, total = refs[10:12]
+def attend_kernel(blocks, cont, thr, *refs):
+    qkv = refs[0:3], refs[3:6]
+    x, s_in, ones, bo, gain, shift = refs[6:12]
+    wo = refs[12:16]
+    att_out, rec_out, st_out, kt_out, mid_out, n_out = refs[16:22]
+    state, total = refs[22:24]
     step = pl.program_id(0)
 
     @pl.when(step == 0)
@@ -168,7 +173,8 @@
         kt_out[b * 8 : (b + 1) * 8, :] = total[...]
         for g in range(QUADS):
             at = slice(g * QW, (g + 1) * QW)
-            qb, kb, vb = q[here, at], k[here, at], v[here, at]
+            own = slice((g % 2) * QW, (g % 2 + 1) * QW)
+            qb, kb, vb = (part[here, own] for part in qkv[g // 2])
             scores = nt(qb, spread_heads(kb, low_picks))
             scores = jnp.where(lower, scores, 0.0).astype(bf16)
             numer = nn(scores, spread_heads(vb, low_picks)) + nn(
@@ -181,15 +187,6 @@
             att_out[here, at] = (numer * rec).astype(bf16)
             state[:, at] += gather_state(tn(kb, vb), picks)
             total[:, at] += jnp.sum(kb.astype(f32), axis=0, keepdims=True)
-    return picks
-
-
-def attend_tile(blocks, cont, thr, *refs):
-    q, k, v, x, s_in, ones, bo, gain, shift = refs[0:9]
-    wo = refs[9:13]
-    att_out, rec_out, st_out, kt_out, mid_out, n_out = refs[13:19]
-    attend_kernel(blocks, cont, q, k, v, x, s_in, ones, bo, gain, shift, *refs[9:])
-    step = pl.program_id(0)
     place = lax.broadcasted_iota(jnp.int32, (STRETCH, D), 0)
     for b in range(blocks):
         here = slice(b * STRETCH, (b + 1) * STRETCH)
@@ -197,8 +194,7 @@
         @pl.when(thr[step * blocks + b] > 0)
         def _(b=b, here=here):
             valid = (place >= thr[step * blocks + b]).astype(f32)
-            rec = rec_out[here, :] * valid
-            rec_out[here, :] = rec
+            rec_out[here, :] = rec_out[here, :] * valid
             att_out[here, :] = (att_out[here, :].astype(f32) * valid).astype(bf16)
 
     middle = x[...].astype(f32) + bo[...]
@@ -209,36 +205,74 @@
     n_out[...] = (xhat * gain[...] + shift[...]).astype(bf16)
 
 
-def ffn_kernel(blocks, first, n2, cot, mid, att, rec, q, gain, be, br, ones, *refs):
-    we, wr, wo = refs[0:4], refs[4:8], refs[8:12]
-    act, gh = refs[12:16], refs[16:20]
-    out, gm_out, gb_out, gn_out, t_out, l_out, sums, be_sum = refs[20:28]
+def ffn_kernel(blocks, slots, fresh, final, *refs):
+    refs = list(refs)
+
+    def take(count):
+        taken = refs[:count]
+        del refs[:count]
+        return taken
+
+    count = sum(len(widths) for widths in slots)
+    if final:
+        (first,) = take(1)
+    n2, cot = take(2)
+    be = take(len(slots))
+    if not fresh:
+        part_out, part_grad = take(2)
+    we, wr = take(count), take(count)
+    if final:
+        mid, att, rec, q01, q23, gain, br, ones = take(8)
+        wo = take(4)
+    de_out, dr_out, be_sum = take(len(slots)), take(len(slots)), take(len(slots))
+    if final:
+        out, gm_out, gb_out, gn_out, t_out, l_out, sums = take(7)
+    else:
+        next_out, next_grad = take(2)
+    de_sum, dr_sum = take(len(slots)), take(len(slots))
     step = pl.program_id(0)
 
     @pl.when(step == 0)
     def _():
-        l_out[...] = jnp.zeros_like(l_out)
-        sums[...] = jnp.zeros_like(sums)
-        be_sum[...] = jnp.zeros_like(be_sum)
+        for total in de_sum + dr_sum + be_sum:
+            total[...] = jnp.zeros_like(total)
+        if final:
+            l_out[...] = jnp.zeros_like(l_out)
+            sums[...] = jnp.zeros_like(sums)
 
     normed = n2[...]
     cotangent = cot[...]
-    reduced = None
-    grad = None
-    for g in range(QUADS):
-        at = slice(g * D, (g + 1) * D)
-        hidden = nn(normed, we[g][...]) + be[:, at]
-        grad_act = nt(cotangent, wr[g][...])
-        phi, bell = normal_parts(hidden)
-        active = (hidden * phi).astype(bf16)
-        back = (grad_act * (phi + hidden * (0.3989422804014327 * bell))).astype(bf16)
-        act[g][...] = active
-        gh[g][...] = back
-        be_sum[:, at] += fold_rows(back.astype(f32))
-        part = nn(active, wr[g][...])
-        reduced = part if reduced is None else reduced + part
-        part = nt(back, we[g][...])
-        grad = part if grad is None else grad + part
+    reduced = None if fresh else part_out[...]
+    grad = None if fresh else part_grad[...]
+    i = 0
+    for slot, widths in enumerate(slots):
+        start = 0
+        for width in widths:
+            at = slice(start, start + width)
+            hidden = nn(normed, we[i][...]) + be[slot][:, at]
+            grad_act = nt(cotangent, wr[i][...])
+            phi, bell = normal_parts(hidden)
+            active = (hidden * phi).astype(bf16)
+            back = (grad_act * (phi + hidden * (0.3989422804014327 * bell))).astype(bf16)
+            be_sum[slot][:, at] += fold_rows(back.astype(f32))
+            de_sum[slot][:, at] += tn(normed, back)
+            dr_sum[slot][at, :] += tn(active, cotangent)
+            more = nn(active, wr[i][...])
+            reduced = more if reduced is None else reduced + more
+            more = nt(back, we[i][...])
+            grad = more if grad is None else grad + more
+            start += width
+            i += 1
+
+    @pl.when(step == pl.num_programs(0) - 1)
+    def _():
+        for out_ref, total in zip(de_out + dr_out, de_sum + dr_sum):
+            out_ref[...] = total[...].astype(bf16)
+
+    if not final:
+        next_out[...] = reduced
+        next_grad[...] = grad
+        return
     middle = mid[...]
     out[...] = (middle + reduced + br[...]).astype(bf16)
     xhat, inverse = centre(middle)
@@ -268,15 +302,16 @@
             here = slice(b * STRETCH, (b + 1) * STRETCH)
             for g in range(QUADS):
                 at = slice(g * QW, (g + 1) * QW)
-                query = q[here, at]
+                query = (q01, q23)[g // 2][here, (g % 2) * QW : (g % 2 + 1) * QW]
                 l_out[0:DH, at] += gather_state(tn(query, gn_out[here, at]), picks)
                 grad_denom = nn(t_out[here, at], ones[512:768])
                 l_out[DH : DH + 8, at] += fold_rows(grad_denom * query.astype(f32))
 
 
-def back_kernel(blocks, tiles, cont, q, k, v, gn, t, st, kt, g_in, ones, *refs):
-    gp_out, ba_sum = refs[0:4], refs[4]
-    state, total = refs[5:7]
+def back_kernel(blocks, tiles, quads, cont, q, k, v, gn, t, st, kt, g_in, ones, normed, *refs):
+    gp_out, da_out, ba_sum = refs[0:quads], refs[quads : 2 * quads], refs[2 * quads]
+    state, total = refs[2 * quads + 1 : 2 * quads + 3]
+    da_sum = refs[2 * quads + 3 :]
     step = pl.program_id(0)
     tile = tiles - 1 - step
 
@@ -287,6 +322,8 @@
             jnp.sum(g_in[DH : DH + 8], axis=0, keepdims=True), total.shape
         )
         ba_sum[...] = jnp.zeros_like(ba_sum)
+        for da in da_sum:
+            da[...] = jnp.zeros_like(da)
 
     picks = head_rows()
     low_picks = [p.astype(bf16) for p in picks]
@@ -302,7 +339,7 @@
         state[...] = state[...] * keep
         total[...] = total[...] * keep
         low_state = state[...].astype(bf16)
-        for g in range(QUADS):
+        for g in range(quads):
             at = slice(g * QW, (g + 1) * QW)
             qb, kb, vb, gb, tb = q[here, at], k[here, at], v[here, at], gn[here, at], t[here, at]
             q_wide = qb.astype(f32)
@@ -343,11 +380,18 @@
                     )
             state[:, at] += gather_state(tn(qb, gb), picks)
             total[:, at] += jnp.sum(grad_denom * q_wide, axis=0, keepdims=True)
+    for g in range(quads):
+        da_sum[g][...] += tn(normed[...], gp_out[g][...])
+
+    @pl.when(step == tiles - 1)
+    def _():
+        for out, da in zip(da_out, da_sum):
+            out[...] = da[...].astype(bf16)
 
 
 def input_kernel(x, gm, gain, *refs):
     gp, wa = refs[0:4], refs[4:8]
-    out, sums = refs[8:10]
+    out, sums = refs[-2:]
 
     @pl.when(pl.program_id(0) == 0)
     def _():
@@ -362,30 +406,45 @@
     sums[8:16, :] += fold_rows(grad)
 
 
-def rows_spec(rows, columns):
-    return pl.BlockSpec((rows, columns), lambda i, *_: (i, 0))
-
-
-def back_spec(rows, columns, tiles):
-    return pl.BlockSpec((rows, columns), lambda i, *_: (tiles - 1 - i, 0))
-
-
-def whole_spec(shape):
-    return pl.BlockSpec(shape, lambda i, *_: (0,) * len(shape), pipeline_mode=pl.Buffered(1))
+def rows_spec(rows, columns, at=0, start=0):
+    return pl.BlockSpec((rows, columns), lambda i, *_: (i + start, at))
+
+
+def back_spec(rows, columns, tiles, at=0):
+    return pl.BlockSpec((rows, columns), lambda i, *_: (tiles - 1 - i, at))
+
+
+def whole_spec(shape, at=0):
+    last = len(shape) - 1
+    return pl.BlockSpec(
+        shape, lambda i, *_: (0,) * last + (at,), pipeline_mode=pl.Buffered(1)
+    )
 
 
 def sum_spec(shape):
     return pl.BlockSpec(shape, lambda i, *_: (0,) * len(shape))
 
 
-def grid_spec(scalars, tiles, in_specs, out_specs, scratch=()):
-    return pltpu.PrefetchScalarGridSpec(
-        num_scalar_prefetch=scalars,
-        grid=(tiles,),
-        in_specs=in_specs,
-        out_specs=out_specs,
-        scratch_shapes=list(scratch),
-    )
+def call(kernel, name, scalars, tiles, ins, outs, scratch, flops, moved, aliases=None):
+    return pl.pallas_call(
+        kernel,
+        grid_spec=pltpu.PrefetchScalarGridSpec(
+            num_scalar_prefetch=len(scalars),
+            grid=(tiles,),
+            in_specs=[spec for _, spec in ins],
+            out_specs=[spec for _, spec in outs],
+            scratch_shapes=list(scratch),
+        ),
+        out_shape=[shape for shape, _ in outs],
+        compiler_params=pltpu.CompilerParams(vmem_limit_bytes=VMEM),
+        cost_estimate=pl.CostEstimate(flops=flops, bytes_accessed=moved, transcendentals=0),
+        input_output_aliases=aliases or {},
+        name=name,
+    )(*scalars, *[array for array, _ in ins])
+
+
+def tie(*values):
+    return lax.optimization_barrier(list(values))
 
 
 def swap(value, axis, bit):
@@ -410,9 +469,14 @@
     return [held[k] for k in range(size)]
 
 
+def half_of(value, which, axis):
+    size = value.shape[axis] // 2
+    return lax.dynamic_slice_in_dim(value, which * size, size, axis)
+
+
 def regroup(parts, count, axis):
     if len(parts) == count:
-        return parts
+        return list(parts)
     whole = jnp.concatenate(parts, axis=axis)
     width = whole.shape[axis] // count
     return [
@@ -442,37 +506,106 @@
     return held[0]
 
 
-def sum_groups(value):
+class Stages:
+    def __init__(self, generator):
+        self.generator, self.got = generator, None
+
+    def advance(self):
+        sent, self.got = self.generator.send(self.got)
+        return sent
+
+    def finish(self):
+        while self.advance():
+            pass
+        return self.got[0]
+
+
+def sum_stages(terms):
     size = lax.axis_size("dp")
     me = lax.axis_index("dp")
-    bits = bits_of(size)
-    value = value.astype(bf16)
-    for bit in bits:
-        half = value.shape[0] // 2
-        mine = jnp.where((me & bit) != 0, 1, 0)
-        sent = lax.dynamic_slice_in_dim(value, (1 - mine) * half, half, 0)
-        kept = lax.dynamic_slice_in_dim(value, mine * half, half, 0)
-        got = swap(sent, "dp", bit)
-        value = (kept.astype(f32) + got.astype(f32)).astype(bf16)
-    for bit in reversed(bits):
-        got = swap(value, "dp", bit)
-        upper = (me & bit) != 0
-        value = jnp.concatenate(
-            [jnp.where(upper, got, value), jnp.where(upper, value, got)], axis=0
-        )
-    return value.astype(f32)
-
-
-def sum_small(shared, split):
+    x, z, depth = me % 2, me // 2, size // 2
+
+    def half(which):
+        total = None
+        for term in terms:
+            part = half_of(term, which, 0).astype(f32)
+            total = part if total is None else total + part
+        return total.astype(bf16)
+
+    sent, kept = tie(half(1 - x), half(x))
+    (got,) = yield [sent, kept], [swap(sent, "dp", 1)]
+    mine = (kept.astype(f32) + got.astype(f32)).astype(bf16)
+    rows = mine.shape[0] // depth
+    own = lax.dynamic_slice_in_dim(mine, z * rows, rows, 0)
+    sent = [
+        lax.dynamic_slice_in_dim(mine, (z ^ j) * rows, rows, 0) for j in range(1, depth)
+    ]
+    own, *sent = tie(own, *sent)
+    got = yield [own] + sent, [swap(part, "dp", 2 * j) for j, part in enumerate(sent, 1)]
+    total = own.astype(f32)
+    for part in got:
+        total = total + part.astype(f32)
+    (own,) = tie(total.astype(bf16))
+    got = yield [own], [swap(own, "dp", 2 * j) for j in range(1, depth)]
+    (mine,) = tie(jnp.concatenate([own] + list(got), axis=0))
+    (other,) = yield [mine], [swap(mine, "dp", 1)]
+
+    def natural(value):
+        for bit in bits_of(depth):
+            shaped = value.reshape(depth // (2 * bit), 2, bit * rows, value.shape[1])
+            turned = jnp.flip(shaped, axis=1)
+            value = jnp.where((z & bit) != 0, turned, shaped).reshape(value.shape)
+        return value
+
+    mine, other = natural(mine), natural(other)
+    pair = [jnp.where(x == 0, mine, other), jnp.where(x == 0, other, mine)]
+    yield [], [jnp.concatenate(pair, axis=0).astype(f32)]
+
+
+class Window:
+    def __init__(self, *after):
+        self.after, self.sent, self.got, self.chains = after, [], [], []
+
+    def swap(self, value, axis, bit):
+        value = tie(value, *self.after)[0]
+        self.sent.append(value)
+        self.got.append(swap(value, axis, bit))
+        return Later(self, len(self.got) - 1)
+
+    def step(self, chain):
+        self.sent += chain.advance()
+        self.chains.append((chain, len(self.got)))
+        self.got += chain.got
+
+    def open(self, *values):
+        return tie(*values, *self.sent)[: len(values)]
+
+    def close(self, *values):
+        tied = tie(*values, *self.got)
+        self.got = tied[len(values) :]
+        for chain, start in self.chains:
+            chain.got = self.got[start : start + len(chain.got)]
+        return tied[: len(values)]
+
+
+class Later:
+    def __init__(self, window, place):
+        self.window, self.place = window, place
+
+    def get(self):
+        return self.window.got[self.place]
+
+
+def small_stages(shared, split):
     size = len(split)
     held = dict(enumerate(split))
     flat = shared.reshape(-1)
     for bit in bits_of(size):
         gone = [k for k in held if k & bit]
-        sent = jnp.concatenate([flat] + [held[k] for k in gone])
-        got = swap(sent, "head", bit)
-        flat = flat + got[: flat.shape[0]]
+        (sent,) = tie(jnp.concatenate([flat] + [held[k] for k in gone]))
+        (got,) = yield [sent], [swap(sent, "head", bit)]
         at = flat.shape[0]
+        flat = flat + got[:at]
         for k in gone:
             width = held[k].shape[0]
             held[k ^ bit] = held[k ^ bit] + got[at : at + width]
@@ -480,8 +613,10 @@
             at += width
     both = jnp.concatenate([flat, held[0]])
     for bit in bits_of(lax.axis_size("dp")):
-        both = both + swap(both, "dp", bit)
-    return both[: flat.shape[0]].reshape(shared.shape), both[flat.shape[0] :]
+        (both,) = tie(both)
+        (got,) = yield [both], [swap(both, "dp", bit)]
+        both = both + got
+    yield [], [(both[: flat.shape[0]].reshape(shared.shape), both[flat.shape[0] :])]
 
 
 def on_device(
@@ -505,21 +640,26 @@
     R = layer_input.shape[0]
     n = lax.axis_size("head")
     me = lax.axis_index("head")
+    x = lax.axis_index("dp") % 2
     nb = R // STRETCH
     FF = expand_weight.shape[1] * n
-
-    wa_all = gather_shards(attend_weight)
-    ba_all = gather_shards(attend_bias)
-    wo_all = gather_shards(output_weight)
-    we_all = gather_shards(expand_weight)
-    wr_all = gather_shards(reduce_weight)
-    be_all = gather_shards(expand_bias)
-    wa = regroup(wa_all, QUADS, 1)
-    wo = regroup(wo_all, QUADS, 0)
-    we = regroup(we_all, QUADS, 1)
-    wr = regroup(wr_all, QUADS, 0)
-    ba = jnp.concatenate(ba_all)[None, :]
-    be = jnp.concatenate(be_all)[None, :]
+    FQ = FF // QUADS
+    fast = n == QUADS
+
+    if fast:
+        near = swap(attend_weight, "head", 1)
+        ba_near = jnp.concatenate([attend_bias, swap(attend_bias, "head", 1)])
+        be_near = jnp.concatenate([expand_bias, swap(expand_bias, "head", 1)])
+        wa = [attend_weight, near, None, None]
+        w = Window()
+        wa_far = w.swap(attend_weight, "head", 2)
+        bias_far = w.swap(jnp.concatenate([ba_near, be_near]), "head", 2)
+        wo_near = w.swap(output_weight, "head", 1)
+        we_near = w.swap(expand_weight, "head", 1)
+        wr_near = w.swap(reduce_weight, "head", 1)
+    else:
+        wa = regroup(gather_shards(attend_weight), QUADS, 1)
+        ba_near, ba_far = jnp.split(jnp.concatenate(gather_shards(attend_bias)), 2)
 
     sizes, pads = crop_blocks[0], crop_padding[0]
     crops = sizes.shape[0]
@@ -551,136 +691,331 @@
     blocks = 2 if nb % 2 == 0 else 1
     rows = blocks * STRETCH
     tiles = R // rows
-    vec = whole_spec((1, D))
     gain1, shift1 = first_gain[None, :], first_shift[None, :]
     gain2, shift2 = second_gain[None, :], second_shift[None, :]
     like = jax.ShapeDtypeStruct
-    low = like((R, D), bf16)
-    wide = like((R, D), f32)
-    state_shape = (DH + 8, D)
-
-    q, k, v, normed, trailing = pl.pallas_call(
-        functools.partial(qkv_kernel, blocks),
-        grid_spec=grid_spec(
-            2,
+    HALF = D // 2
+    full, side = rows_spec(rows, D), rows_spec(rows, HALF)
+    low, wide = (like((R, D), bf16), full), (like((R, D), f32), full)
+    narrow = (like((R, HALF), bf16), side)
+    vec = whole_spec((1, D))
+    state_rows = DH + 8
+
+    def vector(value):
+        return (value, vec)
+
+    def project(source, pick, bias, fresh):
+        ins = [(source, full)]
+        if fresh:
+            ins += [vector(gain1), vector(shift1)]
+        ins += [(wa[k], whole_spec((D, PW))) for k in pick]
+        ins += [(bias, whole_spec((1, 2 * PW)))]
+        outs = [narrow] * 3 + ([low] if fresh else [])
+        outs += [(like((state_rows, HALF), f32), sum_spec((state_rows, HALF)))]
+        return call(
+            functools.partial(qkv_kernel, blocks, fresh),
+            "qkv",
+            (thr, last),
             tiles,
-            [rows_spec(rows, D), vec, vec]
-            + [whole_spec((D, PW))] * 4
-            + [whole_spec((1, 3 * D))],
-            [rows_spec(rows, D)] * 4 + [sum_spec(state_shape)],
-        ),
-        out_shape=[low] * 4 + [like(state_shape, f32)],
-        compiler_params=params(),
-        cost_estimate=cost(2 * R * D * 3 * D, 10 * R * D + 6 * D * D),
-        name="qkv",
-    )(thr, last, layer_input, gain1, shift1, *wa, ba)
-
-    s_in = swap_state(trailing, before)
-
-    att, rec, st, kt, middle, n2 = pl.pallas_call(
-        functools.partial(attend_tile, blocks),
-        grid_spec=grid_spec(
-            2,
+            ins,
+            outs,
+            [],
+            3 * R * D * D,
+            8 * R * D + 3 * D * D,
+        )
+
+    bias = ba_near[None, :]
+    source = layer_input
+    if fast:
+        source, bias = w.open(source, bias)
+    q01, k01, v01, normed, trail01 = project(source, (0, 1), bias, True)
+    if fast:
+        q01, k01, v01, normed, trail01 = w.close(q01, k01, v01, normed, trail01)
+        wa[2] = wa_far.get()
+        wa[3] = swap(wa[2], "head", 1)
+        ba_far, be_far = bias_far.get()[: ba_near.shape[0]], bias_far.get()[ba_near.shape[0] :]
+        be_slots = jnp.split(jnp.concatenate([be_near, be_far]), QUADS)
+        wo = [output_weight, wo_near.get(), None, None]
+        w = Window(trail01)
+        wo_far = w.swap(output_weight, "head", 2)
+        normed, wa[3] = w.open(normed, wa[3])
+    else:
+        wo = regroup(gather_shards(output_weight), QUADS, 0)
+        we = regroup(gather_shards(expand_weight), QUADS, 1)
+        wr = regroup(gather_shards(reduce_weight), QUADS, 0)
+        be_slots = jnp.split(jnp.concatenate(gather_shards(expand_bias)), QUADS)
+    q23, k23, v23, trail23 = project(normed, (2, 3), ba_far[None, :], False)
+    if fast:
+        q23, k23, v23, trail23 = w.close(q23, k23, v23, trail23)
+        wo[2] = wo_far.get()
+        wo[3] = swap(wo[2], "head", 1)
+    s_in = swap_state(jnp.concatenate([trail01, trail23], axis=1), before)
+    if fast:
+        w = Window(s_in)
+        wr_far = w.swap(reduce_weight, "head", 2)
+        (s_in,) = w.open(s_in)
+
+    att, rec, st, kt, middle, n2 = call(
+        functools.partial(attend_kernel, blocks),
+        "attend",
+        (cont, thr),
+        tiles,
+        [(a, side) for a in (q01, k01, v01, q23, k23, v23)]
+        + [
+            (layer_input, full),
+            (s_in, whole_spec((state_rows, D))),
+            (ones, whole_spec((768, QW))),
+            vector(output_bias[None, :]),
+            vector(gain2),
+            vector(shift2),
+        ]
+        + [(w, whole_spec((QW, D))) for w in wo],
+        [
+            low,
+            wide,
+            (like((nb * DH, D), bf16), rows_spec(blocks * DH, D)),
+            (like((nb * 8, D), f32), rows_spec(blocks * 8, D)),
+            wide,
+            low,
+        ],
+        [pltpu.VMEM((DH, D), f32), pltpu.VMEM((8, D), f32)],
+        12 * R * D * D,
+        20 * R * D,
+    )
+
+    if fast:
+        att, rec, st, kt, middle, n2 = w.close(att, rec, st, kt, middle, n2)
+        we = [expand_weight, we_near.get(), None, None]
+        wr = [reduce_weight, wr_near.get(), wr_far.get(), None]
+
+    def ffn(picks, part, extra):
+        slots = [[FQ]] * len(picks)
+        ins = [(n2, full), (cotangent, full)]
+        ins += [(be_slots[k][None, :], whole_spec((1, FQ))) for k in picks]
+        if part is not None:
+            ins += [(part[0], full), (part[1], full)]
+        ins += [(we[k], whole_spec(we[k].shape)) for k in picks]
+        ins += [(wr[k], whole_spec(wr[k].shape)) for k in picks]
+        outs = [(like((D, FQ), bf16), whole_spec((D, FQ)))] * len(picks)
+        outs += [(like((FQ, D), bf16), whole_spec((FQ, D)))] * len(picks)
+        outs += [(like((8, FQ), f32), sum_spec((8, FQ)))] * len(picks)
+        if extra is None:
+            outs += [wide, wide]
+        else:
+            ins += extra
+            outs += [low, wide, low, low, low]
+            outs += [
+                (like((state_rows, D), f32), sum_spec((state_rows, D))),
+                (like((32, D), f32), sum_spec((32, D))),
+            ]
+        results = call(
+            functools.partial(ffn_kernel, blocks, slots, part is None, extra is not None),
+            "ffn",
+            (first,) if extra is not None else (),
             tiles,
-            [rows_spec(rows, D)] * 4
-            + [whole_spec(state_shape), whole_spec((768, QW)), vec, vec, vec]
-            + [whole_spec((QW, D))] * 4,
-            [
-                rows_spec(rows, D),
-                rows_spec(rows, D),
-                rows_spec(blocks * DH, D),
-                rows_spec(blocks * 8, D),
-                rows_spec(rows, D),
-                rows_spec(rows, D),
+            ins,
+            outs,
+            [pltpu.VMEM((D, FQ), f32)] * len(picks) + [pltpu.VMEM((FQ, D), f32)] * len(picks),
+            12 * R * D * FQ * len(picks),
+            20 * R * D,
+        )
+        for i, k in enumerate(picks):
+            de[k], dr[k], eb[k] = (results[i + j * len(picks)] for j in range(3))
+        return list(results[3 * len(picks) :])
+
+    de, dr, eb = [None] * 4, [None] * 4, [None] * 4
+    extra = [
+        (middle, full),
+        (att, full),
+        (rec, full),
+        (q01, side),
+        (q23, side),
+        vector(gain2),
+        vector(reduce_bias[None, :]),
+        (ones, whole_spec((768, QW))),
+    ] + [(w, whole_spec((QW, D))) for w in wo]
+    if fast:
+        w = Window(n2)
+        we_far = w.swap(expand_weight, "head", 2)
+        wr_last = w.swap(wr[2], "head", 1)
+        (n2,) = w.open(n2)
+        part = ffn((1,), None, None)
+        n2, *part = w.close(n2, *part)
+        we[2], wr[3] = we_far.get(), wr_last.get()
+        we[3] = swap(we[2], "head", 1)
+        w = Window(part[0])
+        near = w.swap(de[1], "head", 1), w.swap(dr[1], "head", 1)
+        (part[0],) = w.open(part[0])
+        part = ffn((3,), part, None)
+        part = w.close(*part)
+        near = [late.get() for late in near]
+        w = Window(part[0])
+        got = w.swap(de[3], "head", 1), w.swap(dr[3], "head", 1)
+        (part[0],) = w.open(part[0])
+        part = ffn((2,), part, None)
+        part[0], part[1], de[2], dr[2] = w.close(*part, de[2], dr[2])
+        far = [
+            (a.astype(f32) + b.get().astype(f32)).astype(bf16)
+            for a, b in zip((de[2], dr[2]), got)
+        ]
+        w = Window(part[0])
+        r_cut = jnp.split(far[1], 2)
+        e_far = w.swap(far[0], "head", 2)
+        r_far = w.swap(r_cut[0], "head", 2)
+        (part[0],) = w.open(part[0])
+        results = ffn((0,), part, extra)
+        de[0], dr[0], *results = w.close(de[0], dr[0], *results)
+    else:
+        part = ffn((3,), None, None)
+        part = ffn((2,), part, None)
+        results = ffn((1, 0), part, extra)
+    layer_output, grad_middle, branch, gn, t, leading, sums2 = results
+
+    def back(pick, q, k, v, state):
+        count = len(pick)
+        at, inner, width = pick[0] // count, (pick[0] % 2) // count, count * QW
+        return call(
+            functools.partial(back_kernel, blocks, tiles, count),
+            "attend_back",
+            (cont,),
+            tiles,
+            [(a, back_spec(rows, width, tiles, inner)) for a in (q, k, v)]
+            + [(a, back_spec(rows, width, tiles, at)) for a in (gn, t)]
+            + [
+                (st, back_spec(blocks * DH, width, tiles, at)),
+                (kt, back_spec(blocks * 8, width, tiles, at)),
+                (state, whole_spec((state_rows, width), at)),
+                (ones, whole_spec((768, QW))),
+                (normed, back_spec(rows, D, tiles)),
             ],
-            [pltpu.VMEM((DH, D), f32), pltpu.VMEM((8, D), f32)],
-        ),
-        out_shape=[low, wide, like((nb * DH, D), bf16), like((nb * 8, D), f32), wide, low],
-        compiler_params=params(),
-        cost_estimate=cost(6 * R * D * D, 20 * R * D),
-        name="attend",
-    )(cont, thr, q, k, v, layer_input, s_in, ones, output_bias[None, :], gain2, shift2, *wo)
-
-    results = pl.pallas_call(
-        functools.partial(ffn_kernel, blocks),
-        grid_spec=grid_spec(
-            1,
-            tiles,
-            [rows_spec(rows, D)] * 6
-            + [vec, whole_spec((1, FF)), vec, whole_spec((768, QW))]
-            + [whole_spec((D, FF // 4))] * 4
-            + [whole_spec((FF // 4, D))] * 4
-            + [whole_spec((QW, D))] * 4,
-            [rows_spec(rows, FF // 4)] * 8
-            + [rows_spec(rows, D)] * 5
-            + [sum_spec(state_shape), sum_spec((32, D)), sum_spec((8, FF))],
-        ),
-        out_shape=[like((R, FF // 4), bf16)] * 8
-        + [low, wide, low, low, low]
-        + [like(state_shape, f32), like((32, D), f32), like((8, FF), f32)],
-        compiler_params=params(),
-        cost_estimate=cost(8 * R * D * FF + 2 * R * D * D, 40 * R * D),
-        name="ffn",
-    )(
-        first, n2, cotangent, middle, att, rec, q, gain2, be, reduce_bias[None, :], ones,
-        *we, *wr, *wo,
-    )
-    act, gh = results[0:4], results[4:8]
-    layer_output, grad_middle, branch, gn, t, leading, sums2, be_sum = results[8:]
-
-    g_in = swap_state(leading, after)
-
-    reduce_grads = regroup([tn(a, cotangent) for a in act], n, 0)
-    expand_grads = regroup([tn(n2, g) for g in gh], n, 1)
-    reduce_weight_grad = sum_groups(scatter_head(reduce_grads))
-    expand_weight_grad = sum_groups(scatter_head(expand_grads))
-
-    gp_and_sum = pl.pallas_call(
-        functools.partial(back_kernel, blocks, tiles),
-        grid_spec=grid_spec(
-            1,
-            tiles,
-            [back_spec(rows, D, tiles)] * 5
-            + [back_spec(blocks * DH, D, tiles), back_spec(blocks * 8, D, tiles)]
-            + [whole_spec(state_shape), whole_spec((768, QW))],
-            [back_spec(rows, PW, tiles)] * 4 + [sum_spec((8, 3 * D))],
-            [pltpu.VMEM((DH, D), f32), pltpu.VMEM((8, D), f32)],
-        ),
-        out_shape=[like((R, PW), bf16)] * 4 + [like((8, 3 * D), f32)],
-        compiler_params=params(),
-        cost_estimate=cost(8 * R * D * D, 18 * R * D),
-        name="attend_back",
-    )(cont, q, k, v, gn, t, st, kt, g_in, ones)
-    gp, ba_sum = gp_and_sum[0:4], gp_and_sum[4]
-
-    out_grads = regroup([tn(att, branch)], n, 0)
-    output_weight_grad = sum_groups(scatter_head(out_grads))
-    attend_grads = regroup([tn(normed, g) for g in gp], n, 1)
-    attend_weight_grad = sum_groups(scatter_head(attend_grads))
-
-    input_grad, sums1 = pl.pallas_call(
-        input_kernel,
-        grid_spec=grid_spec(
-            0,
-            tiles,
-            [rows_spec(rows, D)] * 2
-            + [vec]
-            + [rows_spec(rows, PW)] * 4
-            + [whole_spec((D, PW))] * 4,
-            [rows_spec(rows, D), sum_spec((16, D))],
-        ),
-        out_shape=[wide, like((16, D), f32)],
-        compiler_params=params(),
-        cost_estimate=cost(2 * R * D * 3 * D, 16 * R * D),
-        name="input_grad",
-    )(layer_input, grad_middle, gain1, *gp, *wa)
-
-    shared2, expand_bias_grad = sum_small(
-        jnp.sum(sums2.reshape(4, 8, D), axis=1), regroup([jnp.sum(be_sum, axis=0)], n, 0)
-    )
-    shared1, attend_bias_grad = sum_small(
-        jnp.sum(sums1.reshape(2, 8, D), axis=1), regroup([jnp.sum(ba_sum, axis=0)], n, 0)
-    )
+            [(like((R, PW), bf16), back_spec(rows, PW, tiles))] * count
+            + [(like((D, PW), bf16), whole_spec((D, PW)))] * count
+            + [(like((8, count * PW), f32), sum_spec((8, count * PW)))],
+            [pltpu.VMEM((DH, width), f32), pltpu.VMEM((8, width), f32)]
+            + [pltpu.VMEM((D, PW), f32)] * count,
+            6 * count * R * D * D,
+            5 * count * R * D,
+        )
+
+    def inputs(start, count, out, x_in):
+        at = rows_spec(rows, D, 0, start)
+        ins = [(x_in, at), (grad_middle, at), vector(gain1)]
+        ins += [(g, rows_spec(rows, PW, 0, start)) for g in gp]
+        ins += [(w, whole_spec((D, PW))) for w in wa]
+        if out is not None:
+            ins += [(out, pl.BlockSpec(memory_space=pl.ANY))]
+        return call(
+            input_kernel,
+            "input_grad",
+            (),
+            count,
+            ins,
+            [(wide[0], at), (like((16, D), f32), sum_spec((16, D)))],
+            [],
+            6 * rows * count * D * D,
+            16 * rows * count * D,
+            None if out is None else {len(ins) - 1: 0},
+        )
+
+    gp = [None] * 4
+    shared2 = jnp.sum(sums2.reshape(4, 8, D), axis=1)
+    eb = regroup([jnp.sum(e, axis=0) for e in eb], n, 0)
+    ss = Stages(small_stages(shared2, eb))
+    if fast:
+        es = Stages(sum_stages([de[0], near[0], e_far.get()]))
+        w = Window(branch)
+        w.step(es)
+        g_in = swap_state(leading, after)
+        (branch,) = tie(branch, *w.sent)[:1]
+        do = tn(att, branch).astype(bf16)
+        do, g_in = tie(do, g_in)
+        w.after = (g_in,)
+        do = jnp.split(do, QUADS)
+        r_far_last = w.swap(r_cut[1], "head", 2)
+
+        def back_beside(w, k, g_in):
+            w.step(ss)
+            (g_in,) = w.open(g_in)
+            parts = (q01, k01, v01) if k < 2 else (q23, k23, v23)
+            gp[k], da, ba_part = back((k,), *parts, g_in)
+            gp[k], da, ba_part, g_in = w.close(gp[k], da, ba_part, g_in)
+            return da, ba_part, g_in
+
+        o_got = w.swap(do[3], "head", 1), w.swap(do[1], "head", 1)
+        da3, ba3, g_in = back_beside(w, 3, g_in)
+
+        o_far = (do[2].astype(f32) + o_got[0].get().astype(f32)).astype(bf16)
+        r_far = jnp.concatenate([r_far.get(), r_far_last.get()], axis=0)
+        rs = Stages(sum_stages([dr[0], near[1], r_far]))
+        w = Window(g_in)
+        w.step(es)
+        w.step(rs)
+        a_got = w.swap(da3, "head", 1)
+        o_far = w.swap(o_far, "head", 2)
+        da2, ba2, g_in = back_beside(w, 2, g_in)
+
+        a_far = (da2.astype(f32) + a_got.get().astype(f32)).astype(bf16)
+        os = Stages(sum_stages([do[0], o_got[1].get(), o_far.get()]))
+        a_cut = jnp.split(a_far, 2)
+        w = Window(g_in)
+        a_far = w.swap(a_cut[0], "head", 2)
+        w.step(rs)
+        w.step(os)
+        da1, ba1, g_in = back_beside(w, 1, g_in)
+
+        w = Window(g_in)
+        a_far_last = w.swap(a_cut[1], "head", 2)
+        a_near = w.swap(da1, "head", 1)
+        w.step(es)
+        w.step(os)
+        da0, ba0, g_in = back_beside(w, 0, g_in)
+
+        a_far = jnp.concatenate([a_far.get(), a_far_last.get()], axis=0)
+        at = Stages(sum_stages([da0, a_near.get(), a_far]))
+        w = Window(g_in)
+        w.step(at)
+        w.step(rs)
+        w.step(ss)
+        half = tiles // 2
+        (layer_in,) = w.open(layer_input)
+        input_grad, sums1 = inputs(0, half, None, layer_in)
+        input_grad, sums1 = w.close(input_grad, sums1)
+        w = Window(input_grad)
+        w.step(at)
+        w.step(es)
+        w.step(os)
+        (input_grad,) = w.open(input_grad)
+        input_grad, more = inputs(half, tiles - half, input_grad, layer_in)
+        input_grad, more = w.close(input_grad, more)
+        sums1 = sums1 + more
+        expand_weight_grad = es.finish()
+        reduce_weight_grad = rs.finish()
+        attend_weight_grad = at.finish()
+        output_weight_grad = os.finish()
+        ba_sum = jnp.concatenate([ba0, ba1, ba2, ba3], axis=1)
+    else:
+        g_in = swap_state(leading, after)
+        gp[2], gp[3], *da23, ba23 = back((2, 3), q23, k23, v23, g_in)
+        gp[0], gp[1], *da01, ba01 = back((0, 1), q01, k01, v01, g_in)
+        do = [tn(att, branch).astype(bf16)]
+
+        def reduce(grads, axis):
+            return Stages(sum_stages([scatter_head(regroup(grads, n, axis))])).finish()
+
+        expand_weight_grad = reduce(de, 1)
+        reduce_weight_grad = reduce(dr, 0)
+        attend_weight_grad = reduce(da01 + da23, 1)
+        output_weight_grad = reduce(do, 0)
+        input_grad, sums1 = inputs(0, tiles, None, layer_input)
+        ba_sum = jnp.concatenate([ba01, ba23], axis=1)
+
+    shared2, expand_bias_grad = ss.finish()
+    shared1, attend_bias_grad = Stages(
+        small_stages(
+            jnp.sum(sums1.reshape(2, 8, D), axis=1),
+            regroup([jnp.sum(ba_sum, axis=0)], n, 0),
+        )
+    ).finish()
     return (
         layer_output,
         input_grad,

time: 855 us -> 690 us (0.81)
  waiting for transfers between devices: 329 us -> 64.9 us
  Pallas kernels: 296 us -> 438 us
  matrix products: 100 us -> 7.54 us
  other arithmetic: 34.7 us -> 69.4 us
  local copies, waits for them, and re-layouts: 5.82 us -> 19.1 us
    ppermute x70 -> x77, waiting for transfers between devices: 329 us -> 64.9 us  [swap(): return lax.ppermute(value, axis, [(i, i ^ bit) for i in range(size)])]
    pallas_call x5 -> x13, Pallas kernels: 296 us -> 438 us  [call(): pl.pallas_call(kernel, grid_spec=pltpu.PrefetchScalarGridSpec(num_scalar_...]
    dot_general x13 -> x1, matrix products: 100 us -> 7.54 us  [tn(): lax.dot_general(a, b, (((0,), (0,)), ((), ())), preferred_element_type=f32)]
    convert_element_type x18 -> x20, other arithmetic: 12.8 us -> 39.1 us  [the longest x4 12.8 us: half(): return total.astype(bf16)]
    ppermute x70 -> x77, starting transfers between devices: 79.4 us -> 80.3 us  [swap(): return lax.ppermute(value, axis, [(i, i ^ bit) for i in range(size)])]
  transfers between devices with their start and end apart: 70 -> 77, of which waited for: 26 -> 18; matrix products, arithmetic and copies ran while one was open for 16% -> 10% of each run, Pallas kernels for 19% -> 64%
where the time goes in v2:
time: 690 us; the launch traced here: 681 us
  Pallas kernels  438 us (63%)
  starting transfers between devices  80.3 us (12%)
  other arithmetic  69.4 us (10%)
  waiting for transfers between devices  64.9 us (9%)
  local copies, waits for them, and re-layouts  19.1 us (3%)
  matrix products  7.54 us (1%)
    pallas_call x13, Pallas kernels, call(): pl.pallas_call(kernel, grid_spec=pltpu.PrefetchScalarGridSpec(num_scalar_...  438 us
    ppermute x77, starting transfers between devices, swap(): return lax.ppermute(value, axis, [(i, i ^ bit) for i in range(size)])  80.3 us
    ppermute x77, waiting for transfers between devices, swap(): return lax.ppermute(value, axis, [(i, i ^ bit) for i in range(size)])  64.9 us
  transfers between devices with their start and end apart: 77, of which 18 were waited for; matrix products, arithmetic and copies ran while one was open for 10% of the time, Pallas kernels for 64%

profile of v2, /device:TPU:8, one launch (start us, length us, event | category | flops | bytes accessed | tf_op | source)
XLA Modules:
  0.0 680.8 jit_solution(2804499948621665771)
XLA Ops:
  13.2 22.1 %qkv.2 = (bf16[2560,512]{1,0:T(8,128)(2,1)}, bf16[2560,512]{1,0:T(8,128)(2,1)}, bf16[2560,512]{1,0:T(8,128)(2,1)}, bf16[2560,1024]{1,0:T(8,128)(2,1)}, f32[72,512]{1,0:T(8,128)}) custom-call(s32[20]{0:T(128)} %subtract_maximum_fusion.thr, s32[20]{0:T(128)} %get-tuple-element.538.last, bf16[2560,1024]{1,0:T(8,128)(2,1)} %x.1, f32[1,1024]{1,0:T(1,128)} %bitcast.97, ...), custom_call_target="tpu_custom_call" | custom-call | flops 8053063680 | bytes 24117248 | tf_op jit(solution)/shard_map/qkv/pallas_call | solution.py:429
  46.3 19.1 %qkv.3 = (bf16[2560,512]{1,0:T(8,128)(2,1)}, bf16[2560,512]{1,0:T(8,128)(2,1)}, bf16[2560,512]{1,0:T(8,128)(2,1)}, f32[72,512]{1,0:T(8,128)}) custom-call(s32[20]{0:T(128)} %subtract_maximum_fusion.thr, s32[20]{0:T(128)} %get-tuple-element.538.last, bf16[2560,1024]{1,0:T(8,128)(2,1)} %get-tuple-element.250.refs_0_.normed, bf16[1024,768]{1,0:T(8,128)(2,1)} %copy-done.1, ...), custom_call_target="tpu_custom_call" | custom-call | flops 8053063680 | bytes 24117248 | tf_op jit(solution)/shard_map/qkv/pallas_call | solution.py:429
  71.7 4.0 collective-permute-done.11
  79.9 38.2 %attend.1 = (bf16[2560,1024]{1,0:T(8,128)(2,1)}, f32[2560,1024]{1,0:T(8,128)}, bf16[1280,1024]{1,0:T(8,128)(2,1)}, f32[160,1024]{1,0:T(8,128)}, f32[2560,1024]{1,0:T(8,128)}, /*index=5*/bf16[2560,1024]{1,0:T(8,128)(2,1)}) custom-call(s32[21]{0:T(128)} %add_convert_fusion.20.cont, s32[20]{0:T(128)} %subtract_maximum_fusion.thr, ...), custom_call_target="tpu_custom_call" | custom-call | flops 32212254720 | bytes 52428800 | tf_op jit(solution)/shard_map/attend/pallas_call | solution.py:429
  118.1 7.3 %collective-permute-done.14.refs_6_ = bf16[1024,1024]{1,0:T(8,128)(2,1)} collective-permute-done((bf16[1024,1024]{1,0:T(8,128)(2,1)}, bf16[1024,1024]{1,0:T(8,128)(2,1)}, u32[]{:S(2)}, u32[]{:S(2)}) %collective-permute-start.14) | collective-permute-done | bytes 2097184 | tf_op jit(solution)/shard_map/ppermute | solution.py:452
  126.4 50.1 %ffn.4 = (bf16[1024,1024]{1,0:T(8,128)(2,1)}, bf16[1024,1024]{1,0:T(8,128)(2,1)}, f32[8,1024]{1,0:T(8,128)}, f32[2560,1024]{1,0:T(8,128)}, f32[2560,1024]{1,0:T(8,128)}) custom-call(bf16[2560,1024]{1,0:T(8,128)(2,1)} %get-tuple-element.280.refs_0_.refs_1_, bf16[2560,1024]{1,0:T(8,128)(2,1)} %refs_2_.1, f32[1,1024]{1,0:T(1,128)} %bitcast.103, ...), custom_call_target="tpu_custom_call" | custom-call | flops 32212254720 | bytes 52428800 | tf_op jit(solution)/shard_map/ffn/pallas_call | solution.py:429
  182.4 50.7 %ffn.5 = (bf16[1024,1024]{1,0:T(8,128)(2,1)}, bf16[1024,1024]{1,0:T(8,128)(2,1)}, f32[8,1024]{1,0:T(8,128)}, f32[2560,1024]{1,0:T(8,128)}, f32[2560,1024]{1,0:T(8,128)}) custom-call(bf16[2560,1024]{1,0:T(8,128)(2,1)} %get-tuple-element.280.refs_0_.refs_1_, bf16[2560,1024]{1,0:T(8,128)(2,1)} %refs_2_.1, f32[1,1024]{1,0:T(1,128)} %bitcast.101, ...), custom_call_target="tpu_custom_call" | custom-call | flops 32212254720 | bytes 52428800 | tf_op jit(solution)/shard_map/ffn/pallas_call | solution.py:429
  234.4 51.2 %ffn.6 = (bf16[1024,1024]{1,0:T(8,128)(2,1)}, bf16[1024,1024]{1,0:T(8,128)(2,1)}, f32[8,1024]{1,0:T(8,128)}, f32[2560,1024]{1,0:T(8,128)}, f32[2560,1024]{1,0:T(8,128)}) custom-call(bf16[2560,1024]{1,0:T(8,128)(2,1)} %get-tuple-element.280.refs_0_.refs_1_, bf16[2560,1024]{1,0:T(8,128)(2,1)} %refs_2_.1, f32[1,1024]{1,0:T(1,128)} %bitcast.100, ...), custom_call_target="tpu_custom_call" | custom-call | flops 32212254720 | bytes 52428800 | tf_op jit(solution)/shard_map/ffn/pallas_call | solution.py:429
  286.4 4.1 add_convert_fusion.1
  296.6 70.8 %ffn.7 = (bf16[1024,1024]{1,0:T(8,128)(2,1)}, bf16[1024,1024]{1,0:T(8,128)(2,1)}, f32[8,1024]{1,0:T(8,128)}, bf16[2560,1024]{1,0:T(8,128)(2,1)}, f32[2560,1024]{...) custom-call(s32[20]{0:T(128)} %get-tuple-element.539.refs_0_, ...), custom_call_target="tpu_custom_call" | custom-call | flops 32212254720 | bytes 52428800 | tf_op jit(solution)/shard_map/ffn/pallas_call | solution.py:429
  371.3 6.0 collective-permute-start.25
  377.3 5.3 add_convert_fusion.7
  383.0 7.5 %convolution_convert_fusion = bf16[1024,1024]{1,0:T(8,128)(2,1)S(1)} fusion(bf16[2560,1024]{1,0:T(8,128)(2,1)} %get-tuple-element.313.refs_9_, bf16[2560,1024]{1,0:T(8,128)(2,1)S(1)} %copy-done.35), kind=kOutput, calls=%fused_computation.11 | convolution fusion | flops 5369757696 | bytes 12582912 | tf_op jit(solution)/shard_map/dot_general | solution.py:32
  395.7 25.7 %attend_back.4 = (bf16[2560,768]{1,0:T(8,128)(2,1)}, bf16[1024,768]{1,0:T(8,128)(2,1)}, f32[8,768]{1,0:T(8,128)}) custom-call(s32[21]{0:T(128)} %add_convert_fusion.20.cont, bf16[2560,512]{1,0:T(8,128)(2,1)} %get-tuple-element.257.refs_3_.refs_12_.q, bf16[2560,512]{1,0:T(8,128)(2,1)} %get-tuple-element.258.refs_4_.k, ...), custom_call_target="tpu_custom_call" | custom-call | flops 16106127360 | bytes 13107200 | tf_op jit(solution)/shard_map/attend_back/pallas_call | solution.py:429
  439.5 25.4 %attend_back.5 = (bf16[2560,768]{1,0:T(8,128)(2,1)}, bf16[1024,768]{1,0:T(8,128)(2,1)}, f32[8,768]{1,0:T(8,128)}) custom-call(s32[21]{0:T(128)} %add_convert_fusion.20.cont, bf16[2560,512]{1,0:T(8,128)(2,1)} %get-tuple-element.257.refs_3_.refs_12_.q, bf16[2560,512]{1,0:T(8,128)(2,1)} %get-tuple-element.258.refs_4_.k, ...), custom_call_target="tpu_custom_call" | custom-call | flops 16106127360 | bytes 13107200 | tf_op jit(solution)/shard_map/attend_back/pallas_call | solution.py:429
  478.5 25.9 %attend_back.6 = (bf16[2560,768]{1,0:T(8,128)(2,1)}, bf16[1024,768]{1,0:T(8,128)(2,1)}, f32[8,768]{1,0:T(8,128)}) custom-call(s32[21]{0:T(128)} %add_convert_fusion.20.cont, bf16[2560,512]{1,0:T(8,128)(2,1)} %get-tuple-element.243.refs_0_.refs_11_.q, bf16[2560,512]{1,0:T(8,128)(2,1)} %get-tuple-element.244.refs_1_.k, ...), custom_call_target="tpu_custom_call" | custom-call | flops 16106127360 | bytes 13107200 | tf_op jit(solution)/shard_map/attend_back/pallas_call | solution.py:429
  513.7 25.6 %attend_back.7 = (bf16[2560,768]{1,0:T(8,128)(2,1)}, bf16[1024,768]{1,0:T(8,128)(2,1)}, f32[8,768]{1,0:T(8,128)}) custom-call(s32[21]{0:T(128)} %add_convert_fusion.20.cont, bf16[2560,512]{1,0:T(8,128)(2,1)} %get-tuple-element.243.refs_0_.refs_11_.q, bf16[2560,512]{1,0:T(8,128)(2,1)} %get-tuple-element.244.refs_1_.k, ...), custom_call_target="tpu_custom_call" | custom-call | flops 16106127360 | bytes 13107200 | tf_op jit(solution)/shard_map/attend_back/pallas_call | solution.py:429
  549.1 9.3 %collective-permute-done.51 = bf16[32,1024]{1,0:T(8,128)(2,1)S(1)} collective-permute-done((bf16[32,1024]{1,0:T(8,128)(2,1)}, bf16[32,1024]{1,0:T(8,128)(2,1)S(1)}, u32[]{:S(2)}, u32[]{:S(2)}) %collective-permute-start.51) | collective-permute-done | bytes 65568 | tf_op jit(solution)/shard_map/ppermute | solution.py:452
  571.1 16.3 %input_grad.2 = (f32[2560,1024]{1,0:T(8,128)}, f32[16,1024]{1,0:T(8,128)}) custom-call(bf16[2560,1024]{1,0:T(8,128)(2,1)} %x.1, f32[2560,1024]{1,0:T(8,128)} %get-tuple-element.418.gm, f32[1,1024]{1,0:T(1,128)} %bitcast.98, bf16[2560,768]{1,0:T(8,128)(2,1)} %get-tuple-element.419.refs_0_, bf16[2560,768]{1,0:T(8,128)(2,1)} %get-tuple-element.420.refs_1_, ...), custom_call_target="tpu_custom_call" | custom-call | flops 8053063680 | bytes 20971520 | tf_op jit(solution)/shard_map/input_grad/pallas_call | solution.py:429
  597.5 16.4 %input_grad.3 = (f32[2560,1024]{1,0:T(8,128)}, f32[16,1024]{1,0:T(8,128)}) custom-call(bf16[2560,1024]{1,0:T(8,128)(2,1)} %x.1, f32[2560,1024]{1,0:T(8,128)} %get-tuple-element.418.gm, f32[1,1024]{1,0:T(1,128)} %bitcast.99, bf16[2560,768]{1,0:T(8,128)(2,1)} %get-tuple-element.419.refs_0_, ...), custom_call_target="tpu_custom_call", output_to_operand_aliasing={{0}: (11, {})} | custom-call | flops 8053063680 | bytes 20971520 | tf_op jit(solution)/shard_map/input_grad/pallas_call | solution.py:429
  618.8 7.2 %collective-permute-done.60 = bf16[128,768]{1,0:T(8,128)(2,1)S(1)} collective-permute-done((bf16[128,768]{1,0:T(8,128)(2,1)S(1)}, bf16[128,768]{1,0:T(8,128)(2,1)S(1)}, u32[]{:S(2)}, u32[]{:S(2)}) %collective-permute-start.60) | collective-permute-done | bytes 196640 | tf_op jit(solution)/shard_map/ppermute | solution.py:452
  626.1 5.4 collective-permute-done.61
  657.5 5.7 collective-permute-done.75
  667.9 10.3 %collective-permute-done.74 = bf16[512,768]{1,0:T(8,128)(2,1)S(1)} collective-permute-done((bf16[512,768]{1,0:T(8,128)(2,1)S(1)}, bf16[512,768]{1,0:T(8,128)(2,1)S(1)}, u32[]{:S(2)}, u32[]{:S(2)}) %collective-permute-start.74) | collective-permute-done | bytes 786464 | tf_op jit(solution)/shard_map/ppermute | solution.py:452
  (337 shorter events, 169.2 us)
Async XLA Ops:
  1.2 36.9 %collective-permute-start.3 = (bf16[1024,768]{1,0:T(8,128)(2,1)}, bf16[1024,768]{1,0:T(8,128)(2,1)S(1)}, u32[]{:S(2)}, u32[]{:S(2)}) collective-permute-start(bf16[1024,768]{1,0:T(8,128)(2,1)} %refs_4_.3), channel_id=1, source_target_pairs={{0,2},{1,3},{2,0},{3,1},{4,6},{5,7},{6,4},{7,5},{8,10},{9,11},{10,... | collective-permute-start | bytes 4718600 | tf_op jit(solution)/shard_map/ppermute | solution.py:452
  2.7 35.4 %collective-permute-start.7 = (bf16[1024,1024]{1,0:T(8,128)(2,1)}, bf16[1024,1024]{1,0:T(8,128)(2,1)}, u32[]{:S(2)}, u32[]{:S(2)}) collective-permute-start(bf16[1024,1024]{1,0:T(8,128)(2,1)} %refs_7_.1), channel_id=1, source_target_pairs={{0,1},{1,0},{2,3},{3,2},{4,5},{5,4},{6,7},{7,6},{8,9},{9,8},{10,11... | collective-permute-start | bytes 6291464 | tf_op jit(solution)/shard_map/ppermute | solution.py:452
  2.7 35.4 %collective-permute-start.6 = (bf16[1024,1024]{1,0:T(8,128)(2,1)}, bf16[1024,1024]{1,0:T(8,128)(2,1)}, u32[]{:S(2)}, u32[]{:S(2)}) collective-permute-start(bf16[1024,1024]{1,0:T(8,128)(2,1)} %refs_6_.3), channel_id=1, source_target_pairs={{0,1},{1,0},{2,3},{3,2},{4,5},{5,4},{6,7},{7,6},{8,9},{9,8},{10,11... | collective-permute-start | bytes 6291464 | tf_op jit(solution)/shard_map/ppermute | solution.py:452
  78.5 46.9 %collective-permute-start.14 = (bf16[1024,1024]{1,0:T(8,128)(2,1)}, bf16[1024,1024]{1,0:T(8,128)(2,1)}, u32[]{:S(2)}, u32[]{:S(2)}) collective-permute-start(bf16[1024,1024]{1,0:T(8,128)(2,1)} %refs_7_.1), channel_id=1, source_target_pairs={{0,2},{1,3},{2,0},{3,1},{4,6},{5,7},{6,4},{7,5},{8,10},{9,11},{10,... | collective-permute-start | bytes 6291464 | tf_op jit(solution)/shard_map/ppermute | solution.py:452
  125.4 51.1 %collective-permute-start.15 = (bf16[1024,1024]{1,0:T(8,128)(2,1)S(1)}, bf16[1024,1024]{1,0:T(8,128)(2,1)}, u32[]{:S(2)}, u32[]{:S(2)}) collective-permute-start(bf16[1024,1024]{1,0:T(8,128)(2,1)S(1)} %copy-done.32), channel_id=1, source_target_pairs={{0,2},{1,3},{2,0},{3,1},{4,6},{5,7},{6,4},{7,5},{8,10},{9,11},{10,... | collective-permute-start | bytes 6291464 | tf_op jit(solution)/shard_map/ppermute | solution.py:452
  126.4 50.1 %collective-permute-start.16 = (bf16[1024,1024]{1,0:T(8,128)(2,1)}, bf16[1024,1024]{1,0:T(8,128)(2,1)}, u32[]{:S(2)}, u32[]{:S(2)}) collective-permute-start(bf16[1024,1024]{1,0:T(8,128)(2,1)} %collective-permute-done.14.refs_6_), channel_id=1, source_target_pairs={{0,1},{1,0},{2,3},{3,2},{4,5},{5,4},{6,7},{7,6},{8,9},{9,8},{10,11... | collective-permute-start | bytes 6291464 | tf_op jit(solution)/shard_map/ppermute | solution.py:452
  179.0 54.0 %collective-permute-start.18 = (bf16[1024,1024]{1,0:T(8,128)(2,1)}, bf16[1024,1024]{1,0:T(8,128)(2,1)}, u32[]{:S(2)}, u32[]{:S(2)}) collective-permute-start(bf16[1024,1024]{1,0:T(8,128)(2,1)} %get-tuple-element.283), channel_id=1, source_target_pairs={{0,1},{1,0},{2,3},{3,2},{4,5},{5,4},{6,7},{7,6},{8,9},{9,8},{10,11... | collective-permute-start | bytes 6291464 | tf_op jit(solution)/shard_map/ppermute | solution.py:452
  179.2 53.8 %collective-permute-start.19 = (bf16[1024,1024]{1,0:T(8,128)(2,1)}, bf16[1024,1024]{1,0:T(8,128)(2,1)}, u32[]{:S(2)}, u32[]{:S(2)}) collective-permute-start(bf16[1024,1024]{1,0:T(8,128)(2,1)} %get-tuple-element.285), channel_id=1, source_target_pairs={{0,1},{1,0},{2,3},{3,2},{4,5},{5,4},{6,7},{7,6},{8,9},{9,8},{10,11... | collective-permute-start | bytes 6291464 | tf_op jit(solution)/shard_map/ppermute | solution.py:452
  233.1 53.4 %collective-permute-start.20 = (bf16[1024,1024]{1,0:T(8,128)(2,1)}, bf16[1024,1024]{1,0:T(8,128)(2,1)S(1)}, u32[]{:S(2)}, u32[]{:S(2)}) collective-permute-start(bf16[1024,1024]{1,0:T(8,128)(2,1)} %get-tuple-element.294), channel_id=1, source_target_pairs={{0,1},{1,0},{2,3},{3,2},{4,5},{5,4},{6,7},{7,6},{8,9},{9,8},{10,11... | collective-permute-start | bytes 6291464 | tf_op jit(solution)/shard_map/ppermute | solution.py:452
  233.5 53.0 %collective-permute-start.21 = (bf16[1024,1024]{1,0:T(8,128)(2,1)}, bf16[1024,1024]{1,0:T(8,128)(2,1)}, u32[]{:S(2)}, u32[]{:S(2)}) collective-permute-start(bf16[1024,1024]{1,0:T(8,128)(2,1)} %get-tuple-element.296), channel_id=1, source_target_pairs={{0,1},{1,0},{2,3},{3,2},{4,5},{5,4},{6,7},{7,6},{8,9},{9,8},{10,11... | collective-permute-start | bytes 6291464 | tf_op jit(solution)/shard_map/ppermute | solution.py:452
  294.6 73.6 %collective-permute-start.23 = (bf16[512,1024]{1,0:T(8,128)(2,1)}, bf16[512,1024]{1,0:T(8,128)(2,1)S(1)}, u32[]{:S(2)}, u32[]{:S(2)}) collective-permute-start(bf16[512,1024]{1,0:T(8,128)(2,1)} %get-tuple-element.309), channel_id=1, source_target_pairs={{0,2},{1,3},{2,0},{3,1},{4,6},{5,7},{6,4},{7,5},{8,10},{9,11},{10,... | collective-permute-start | bytes 3145736 | tf_op jit(solution)/shard_map/ppermute | solution.py:452
  295.5 72.7 %collective-permute-start.22 = (bf16[1024,1024]{1,0:T(8,128)(2,1)}, bf16[1024,1024]{1,0:T(8,128)(2,1)S(1)}, u32[]{:S(2)}, u32[]{:S(2)}) collective-permute-start(bf16[1024,1024]{1,0:T(8,128)(2,1)} %add_convert_fusion.1), channel_id=1, source_target_pairs={{0,2},{1,3},{2,0},{3,1},{4,6},{5,7},{6,4},{7,5},{8,10},{9,11},{10,... | collective-permute-start | bytes 6291464 | tf_op jit(solution)/shard_map/ppermute | solution.py:452
  382.6 38.9 %collective-permute-start.27 = (bf16[512,1024]{1,0:T(8,128)(2,1)}, bf16[512,1024]{1,0:T(8,128)(2,1)}, u32[]{:S(2)}, u32[]{:S(2)}) collective-permute-start(bf16[512,1024]{1,0:T(8,128)(2,1)} %get-tuple-element.333), channel_id=1, source_target_pairs={{0,4},{4,0},{8,12},{12,8},{16,20},{20,16},{24,28},{28,24},{1,5},{5... | collective-permute-start | bytes 3145736 | tf_op jit(solution)/shard_map/ppermute | solution.py:452
  429.6 35.5 %collective-permute-start.36 = (bf16[1024,768]{1,0:T(8,128)(2,1)}, bf16[1024,768]{1,0:T(8,128)(2,1)}, u32[]{:S(2)}, u32[]{:S(2)}) collective-permute-start(bf16[1024,768]{1,0:T(8,128)(2,1)} %get-tuple-element.362), channel_id=1, source_target_pairs={{0,1},{1,0},{2,3},{3,2},{4,5},{5,4},{6,7},{7,6},{8,9},{9,8},{10,11... | collective-permute-start | bytes 4718600 | tf_op jit(solution)/shard_map/ppermute | solution.py:452
  473.5 34.1 %collective-permute-start.40 = (bf16[128,1024]{1,0:T(8,128)(2,1)}, bf16[128,1024]{1,0:T(8,128)(2,1)S(1)}, u32[]{:S(2)}, u32[]{:S(2)}) collective-permute-start(bf16[128,1024]{1,0:T(8,128)(2,1)} %get-tuple-element.377), channel_id=1, source_target_pairs={{0,8},{4,12},{8,0},{12,4},{16,24},{20,28},{24,16},{28,20},{1,9},{5... | collective-permute-start | bytes 786440 | tf_op jit(solution)/shard_map/ppermute | solution.py:452
  475.2 35.2 %collective-permute-start.41 = (bf16[128,1024]{1,0:T(8,128)(2,1)}, bf16[128,1024]{1,0:T(8,128)(2,1)S(1)}, u32[]{:S(2)}, u32[]{:S(2)}) collective-permute-start(bf16[128,1024]{1,0:T(8,128)(2,1)} %get-tuple-element.378), channel_id=1, source_target_pairs={{0,16},{4,20},{8,24},{12,28},{16,0},{20,4},{24,8},{28,12},{1,17},{... | collective-permute-start | bytes 786440 | tf_op jit(solution)/shard_map/ppermute | solution.py:452
  477.0 33.5 %collective-permute-start.42 = (bf16[128,1024]{1,0:T(8,128)(2,1)}, bf16[128,1024]{1,0:T(8,128)(2,1)S(1)}, u32[]{:S(2)}, u32[]{:S(2)}) collective-permute-start(bf16[128,1024]{1,0:T(8,128)(2,1)} %get-tuple-element.379), channel_id=1, source_target_pairs={{0,24},{4,28},{8,16},{12,20},{16,8},{20,12},{24,0},{28,4},{1,25},{... | collective-permute-start | bytes 786440 | tf_op jit(solution)/shard_map/ppermute | solution.py:452
  505.6 33.8 %collective-permute-start.49 = (bf16[128,1024]{1,0:T(8,128)(2,1)S(1)}, bf16[128,1024]{1,0:T(8,128)(2,1)S(1)}, u32[]{:S(2)}, u32[]{:S(2)}) collective-permute-start(bf16[128,1024]{1,0:T(8,128)(2,1)S(1)} %add_convert_fusion.15), channel_id=1, source_target_pairs={{0,24},{4,28},{8,16},{12,20},{16,8},{20,12},{24,0},{28,4},{1,25},{... | collective-permute-start | bytes 786440 | tf_op jit(solution)/shard_map/ppermute | solution.py:452
  507.7 34.1 %collective-permute-start.48 = (bf16[128,1024]{1,0:T(8,128)(2,1)S(1)}, bf16[128,1024]{1,0:T(8,128)(2,1)}, u32[]{:S(2)}, u32[]{:S(2)}) collective-permute-start(bf16[128,1024]{1,0:T(8,128)(2,1)S(1)} %add_convert_fusion.15), channel_id=1, source_target_pairs={{0,16},{4,20},{8,24},{12,28},{16,0},{20,4},{24,8},{28,12},{1,17},{... | collective-permute-start | bytes 786440 | tf_op jit(solution)/shard_map/ppermute | solution.py:452
  512.4 50.2 %collective-permute-start.45 = (bf16[512,768]{1,0:T(8,128)(2,1)}, bf16[512,768]{1,0:T(8,128)(2,1)}, u32[]{:S(2)}, u32[]{:S(2)}) collective-permute-start(bf16[512,768]{1,0:T(8,128)(2,1)} %get-tuple-element.391), channel_id=1, source_target_pairs={{0,2},{1,3},{2,0},{3,1},{4,6},{5,7},{6,4},{7,5},{8,10},{9,11},{10,... | collective-permute-start | bytes 2359304 | tf_op jit(solution)/shard_map/ppermute | solution.py:452
  513.7 48.8 %collective-permute-start.46 = (bf16[1024,768]{1,0:T(8,128)(2,1)}, bf16[1024,768]{1,0:T(8,128)(2,1)S(1)}, u32[]{:S(2)}, u32[]{:S(2)}) collective-permute-start(bf16[1024,768]{1,0:T(8,128)(2,1)} %get-tuple-element.393), channel_id=1, source_target_pairs={{0,1},{1,0},{2,3},{3,2},{4,5},{5,4},{6,7},{7,6},{8,9},{9,8},{10,11... | collective-permute-start | bytes 4718600 | tf_op jit(solution)/shard_map/ppermute | solution.py:452
  546.3 42.7 %collective-permute-start.57 = (bf16[128,1024]{1,0:T(8,128)(2,1)S(1)}, bf16[128,1024]{1,0:T(8,128)(2,1)}, u32[]{:S(2)}, u32[]{:S(2)}) collective-permute-start(bf16[128,1024]{1,0:T(8,128)(2,1)S(1)} %add_convert_fusion.13), channel_id=1, source_target_pairs={{0,24},{4,28},{8,16},{12,20},{16,8},{20,12},{24,0},{28,4},{1,25},{... | collective-permute-start | bytes 786440 | tf_op jit(solution)/shard_map/ppermute | solution.py:452
  592.6 38.8 %collective-permute-start.62 = (bf16[512,1024]{1,0:T(8,128)(2,1)S(1)}, bf16[512,1024]{1,0:T(8,128)(2,1)}, u32[]{:S(2)}, u32[]{:S(2)}) collective-permute-start(bf16[512,1024]{1,0:T(8,128)(2,1)S(1)} %pad_maximum_fusion), channel_id=1, source_target_pairs={{0,4},{4,0},{8,12},{12,8},{16,20},{20,16},{24,28},{28,24},{1,5},{5... | collective-permute-start | bytes 3145736 | tf_op jit(solution)/shard_map/ppermute | solution.py:452
  616.9 47.6 %collective-permute-start.76 = (bf16[512,1024]{1,0:T(8,128)(2,1)S(1)}, bf16[512,1024]{1,0:T(8,128)(2,1)S(1)}, u32[]{:S(2)}, u32[]{:S(2)}) collective-permute-start(bf16[512,1024]{1,0:T(8,128)(2,1)S(1)} %pad_maximum_fusion.1), channel_id=1, source_target_pairs={{0,4},{4,0},{8,12},{12,8},{16,20},{20,16},{24,28},{28,24},{1,5},{5... | collective-permute-start | bytes 3145736 | tf_op jit(solution)/shard_map/ppermute | solution.py:452
  (89 other events, 1309.4 us)

commit v3 on v2

--- a/solution.py
+++ b/solution.py
@@ -32,24 +32,25 @@
     return lax.dot_general(a, b, (((0,), (0,)), ((), ())), preferred_element_type=f32)
 
 
-def head_rows():
-    lane = lax.broadcasted_iota(jnp.int32, (1, QW), 1) // DH
-    return [(lane == h).astype(f32) for h in range(4)]
-
-
-def spread_heads(block, picks):
-    return jnp.concatenate([block * pick for pick in picks], axis=0)
-
-
-def spread_state(state, picks):
-    return jnp.concatenate([state * pick for pick in picks], axis=0)
-
-
-def gather_state(square, picks):
-    total = square[0:DH] * picks[0]
-    for h in range(1, 4):
-        total = total + square[h * DH : (h + 1) * DH] * picks[h]
-    return total
+PAIR = 2 * DH
+
+
+def side_rows(kind):
+    lane = lax.broadcasted_iota(jnp.int32, (1, PAIR), 1) // DH
+    return [(lane == h).astype(kind) for h in range(2)]
+
+
+def spread(block, picks):
+    return jnp.concatenate([block * picks[0], block * picks[1]], axis=0)
+
+
+def pair_product(left, right, picks):
+    square = tn(left, right)
+    return square[0:DH] * picks[0] + square[DH:PAIR] * picks[1]
+
+
+def cut(start, width=PAIR):
+    return slice(start * width, (start + 1) * width)
 
 
 def centre(values):
@@ -86,23 +87,24 @@
     return jnp.where(v < 0, tail, 1.0 - tail), bell
 
 
-def qkv_kernel(blocks, fresh, thr, last, *refs):
+def qkv_kernel(blocks, fresh, thr, cont, *refs):
     if fresh:
         x, gain, shift, n_out = refs[0], refs[1], refs[2], refs[9]
         wa, ba = refs[3:5], refs[5]
         q_out, k_out, v_out = refs[6:9]
-        t_out = refs[10]
+        t_out, st_out, kt_out, state, sums = refs[10:15]
     else:
         n_in = refs[0]
         wa, ba = refs[1:3], refs[3]
         q_out, k_out, v_out = refs[4:7]
-        t_out = refs[7]
+        t_out, st_out, kt_out, state, sums = refs[7:12]
     step = pl.program_id(0)
     rows = blocks * STRETCH
 
     @pl.when(step == 0)
     def _():
-        t_out[...] = jnp.zeros_like(t_out)
+        state[...] = jnp.zeros_like(state)
+        sums[...] = jnp.zeros_like(sums)
 
     if fresh:
         xhat, _ = centre(x[...].astype(f32))
@@ -130,63 +132,60 @@
             key = pltpu.roll(jnp.where(low, c2, c0), DH, 1)
             k_out[:, at] = (valid * feature(key)).astype(bf16)
             v_out[:, at] = jnp.where(low, c1, c2).astype(bf16)
-    picks = head_rows()
-    for b in range(blocks):
-
-        @pl.when(last[step * blocks + b] == 1)
-        def _(b=b):
-            here = slice(b * STRETCH, (b + 1) * STRETCH)
-            for g in range(2):
-                at = slice(g * QW, (g + 1) * QW)
-                key = k_out[here, at]
-                t_out[0:DH, at] += gather_state(tn(key, v_out[here, at]), picks)
-                t_out[DH : DH + 8, at] += fold_rows(key.astype(f32))
-
-
-def attend_kernel(blocks, cont, thr, *refs):
-    qkv = refs[0:3], refs[3:6]
-    x, s_in, ones, bo, gain, shift = refs[6:12]
-    wo = refs[12:16]
-    att_out, rec_out, st_out, kt_out, mid_out, n_out = refs[16:22]
-    state, total = refs[22:24]
-    step = pl.program_id(0)
-
-    @pl.when(step == 0)
-    def _():
-        state[...] = s_in[0:DH]
-        total[...] = jnp.broadcast_to(
-            jnp.sum(s_in[DH : DH + 8], axis=0, keepdims=True), total.shape
-        )
-
-    picks = head_rows()
-    low_picks = [p.astype(bf16) for p in picks]
-    row = lax.broadcasted_iota(jnp.int32, (STRETCH, 512), 0)
-    lane = lax.broadcasted_iota(jnp.int32, (STRETCH, 512), 1) % STRETCH
-    lower = lane <= row
+    picks = side_rows(f32)
     for b in range(blocks):
         keep = cont[step * blocks + b].astype(f32)
-        here = slice(b * STRETCH, (b + 1) * STRETCH)
+        here = cut(b, STRETCH)
         state[...] = state[...] * keep
-        total[...] = total[...] * keep
-        low_state = state[...].astype(bf16)
-        st_out[b * DH : (b + 1) * DH, :] = low_state
-        kt_out[b * 8 : (b + 1) * 8, :] = total[...]
-        for g in range(QUADS):
-            at = slice(g * QW, (g + 1) * QW)
-            own = slice((g % 2) * QW, (g % 2 + 1) * QW)
-            qb, kb, vb = (part[here, own] for part in qkv[g // 2])
-            scores = nt(qb, spread_heads(kb, low_picks))
+        sums[...] = sums[...] * keep
+        st_out[cut(b, DH), :] = state[...]
+        kt_out[cut(b, 8), :] = sums[...]
+        for p in range(4):
+            key = k_out[here, cut(p)]
+            state[:, cut(p)] += pair_product(key, v_out[here, cut(p)], picks)
+            sums[:, cut(p)] += fold_rows(key.astype(f32))
+
+    @pl.when(step == pl.num_programs(0) - 1)
+    def _():
+        t_out[0:DH, :] = state[...]
+        t_out[DH : DH + 8, :] = sums[...]
+
+
+def attend_kernel(blocks, first, thr, *refs):
+    qkv = refs[0:5], refs[5:10]
+    x, s_in, bo, gain, shift = refs[10:15]
+    wo = refs[15:19]
+    att_out, rec_out, st_out, kt_out, mid_out, n_out = refs[19:25]
+    step = pl.program_id(0)
+    picks = side_rows(bf16)
+    row = lax.broadcasted_iota(jnp.int32, (STRETCH, 2 * STRETCH), 0)
+    lane = lax.broadcasted_iota(jnp.int32, (STRETCH, 2 * STRETCH), 1) % STRETCH
+    lower = lane <= row
+    ones_scores = spread(jnp.ones((STRETCH, PAIR), bf16), picks)
+    ones_state = spread(jnp.ones((DH, PAIR), bf16), picks)
+    zeros = jnp.zeros((PAIR, PAIR), bf16)
+    ones = jnp.concatenate([ones_scores, zeros, ones_state], axis=0)
+    came = jnp.sum(s_in[DH : DH + 8], axis=0, keepdims=True)
+    for b in range(blocks):
+        joins = first[step * blocks + b].astype(f32)
+        here = cut(b, STRETCH)
+        for p in range(8):
+            at, own = cut(p), cut(p % 4)
+            q, k, v, st, kt = qkv[p // 4]
+            qb, kb, vb = q[here, own], k[here, own], v[here, own]
+            state = (st[cut(b, DH), own] + joins * s_in[0:DH, at]).astype(bf16)
+            total = jnp.sum(kt[cut(b, 8), own], axis=0, keepdims=True) + joins * came[:, at]
+            st_out[cut(b, DH), at] = state
+            kt_out[cut(b, 8), at] = jnp.broadcast_to(total, (8, PAIR))
+            scores = nt(qb, spread(kb, picks))
             scores = jnp.where(lower, scores, 0.0).astype(bf16)
-            numer = nn(scores, spread_heads(vb, low_picks)) + nn(
-                qb, spread_state(low_state[:, at], low_picks)
-            )
-            weighted = (qb.astype(f32) * total[0:1, at]).astype(bf16)
-            denom = nn(scores, ones[0:512]) + nn(weighted, ones[512:768])
-            rec = 1.0 / jnp.maximum(denom, 1.0)
+            weighted = (qb.astype(f32) * total).astype(bf16)
+            left = jnp.concatenate([scores, qb, weighted], axis=1)
+            right = jnp.concatenate([spread(vb, picks), spread(state, picks), zeros], axis=0)
+            both = nn(left, jnp.concatenate([right, ones], axis=1))
+            rec = 1.0 / jnp.maximum(both[:, PAIR:], 1.0)
             rec_out[here, at] = rec
-            att_out[here, at] = (numer * rec).astype(bf16)
-            state[:, at] += gather_state(tn(kb, vb), picks)
-            total[:, at] += jnp.sum(kb.astype(f32), axis=0, keepdims=True)
+            att_out[here, at] = (both[:, :PAIR] * rec).astype(bf16)
     place = lax.broadcasted_iota(jnp.int32, (STRETCH, D), 0)
     for b in range(blocks):
         here = slice(b * STRETCH, (b + 1) * STRETCH)
@@ -205,7 +204,7 @@
     n_out[...] = (xhat * gain[...] + shift[...]).astype(bf16)
 
 
-def ffn_kernel(blocks, slots, fresh, final, *refs):
+def ffn_kernel(blocks, widths, fresh, final, *refs):
     refs = list(refs)
 
     def take(count):
@@ -213,28 +212,28 @@
         del refs[:count]
         return taken
 
-    count = sum(len(widths) for widths in slots)
+    count = len(widths)
     if final:
         (first,) = take(1)
     n2, cot = take(2)
-    be = take(len(slots))
+    be = take(count)
     if not fresh:
         part_out, part_grad = take(2)
     we, wr = take(count), take(count)
     if final:
-        mid, att, rec, q01, q23, gain, br, ones = take(8)
+        mid, att, rec, q01, q23, gain, br = take(7)
         wo = take(4)
-    de_out, dr_out, be_sum = take(len(slots)), take(len(slots)), take(len(slots))
+    grad_out, be_sum = take(count), take(count)
     if final:
-        out, gm_out, gb_out, gn_out, t_out, l_out, sums = take(7)
+        out, gm_out, gb_out, gn_out, t_out, l_out, pr_out, kr_out, sums = take(9)
     else:
         next_out, next_grad = take(2)
-    de_sum, dr_sum = take(len(slots)), take(len(slots))
+    grad_sum = take(count)
     step = pl.program_id(0)
 
     @pl.when(step == 0)
     def _():
-        for total in de_sum + dr_sum + be_sum:
+        for total in grad_sum + be_sum:
             total[...] = jnp.zeros_like(total)
         if final:
             l_out[...] = jnp.zeros_like(l_out)
@@ -244,29 +243,23 @@
     cotangent = cot[...]
     reduced = None if fresh else part_out[...]
     grad = None if fresh else part_grad[...]
-    i = 0
-    for slot, widths in enumerate(slots):
-        start = 0
-        for width in widths:
-            at = slice(start, start + width)
-            hidden = nn(normed, we[i][...]) + be[slot][:, at]
-            grad_act = nt(cotangent, wr[i][...])
-            phi, bell = normal_parts(hidden)
-            active = (hidden * phi).astype(bf16)
-            back = (grad_act * (phi + hidden * (0.3989422804014327 * bell))).astype(bf16)
-            be_sum[slot][:, at] += fold_rows(back.astype(f32))
-            de_sum[slot][:, at] += tn(normed, back)
-            dr_sum[slot][at, :] += tn(active, cotangent)
-            more = nn(active, wr[i][...])
-            reduced = more if reduced is None else reduced + more
-            more = nt(back, we[i][...])
-            grad = more if grad is None else grad + more
-            start += width
-            i += 1
+    for i, width in enumerate(widths):
+        hidden = nn(normed, we[i][...]) + be[i][...]
+        grad_act = nt(cotangent, wr[i][...])
+        phi, bell = normal_parts(hidden)
+        active = (hidden * phi).astype(bf16)
+        back = (grad_act * (phi + hidden * (0.3989422804014327 * bell))).astype(bf16)
+        be_sum[i][...] += fold_rows(back.astype(f32))
+        grad_sum[i][0:width, :] += tn(back, normed)
+        grad_sum[i][width : 2 * width, :] += tn(active, cotangent)
+        more = nn(active, wr[i][...])
+        reduced = more if reduced is None else reduced + more
+        more = nt(back, we[i][...])
+        grad = more if grad is None else grad + more
 
     @pl.when(step == pl.num_programs(0) - 1)
     def _():
-        for out_ref, total in zip(de_out + dr_out, de_sum + dr_sum):
+        for out_ref, total in zip(grad_out, grad_sum):
             out_ref[...] = total[...].astype(bf16)
 
     if not final:
@@ -294,21 +287,24 @@
         t_out[:, at] = jnp.where(
             share < 1.0, -(numer * att[:, at].astype(f32)), 0.0
         ).astype(bf16)
-    picks = head_rows()
+    picks = side_rows(f32)
+    ones = spread(jnp.ones((DH, PAIR), bf16), side_rows(bf16))
     for b in range(blocks):
+        here = cut(b, STRETCH)
+        for p in range(8):
+            at = cut(p)
+            query = (q01, q23)[p // 4][here, cut(p % 4)]
+            pr_out[cut(b, DH), at] = pair_product(query, gn_out[here, at], picks)
+            grad_denom = nn(t_out[here, at], ones)
+            kr_out[cut(b, 8), at] = fold_rows(grad_denom * query.astype(f32))
 
         @pl.when(first[step * blocks + b] == 1)
         def _(b=b):
-            here = slice(b * STRETCH, (b + 1) * STRETCH)
-            for g in range(QUADS):
-                at = slice(g * QW, (g + 1) * QW)
-                query = (q01, q23)[g // 2][here, (g % 2) * QW : (g % 2 + 1) * QW]
-                l_out[0:DH, at] += gather_state(tn(query, gn_out[here, at]), picks)
-                grad_denom = nn(t_out[here, at], ones[512:768])
-                l_out[DH : DH + 8, at] += fold_rows(grad_denom * query.astype(f32))
-
-
-def back_kernel(blocks, tiles, quads, cont, q, k, v, gn, t, st, kt, g_in, ones, normed, *refs):
+            l_out[0:DH, :] += pr_out[cut(b, DH), :]
+            l_out[DH : DH + 8, :] += kr_out[cut(b, 8), :]
+
+
+def back_kernel(blocks, tiles, quads, cont, q, k, v, gn, t, st, kt, pr, kr, g_in, normed, att, branch, *refs):
     gp_out, da_out, ba_sum = refs[0:quads], refs[quads : 2 * quads], refs[2 * quads]
     state, total = refs[2 * quads + 1 : 2 * quads + 3]
     da_sum = refs[2 * quads + 3 :]
@@ -325,63 +321,65 @@
         for da in da_sum:
             da[...] = jnp.zeros_like(da)
 
-    picks = head_rows()
-    low_picks = [p.astype(bf16) for p in picks]
-    row = lax.broadcasted_iota(jnp.int32, (STRETCH, 512), 0)
-    lane = lax.broadcasted_iota(jnp.int32, (STRETCH, 512), 1) % STRETCH
+    picks = side_rows(bf16)
+    row = lax.broadcasted_iota(jnp.int32, (STRETCH, 2 * STRETCH), 0)
+    lane = lax.broadcasted_iota(jnp.int32, (STRETCH, 2 * STRETCH), 1) % STRETCH
     lower = lane <= row
     upper = lane >= row
-    low_lane = lax.broadcasted_iota(jnp.int32, (STRETCH, 128), 1) < DH
-    all_ones = jnp.ones((STRETCH, QW), bf16)
+    low_lane = lax.broadcasted_iota(jnp.int32, (STRETCH, PAIR), 1) < DH
+    all_ones = jnp.ones((STRETCH, PAIR), bf16)
+    ones_scores = spread(all_ones, picks)
+    ones_state = spread(jnp.ones((DH, PAIR), bf16), picks)
     for b in reversed(range(blocks)):
         keep = cont[tile * blocks + b + 1].astype(f32)
-        here = slice(b * STRETCH, (b + 1) * STRETCH)
-        state[...] = state[...] * keep
-        total[...] = total[...] * keep
-        low_state = state[...].astype(bf16)
-        for g in range(quads):
-            at = slice(g * QW, (g + 1) * QW)
+        here = cut(b, STRETCH)
+        for p in range(2 * quads):
+            at = cut(p)
             qb, kb, vb, gb, tb = q[here, at], k[here, at], v[here, at], gn[here, at], t[here, at]
-            q_wide = qb.astype(f32)
-            spread_q = spread_heads(qb, low_picks)
-            spread_g = spread_heads(gb, low_picks)
-            forward = spread_state(st[b * DH : (b + 1) * DH, at], low_picks)
-            behind = spread_state(low_state[:, at], low_picks)
-            scores = nt(gb, spread_heads(vb, low_picks)) + nt(tb, ones[0:512])
+            state_here = state[:, at] * keep
+            total_here = total[:, at] * keep
+            behind = spread(state_here.astype(bf16), picks)
+            state[:, at] = state_here + pr[cut(b, DH), at]
+            total[:, at] = total_here + jnp.sum(kr[cut(b, 8), at], axis=0, keepdims=True)
+            spread_q, spread_g = spread(qb, picks), spread(gb, picks)
+            forward = spread(st[cut(b, DH), at], picks)
+            scores = nt(
+                jnp.concatenate([gb, tb], axis=1),
+                jnp.concatenate([spread(vb, picks), ones_scores], axis=1),
+            )
             scores = jnp.where(lower, scores, 0.0).astype(bf16)
-            turned = nt(vb, spread_g) + nt(all_ones, spread_heads(tb, low_picks))
+            turned = nt(
+                jnp.concatenate([vb, all_ones], axis=1),
+                jnp.concatenate([spread_g, spread(tb, picks)], axis=1),
+            )
             turned = jnp.where(upper, turned, 0.0).astype(bf16)
             mixed = jnp.where(upper, nt(kb, spread_q), 0.0).astype(bf16)
-            grad_denom = nn(tb, ones[512:768])
+            grad_denom = nn(tb, ones_state)
             grad_q = (
-                nn(scores, spread_heads(kb, low_picks))
+                nn(scores, spread(kb, picks))
                 + nt(gb, forward)
                 + grad_denom * kt[b * 8 : b * 8 + 1, at]
             )
-            grad_k = nn(turned, spread_q) + nt(vb, behind) + total[0:1, at]
-            grad_v = nn(mixed, spread_g) + nn(kb, behind)
-            grad_q = grad_q * jnp.minimum(q_wide, 1.0)
+            grad_k = nn(turned, spread_q) + nt(vb, behind) + total_here[0:1]
+            grad_v = nn(jnp.concatenate([mixed, kb], axis=1), jnp.concatenate([spread_g, behind]))
+            grad_q = grad_q * jnp.minimum(qb.astype(f32), 1.0)
             grad_k = grad_k * jnp.minimum(kb.astype(f32), 1.0)
-            for pair in range(2):
-                two = slice(pair * 128, (pair + 1) * 128)
-                swapped = pltpu.roll(grad_k[:, two], DH, 1)
-                for j, piece in enumerate(
-                    (
-                        jnp.where(low_lane, grad_q[:, two], swapped),
-                        jnp.where(low_lane, grad_v[:, two], grad_q[:, two]),
-                        jnp.where(low_lane, swapped, grad_v[:, two]),
-                    )
-                ):
-                    piece = piece.astype(bf16)
-                    start = pair * 384 + j * 128
-                    gp_out[g][here, start : start + 128] = piece
-                    ba_sum[:, g * PW + start : g * PW + start + 128] += fold_rows(
-                        piece.astype(f32)
-                    )
-            state[:, at] += gather_state(tn(qb, gb), picks)
-            total[:, at] += jnp.sum(grad_denom * q_wide, axis=0, keepdims=True)
+            swapped = pltpu.roll(grad_k, DH, 1)
+            for j, piece in enumerate(
+                (
+                    jnp.where(low_lane, grad_q, swapped),
+                    jnp.where(low_lane, grad_v, grad_q),
+                    jnp.where(low_lane, swapped, grad_v),
+                )
+            ):
+                piece = piece.astype(bf16)
+                start = (p % 2) * 384 + j * 128
+                gp_out[p // 2][here, start : start + 128] = piece
+                start += (p // 2) * PW
+                ba_sum[:, start : start + 128] += fold_rows(piece.astype(f32))
     for g in range(quads):
-        da_sum[g][...] += tn(normed[...], gp_out[g][...])
+        da_sum[g][0:PW, :] += tn(gp_out[g][...], normed[...])
+        da_sum[g][PW:, :] += tn(att[:, cut(g, QW)], branch[...])
 
     @pl.when(step == tiles - 1)
     def _():
@@ -419,6 +417,10 @@
     return pl.BlockSpec(
         shape, lambda i, *_: (0,) * last + (at,), pipeline_mode=pl.Buffered(1)
     )
+
+
+def part_spec(shape, at):
+    return pl.BlockSpec(shape, lambda i, *_: (at, 0), pipeline_mode=pl.Buffered(1))
 
 
 def sum_spec(shape):
@@ -517,10 +519,10 @@
     def finish(self):
         while self.advance():
             pass
-        return self.got[0]
-
-
-def sum_stages(terms):
+        return self.got
+
+
+def sum_stages(terms, apart=False):
     size = lax.axis_size("dp")
     me = lax.axis_index("dp")
     x, z, depth = me % 2, me // 2, size // 2
@@ -547,8 +549,22 @@
         total = total + part.astype(f32)
     (own,) = tie(total.astype(bf16))
     got = yield [own], [swap(own, "dp", 2 * j) for j in range(1, depth)]
-    (mine,) = tie(jnp.concatenate([own] + list(got), axis=0))
-    (other,) = yield [mine], [swap(mine, "dp", 1)]
+    if apart:
+        parts = [own] + list(got)
+        got = yield parts, [swap(part, "dp", 1) for part in parts]
+        mine, other = jnp.concatenate(parts, axis=0), jnp.concatenate(list(got), axis=0)
+    else:
+        (mine,) = tie(jnp.concatenate([own] + list(got), axis=0))
+        (other,) = yield [mine], [swap(mine, "dp", 1)]
+
+    yield [], [mine, other]
+
+
+def whole_sum(stages):
+    mine, other = stages.finish()
+    me = lax.axis_index("dp")
+    x, z, depth = me % 2, me // 2, lax.axis_size("dp") // 2
+    rows = mine.shape[0] // depth
 
     def natural(value):
         for bit in bits_of(depth):
@@ -559,7 +575,19 @@
 
     mine, other = natural(mine), natural(other)
     pair = [jnp.where(x == 0, mine, other), jnp.where(x == 0, other, mine)]
-    yield [], [jnp.concatenate(pair, axis=0).astype(f32)]
+    return jnp.concatenate(pair, axis=0).astype(f32)
+
+
+def place_kernel(depth, half, where, *refs):
+    sources, out = refs[0:4], refs[4]
+    step = pl.program_id(0)
+    for unit in range(2):
+        for side in range(2):
+
+            @pl.when(jnp.logical_and(step // depth == unit, where[0] == side))
+            def _(unit=unit, side=side):
+                part = sources[2 * unit + (side ^ half)][...].astype(f32)
+                out[...] = part if half else part.T
 
 
 class Window:
@@ -616,7 +644,7 @@
         (both,) = tie(both)
         (got,) = yield [both], [swap(both, "dp", bit)]
         both = both + got
-    yield [], [(both[: flat.shape[0]].reshape(shared.shape), both[flat.shape[0] :])]
+    yield [], [both[: flat.shape[0]].reshape(shared.shape), both[flat.shape[0] :]]
 
 
 def on_device(
@@ -675,7 +703,6 @@
     padding = jnp.sum(jnp.where(belongs, pads[None, :], 0), axis=1)
     thr = jnp.maximum(padding - (spots - opening) * STRETCH, 0).astype(jnp.int32)
     first = (crop == crop[0]).astype(jnp.int32)
-    last = (crop == crop[nb - 1]).astype(jnp.int32)
     one = jnp.ones((1,), jnp.int32)
     cont = jnp.concatenate([one, (crop[1:] == crop[:-1]).astype(jnp.int32), one])
     others = me ^ jnp.arange(n, dtype=jnp.int32)
@@ -683,10 +710,6 @@
     closes = crop_of(others * nb + nb - 1)
     before = jnp.logical_and(others < me, closes == crop[0]).astype(f32)
     after = jnp.logical_and(others > me, opens == crop[nb - 1]).astype(f32)
-
-    line = lax.broadcasted_iota(jnp.int32, (768, QW), 0)
-    lane_head = lax.broadcasted_iota(jnp.int32, (768, QW), 1) // DH
-    ones = (jnp.where(line < 512, line // STRETCH, (line - 512) // DH) == lane_head).astype(bf16)
 
     blocks = 2 if nb % 2 == 0 else 1
     rows = blocks * STRETCH
@@ -711,15 +734,19 @@
         ins += [(wa[k], whole_spec((D, PW))) for k in pick]
         ins += [(bias, whole_spec((1, 2 * PW)))]
         outs = [narrow] * 3 + ([low] if fresh else [])
-        outs += [(like((state_rows, HALF), f32), sum_spec((state_rows, HALF)))]
+        outs += [
+            (like((state_rows, HALF), f32), sum_spec((state_rows, HALF))),
+            (like((nb * DH, HALF), f32), rows_spec(blocks * DH, HALF)),
+            (like((nb * 8, HALF), f32), rows_spec(blocks * 8, HALF)),
+        ]
         return call(
             functools.partial(qkv_kernel, blocks, fresh),
             "qkv",
-            (thr, last),
+            (thr, cont),
             tiles,
             ins,
             outs,
-            [],
+            [pltpu.VMEM((DH, HALF), f32), pltpu.VMEM((8, HALF), f32)],
             3 * R * D * D,
             8 * R * D + 3 * D * D,
         )
@@ -728,7 +755,7 @@
     source = layer_input
     if fast:
         source, bias = w.open(source, bias)
-    q01, k01, v01, normed, trail01 = project(source, (0, 1), bias, True)
+    q01, k01, v01, normed, trail01, st01, kt01 = project(source, (0, 1), bias, True)
     if fast:
         q01, k01, v01, normed, trail01 = w.close(q01, k01, v01, normed, trail01)
         wa[2] = wa_far.get()
@@ -744,7 +771,7 @@
         we = regroup(gather_shards(expand_weight), QUADS, 1)
         wr = regroup(gather_shards(reduce_weight), QUADS, 0)
         be_slots = jnp.split(jnp.concatenate(gather_shards(expand_bias)), QUADS)
-    q23, k23, v23, trail23 = project(normed, (2, 3), ba_far[None, :], False)
+    q23, k23, v23, trail23, st23, kt23 = project(normed, (2, 3), ba_far[None, :], False)
     if fast:
         q23, k23, v23, trail23 = w.close(q23, k23, v23, trail23)
         wo[2] = wo_far.get()
@@ -758,13 +785,19 @@
     att, rec, st, kt, middle, n2 = call(
         functools.partial(attend_kernel, blocks),
         "attend",
-        (cont, thr),
+        (first, thr),
         tiles,
-        [(a, side) for a in (q01, k01, v01, q23, k23, v23)]
+        [
+            (a, spec)
+            for part in ((q01, k01, v01, st01, kt01), (q23, k23, v23, st23, kt23))
+            for a, spec in zip(
+                part,
+                [side] * 3 + [rows_spec(blocks * DH, HALF), rows_spec(blocks * 8, HALF)],
+            )
+        ]
         + [
             (layer_input, full),
             (s_in, whole_spec((state_rows, D))),
-            (ones, whole_spec((768, QW))),
             vector(output_bias[None, :]),
             vector(gain2),
             vector(shift2),
@@ -778,7 +811,7 @@
             wide,
             low,
         ],
-        [pltpu.VMEM((DH, D), f32), pltpu.VMEM((8, D), f32)],
+        [],
         12 * R * D * D,
         20 * R * D,
     )
@@ -789,16 +822,16 @@
         wr = [reduce_weight, wr_near.get(), wr_far.get(), None]
 
     def ffn(picks, part, extra):
-        slots = [[FQ]] * len(picks)
+        widths = [FQ if half is None else FQ // 2 for _, half in picks]
+        spots = [(k, width, half or 0) for (k, half), width in zip(picks, widths)]
         ins = [(n2, full), (cotangent, full)]
-        ins += [(be_slots[k][None, :], whole_spec((1, FQ))) for k in picks]
+        ins += [(be_slots[k][None, :], whole_spec((1, width), at)) for k, width, at in spots]
         if part is not None:
             ins += [(part[0], full), (part[1], full)]
-        ins += [(we[k], whole_spec(we[k].shape)) for k in picks]
-        ins += [(wr[k], whole_spec(wr[k].shape)) for k in picks]
-        outs = [(like((D, FQ), bf16), whole_spec((D, FQ)))] * len(picks)
-        outs += [(like((FQ, D), bf16), whole_spec((FQ, D)))] * len(picks)
-        outs += [(like((8, FQ), f32), sum_spec((8, FQ)))] * len(picks)
+        ins += [(we[k], whole_spec((D, width), at)) for k, width, at in spots]
+        ins += [(wr[k], part_spec((width, D), at)) for k, width, at in spots]
+        outs = [(like((2 * w, D), bf16), whole_spec((2 * w, D))) for w in widths]
+        outs += [(like((8, w), f32), sum_spec((8, w))) for w in widths]
         if extra is None:
             outs += [wide, wide]
         else:
@@ -806,24 +839,26 @@
             outs += [low, wide, low, low, low]
             outs += [
                 (like((state_rows, D), f32), sum_spec((state_rows, D))),
+                (like((nb * DH, D), f32), rows_spec(blocks * DH, D)),
+                (like((nb * 8, D), f32), rows_spec(blocks * 8, D)),
                 (like((32, D), f32), sum_spec((32, D))),
             ]
         results = call(
-            functools.partial(ffn_kernel, blocks, slots, part is None, extra is not None),
+            functools.partial(ffn_kernel, blocks, widths, part is None, extra is not None),
             "ffn",
             (first,) if extra is not None else (),
             tiles,
             ins,
             outs,
-            [pltpu.VMEM((D, FQ), f32)] * len(picks) + [pltpu.VMEM((FQ, D), f32)] * len(picks),
-            12 * R * D * FQ * len(picks),
+            [pltpu.VMEM((2 * w, D), f32) for w in widths],
+            12 * R * D * sum(widths),
             20 * R * D,
         )
-        for i, k in enumerate(picks):
-            de[k], dr[k], eb[k] = (results[i + j * len(picks)] for j in range(3))
-        return list(results[3 * len(picks) :])
-
-    de, dr, eb = [None] * 4, [None] * 4, [None] * 4
+        for i, (k, half) in enumerate(picks):
+            eb[k].append(results[len(picks) + i])
+        return list(results[: len(picks)]), list(results[2 * len(picks) :])
+
+    eb = [[], [], [], []]
     extra = [
         (middle, full),
         (att, full),
@@ -832,44 +867,52 @@
         (q23, side),
         vector(gain2),
         vector(reduce_bias[None, :]),
-        (ones, whole_spec((768, QW))),
     ] + [(w, whole_spec((QW, D))) for w in wo]
+    def total(*terms):
+        return sum(term.astype(f32) for term in terms).astype(bf16)
+
     if fast:
         w = Window(n2)
         we_far = w.swap(expand_weight, "head", 2)
         wr_last = w.swap(wr[2], "head", 1)
         (n2,) = w.open(n2)
-        part = ffn((1,), None, None)
-        n2, *part = w.close(n2, *part)
+        (near, own), part = ffn([(1, 0), (0, 0)], None, None)
+        n2, near, own, *part = w.close(n2, near, own, *part)
         we[2], wr[3] = we_far.get(), wr_last.get()
         we[3] = swap(we[2], "head", 1)
         w = Window(part[0])
-        near = w.swap(de[1], "head", 1), w.swap(dr[1], "head", 1)
+        near = w.swap(near, "head", 1)
         (part[0],) = w.open(part[0])
-        part = ffn((3,), part, None)
-        part = w.close(*part)
-        near = [late.get() for late in near]
+        (last_far, far), part = ffn([(3, 0), (2, 0)], part, None)
+        last_far, far, *part = w.close(last_far, far, *part)
+        far = total(far, swap(last_far, "head", 1))
+        near_a = near.get()
         w = Window(part[0])
-        got = w.swap(de[3], "head", 1), w.swap(dr[3], "head", 1)
+        far = w.swap(far, "head", 2)
         (part[0],) = w.open(part[0])
-        part = ffn((2,), part, None)
-        part[0], part[1], de[2], dr[2] = w.close(*part, de[2], dr[2])
-        far = [
-            (a.astype(f32) + b.get().astype(f32)).astype(bf16)
-            for a, b in zip((de[2], dr[2]), got)
-        ]
+        (last_far, far_b), part = ffn([(3, 1), (2, 1)], part, None)
+        last_far, far_b, *part = w.close(last_far, far_b, *part)
+        sum_a = Stages(sum_stages([own, near_a, far.get()]))
+        far = total(far_b, swap(last_far, "head", 1))
         w = Window(part[0])
-        r_cut = jnp.split(far[1], 2)
-        e_far = w.swap(far[0], "head", 2)
-        r_far = w.swap(r_cut[0], "head", 2)
+        w.step(sum_a)
+        far, part[0] = w.open(far, part[0])
+        (near,), part = ffn([(1, 1)], part, None)
+        near, *part = w.close(near, *part)
+        w = Window(part[0])
+        far = w.swap(far, "head", 2)
+        near = w.swap(near, "head", 1)
+        w.step(sum_a)
         (part[0],) = w.open(part[0])
-        results = ffn((0,), part, extra)
-        de[0], dr[0], *results = w.close(de[0], dr[0], *results)
+        (own,), results = ffn([(0, 1)], part, extra)
+        own, *results = w.close(own, *results)
+        far, near = far.get(), near.get()
     else:
-        part = ffn((3,), None, None)
-        part = ffn((2,), part, None)
-        results = ffn((1, 0), part, extra)
-    layer_output, grad_middle, branch, gn, t, leading, sums2 = results
+        grads, part = [None] * 4, None
+        for k in (3, 2, 1):
+            (grads[k],), part = ffn([(k, None)], part, None)
+        (grads[0],), results = ffn([(0, None)], part, extra)
+    layer_output, grad_middle, branch, gn, t, leading, pr, kr, sums2 = results
 
     def back(pick, q, k, v, state):
         count = len(pick)
@@ -884,15 +927,18 @@
             + [
                 (st, back_spec(blocks * DH, width, tiles, at)),
                 (kt, back_spec(blocks * 8, width, tiles, at)),
+                (pr, back_spec(blocks * DH, width, tiles, at)),
+                (kr, back_spec(blocks * 8, width, tiles, at)),
                 (state, whole_spec((state_rows, width), at)),
-                (ones, whole_spec((768, QW))),
                 (normed, back_spec(rows, D, tiles)),
+                (att, back_spec(rows, width, tiles, at)),
+                (branch, back_spec(rows, D, tiles)),
             ],
             [(like((R, PW), bf16), back_spec(rows, PW, tiles))] * count
-            + [(like((D, PW), bf16), whole_spec((D, PW)))] * count
+            + [(like((PW + QW, D), bf16), whole_spec((PW + QW, D)))] * count
             + [(like((8, count * PW), f32), sum_spec((8, count * PW)))],
             [pltpu.VMEM((DH, width), f32), pltpu.VMEM((8, width), f32)]
-            + [pltpu.VMEM((D, PW), f32)] * count,
+            + [pltpu.VMEM((PW + QW, D), f32)] * count,
             6 * count * R * D * D,
             5 * count * R * D,
         )
@@ -918,104 +964,105 @@
         )
 
     gp = [None] * 4
-    shared2 = jnp.sum(sums2.reshape(4, 8, D), axis=1)
-    eb = regroup([jnp.sum(e, axis=0) for e in eb], n, 0)
-    ss = Stages(small_stages(shared2, eb))
     if fast:
-        es = Stages(sum_stages([de[0], near[0], e_far.get()]))
-        w = Window(branch)
-        w.step(es)
         g_in = swap_state(leading, after)
-        (branch,) = tie(branch, *w.sent)[:1]
-        do = tn(att, branch).astype(bf16)
-        do, g_in = tie(do, g_in)
-        w.after = (g_in,)
-        do = jnp.split(do, QUADS)
-        r_far_last = w.swap(r_cut[1], "head", 2)
-
-        def back_beside(w, k, g_in):
-            w.step(ss)
-            (g_in,) = w.open(g_in)
-            parts = (q01, k01, v01) if k < 2 else (q23, k23, v23)
-            gp[k], da, ba_part = back((k,), *parts, g_in)
-            gp[k], da, ba_part, g_in = w.close(gp[k], da, ba_part, g_in)
-            return da, ba_part, g_in
-
-        o_got = w.swap(do[3], "head", 1), w.swap(do[1], "head", 1)
-        da3, ba3, g_in = back_beside(w, 3, g_in)
-
-        o_far = (do[2].astype(f32) + o_got[0].get().astype(f32)).astype(bf16)
-        r_far = jnp.concatenate([r_far.get(), r_far_last.get()], axis=0)
-        rs = Stages(sum_stages([dr[0], near[1], r_far]))
+        sum_b = Stages(sum_stages([own, near, far]))
         w = Window(g_in)
-        w.step(es)
-        w.step(rs)
-        a_got = w.swap(da3, "head", 1)
-        o_far = w.swap(o_far, "head", 2)
-        da2, ba2, g_in = back_beside(w, 2, g_in)
-
-        a_far = (da2.astype(f32) + a_got.get().astype(f32)).astype(bf16)
-        os = Stages(sum_stages([do[0], o_got[1].get(), o_far.get()]))
-        a_cut = jnp.split(a_far, 2)
+        w.step(sum_b)
+        w.step(sum_a)
+        (g_in,) = w.open(g_in)
+        gp[2], gp[3], da2, da3, ba23 = back((2, 3), q23, k23, v23, g_in)
+        gp[2], gp[3], da2, da3, ba23, g_in = w.close(gp[2], gp[3], da2, da3, ba23, g_in)
+
+        far = total(da2, swap(da3, "head", 1))
         w = Window(g_in)
-        a_far = w.swap(a_cut[0], "head", 2)
-        w.step(rs)
-        w.step(os)
-        da1, ba1, g_in = back_beside(w, 1, g_in)
-
-        w = Window(g_in)
-        a_far_last = w.swap(a_cut[1], "head", 2)
-        a_near = w.swap(da1, "head", 1)
-        w.step(es)
-        w.step(os)
-        da0, ba0, g_in = back_beside(w, 0, g_in)
-
-        a_far = jnp.concatenate([a_far.get(), a_far_last.get()], axis=0)
-        at = Stages(sum_stages([da0, a_near.get(), a_far]))
-        w = Window(g_in)
-        w.step(at)
-        w.step(rs)
-        w.step(ss)
+        far = w.swap(far, "head", 2)
+        w.step(sum_b)
+        w.step(sum_a)
+        (g_in,) = w.open(g_in)
+        gp[0], gp[1], da0, da1, ba01 = back((0, 1), q01, k01, v01, g_in)
+        gp[0], gp[1], da0, da1, ba01 = w.close(gp[0], gp[1], da0, da1, ba01)
+        near = swap(da1, "head", 1)
+        sum_c = Stages(sum_stages([da0, near, far.get()], True))
+        w = Window(gp[0])
+        w.step(sum_c)
+        w.step(sum_b)
         half = tiles // 2
         (layer_in,) = w.open(layer_input)
         input_grad, sums1 = inputs(0, half, None, layer_in)
         input_grad, sums1 = w.close(input_grad, sums1)
         w = Window(input_grad)
-        w.step(at)
-        w.step(es)
-        w.step(os)
+        w.step(sum_c)
+        w.step(sum_b)
         (input_grad,) = w.open(input_grad)
         input_grad, more = inputs(half, tiles - half, input_grad, layer_in)
         input_grad, more = w.close(input_grad, more)
         sums1 = sums1 + more
-        expand_weight_grad = es.finish()
-        reduce_weight_grad = rs.finish()
-        attend_weight_grad = at.finish()
-        output_weight_grad = os.finish()
-        ba_sum = jnp.concatenate([ba0, ba1, ba2, ba3], axis=1)
+        where = lax.axis_index("dp")
+        where = jnp.stack([where % 2, where // 2]).astype(jnp.int32)
+        depth = lax.axis_size("dp") // 2
+        piece = FQ // 2 // depth
+
+        def source(unit):
+            def index(i, where):
+                at = jnp.where(i // depth == unit, i % depth, 0 if unit else depth - 1)
+                return (at ^ where[1], 0)
+
+            return pl.BlockSpec((piece, D), index)
+
+        ins = [(v, source(0)) for v in sum_a.finish()] + [(v, source(1)) for v in sum_b.finish()]
+
+        def placed(half, shape, block, index):
+            w = Window(input_grad)
+            w.step(sum_c)
+            (at,) = w.open(where)
+            out = call(
+                functools.partial(place_kernel, depth, half),
+                "place",
+                (at,),
+                2 * depth,
+                ins,
+                [(like(shape, f32), pl.BlockSpec(block, index))],
+                [],
+                0,
+                6 * FQ * D,
+            )
+            return w.close(*out)[0]
+
+        expand_weight_grad = placed(0, (D, FQ), (D, piece), lambda i, *_: (0, i))
+        sums1 = tie(sums1, expand_weight_grad)[0]
+        eb = [list(tie(*parts, sums1)[: len(parts)]) for parts in eb]
+        reduce_weight_grad = placed(1, (FQ, D), (piece, D), lambda i, *_: (i, 0))
+        sum_c = whole_sum(sum_c)
+        attend_weight_grad, output_weight_grad = sum_c[:PW].T, sum_c[PW:]
     else:
         g_in = swap_state(leading, after)
         gp[2], gp[3], *da23, ba23 = back((2, 3), q23, k23, v23, g_in)
         gp[0], gp[1], *da01, ba01 = back((0, 1), q01, k01, v01, g_in)
-        do = [tn(att, branch).astype(bf16)]
-
-        def reduce(grads, axis):
-            return Stages(sum_stages([scatter_head(regroup(grads, n, axis))])).finish()
-
-        expand_weight_grad = reduce(de, 1)
-        reduce_weight_grad = reduce(dr, 0)
-        attend_weight_grad = reduce(da01 + da23, 1)
-        output_weight_grad = reduce(do, 0)
+        da = da01 + da23
+
+        def reduce(parts):
+            return whole_sum(Stages(sum_stages([scatter_head(regroup(parts, n, 0))])))
+
+        expand_weight_grad = reduce([g[:FQ] for g in grads]).T
+        reduce_weight_grad = reduce([g[FQ:] for g in grads])
+        attend_weight_grad = reduce([g[:PW] for g in da]).T
+        output_weight_grad = reduce([g[PW:] for g in da])
         input_grad, sums1 = inputs(0, tiles, None, layer_input)
-        ba_sum = jnp.concatenate([ba01, ba23], axis=1)
-
-    shared2, expand_bias_grad = ss.finish()
-    shared1, attend_bias_grad = Stages(
-        small_stages(
+
+    eb = [jnp.sum(jnp.concatenate(parts, axis=1), axis=0) for parts in eb]
+    eb = regroup(eb, n, 0)
+    ab = regroup([jnp.sum(jnp.concatenate([ba01, ba23], axis=1), axis=0)], n, 0)
+    shared = jnp.concatenate(
+        [
             jnp.sum(sums1.reshape(2, 8, D), axis=1),
-            regroup([jnp.sum(ba_sum, axis=0)], n, 0),
-        )
-    ).finish()
+            jnp.sum(sums2.reshape(4, 8, D), axis=1),
+        ]
+    )
+    split = [jnp.concatenate(both) for both in zip(eb, ab)]
+    shared, split = Stages(small_stages(shared, split)).finish()
+    shared1, shared2 = shared[:2], shared[2:]
+    expand_bias_grad, attend_bias_grad = split[: eb[0].shape[0]], split[eb[0].shape[0] :]
     return (
         layer_output,
         input_grad,

time: 690 us -> 651 us (0.943)
  starting transfers between devices: 80.3 us -> 49.9 us
  other arithmetic: 69.4 us -> 52 us
  waiting for transfers between devices: 64.9 us -> 79.7 us
  matrix products: 7.54 us -> 0 us
    ppermute x77 -> x62, starting transfers between devices: 80.3 us -> 49.9 us  [swap(): return lax.ppermute(value, axis, [(i, i ^ bit) for i in range(size)])]
    ppermute x77 -> x62, waiting for transfers between devices: 64.9 us -> 79.7 us  [swap(): return lax.ppermute(value, axis, [(i, i ^ bit) for i in range(size)])]
    convert_element_type x10 -> x5, other arithmetic: 22.5 us -> 11.7 us  [the longest x3 10.1 us: total(): return sum((term.astype(f32) for term in terms)).astype(bf16)]
    dot_general x1 -> x0, matrix products: 7.54 us -> none  [tn(): lax.dot_general(a, b, (((0,), (0,)), ((), ())), preferred_element_type=f32)]
    pallas_call x13 -> x14, Pallas kernels: 438 us -> 444 us  [call(): pl.pallas_call(kernel, grid_spec=pltpu.PrefetchScalarGridSpec(num_scalar_...]
  transfers between devices with their start and end apart: 77 -> 62, of which waited for: 18 -> 20; matrix products, arithmetic and copies ran while one was open for 10% -> 7% of each run, Pallas kernels for 64% -> 69%
where the time goes in v3:
time: 651 us; the launch traced here: 641 us
  Pallas kernels  444 us (68%)
  waiting for transfers between devices  79.7 us (12%)
  other arithmetic  52 us (8%)
  starting transfers between devices  49.9 us (8%)
  local copies, waits for them, and re-layouts  13.5 us (2%)
    pallas_call x14, Pallas kernels, call(): pl.pallas_call(kernel, grid_spec=pltpu.PrefetchScalarGridSpec(num_scalar_...  444 us
    ppermute x62, waiting for transfers between devices, swap(): return lax.ppermute(value, axis, [(i, i ^ bit) for i in range(size)])  79.7 us
    ppermute x62, starting transfers between devices, swap(): return lax.ppermute(value, axis, [(i, i ^ bit) for i in range(size)])  49.9 us
    convert_element_type x3, other arithmetic, half(): return total.astype(bf16)  13.1 us
  transfers between devices with their start and end apart: 62, of which 20 were waited for; matrix products, arithmetic and copies ran while one was open for 7% of the time, Pallas kernels for 69%

profile of v3, /device:TPU:8, one launch (start us, length us, event | category | flops | bytes accessed | tf_op | source)
XLA Modules:
  0.0 640.8 jit_solution(5144067829390625836)
XLA Ops:
  12.4 20.7 %qkv.2 = (bf16[2560,512]{1,0:T(8,128)(2,1)}, bf16[2560,512]{1,0:T(8,128)(2,1)}, bf16[2560,512]{1,0:T(8,128)(2,1)}, bf16[2560,1024]{1,0:T(8,128)(2,1)}, f32[72,51...) custom-call(s32[20]{0:T(128)} %subtract_maximum_fusion.thr, s32[21]{0:T(128)} %add_convert_fusion.15.cont, ...), custom_call_target="tpu_custom_call" | custom-call | flops 8053063680 | bytes 24117248 | tf_op jit(solution)/shard_map/qkv/pallas_call | solution.py:431
  33.1 5.5 collective-permute-done.4
  45.8 17.8 %qkv.3 = (bf16[2560,512]{1,0:T(8,128)(2,1)}, bf16[2560,512]{1,0:T(8,128)(2,1)}, bf16[2560,512]{1,0:T(8,128)(2,1)}, f32[72,512]{1,0:T(8,128)}, f32[1280,512]{1,0:T(8,128)}, /*index=5*/f32[160,512]{1,0:T(8,128)}) custom-call(s32[20]{0:T(128)} %subtract_maximum_fusion.thr, s32[21]{0:T(128)} %add_convert_fusion.15.cont, ...), custom_call_target="tpu_custom_call" | custom-call | flops 8053063680 | bytes 24117248 | tf_op jit(solution)/shard_map/qkv/pallas_call | solution.py:431
  78.1 34.8 %attend.1 = (bf16[2560,1024]{1,0:T(8,128)(2,1)}, f32[2560,1024]{1,0:T(8,128)}, bf16[1280,1024]{1,0:T(8,128)(2,1)}, f32[160,1024]{1,0:T(8,128)}, f32[2560,1024]{1,0:T(8,128)}, /*index=5*/bf16[2560,1024]{1,0:T(8,128)(2,1)}) custom-call(s32[20]{0:T(128)} %compare_convert_fusion.first.refs_0_, s32[20]{0:T(128)} %subtract_maximum_fusion.thr, ...), custom_call_target="tpu_custom_call" | custom-call | flops 32212254720 | bytes 52428800 | tf_op jit(solution)/shard_map/attend/pallas_call | solution.py:431
  112.8 11.7 %collective-permute-done.14.refs_9_ = bf16[1024,1024]{1,0:T(8,128)(2,1)} collective-permute-done((bf16[1024,1024]{1,0:T(8,128)(2,1)}, bf16[1024,1024]{1,0:T(8,128)(2,1)}, u32[]{:S(2)}, u32[]{:S(2)}) %collective-permute-start.14) | collective-permute-done | bytes 2097184 | tf_op jit(solution)/shard_map/ppermute | solution.py:454
  124.9 51.9 %ffn.5 = (bf16[1024,1024]{1,0:T(8,128)(2,1)}, bf16[1024,1024]{1,0:T(8,128)(2,1)}, f32[8,512]{1,0:T(8,128)}, f32[8,512]{1,0:T(8,128)}, f32[2560,1024]{1,0:T(8,128)}, /*index=5*/f32[2560,1024]{1,0:T(8,128)}) custom-call(bf16[2560,1024]{1,0:T(8,128)(2,1)} %get-tuple-element.282.refs_0_.refs_1_, bf16[2560,1024]{1,0:T(8,128)(2,1)} %refs_2_.1, ...), custom_call_target="tpu_custom_call" | custom-call | flops 32212254720 | bytes 52428800 | tf_op jit(solution)/shard_map/ffn/pallas_call | solution.py:431
  181.3 53.0 %ffn.6 = (bf16[1024,1024]{1,0:T(8,128)(2,1)}, bf16[1024,1024]{1,0:T(8,128)(2,1)}, f32[8,512]{1,0:T(8,128)}, f32[8,512]{1,0:T(8,128)}, f32[2560,1024]{1,0:T(8,128)}, /*index=5*/f32[2560,1024]{1,0:T(8,128)}) custom-call(bf16[2560,1024]{1,0:T(8,128)(2,1)} %get-tuple-element.282.refs_0_.refs_1_, bf16[2560,1024]{1,0:T(8,128)(2,1)} %refs_2_.1, ...), custom_call_target="tpu_custom_call" | custom-call | flops 32212254720 | bytes 52428800 | tf_op jit(solution)/shard_map/ffn/pallas_call | solution.py:431
  244.3 53.2 %ffn.7 = (bf16[1024,1024]{1,0:T(8,128)(2,1)}, bf16[1024,1024]{1,0:T(8,128)(2,1)}, f32[8,512]{1,0:T(8,128)}, f32[8,512]{1,0:T(8,128)}, f32[2560,1024]{1,0:T(8,128)}, /*index=5*/f32[2560,1024]{1,0:T(8,128)}) custom-call(bf16[2560,1024]{1,0:T(8,128)(2,1)} %get-tuple-element.282.refs_0_.refs_1_, bf16[2560,1024]{1,0:T(8,128)(2,1)} %refs_2_.1, ...), custom_call_target="tpu_custom_call" | custom-call | flops 32212254720 | bytes 52428800 | tf_op jit(solution)/shard_map/ffn/pallas_call | solution.py:431
  297.6 4.8 add_convert_fusion.10
  307.7 30.3 %ffn.8 = (bf16[1024,1024]{1,0:T(8,128)(2,1)}, f32[8,512]{1,0:T(8,128)}, f32[2560,1024]{1,0:T(8,128)}, f32[2560,1024]{1,0:T(8,128)}) custom-call(bf16[2560,1024]{1,0:T(8,128)(2,1)} %get-tuple-element.282.refs_0_.refs_1_, bf16[2560,1024]{1,0:T(8,128)(2,1)} %refs_2_.1, f32[1,1024]{1,0:T(1,128)} %bitcast.61, f32[2560,1024]{1,0:T(8,128)} %get-tuple-element.312.refs_3_, ...), custom_call_target="tpu_custom_call" | custom-call | flops 16106127360 | bytes 52428800 | tf_op jit(solution)/shard_map/ffn/pallas_call | solution.py:431
  345.6 53.9 %ffn.9 = (bf16[1024,1024]{1,0:T(8,128)(2,1)}, f32[8,512]{1,0:T(8,128)}, bf16[2560,1024]{1,0:T(8,128)(2,1)}, f32[2560,1024]{1,0:T(8,128)}, bf16[2560,1024]{1,0:T(...) custom-call(s32[20]{0:T(128)} %compare_convert_fusion.first.refs_0_,, ...), custom_call_target="tpu_custom_call" | custom-call | flops 16106127360 | bytes 52428800 | tf_op jit(solution)/shard_map/ffn/pallas_call | solution.py:431
  406.2 4.6 add_convert_fusion.7
  415.0 39.7 %attend_back.2 = (bf16[2560,768]{1,0:T(8,128)(2,1)}, bf16[2560,768]{1,0:T(8,128)(2,1)}, bf16[1024,1024]{1,0:T(8,128)(2,1)}, bf16[1024,1024]{1,0:T(8,128)(2,1)}, f32[8,1536]{1,0:T(8,128)}) custom-call(s32[21]{0:T(128)} %add_convert_fusion.15.cont, bf16[2560,512]{1,0:T(8,128)(2,1)} %get-tuple-element.255.refs_5_.refs_12_.q, ...), custom_call_target="tpu_custom_call" | custom-call | flops 32212254720 | bytes 26214400 | tf_op jit(solution)/shard_map/attend_back/pallas_call | solution.py:431
  466.7 40.0 %attend_back.3 = (bf16[2560,768]{1,0:T(8,128)(2,1)}, bf16[2560,768]{1,0:T(8,128)(2,1)}, bf16[1024,1024]{1,0:T(8,128)(2,1)}, bf16[1024,1024]{1,0:T(8,128)(2,1)}, f32[8,1536]{1,0:T(8,128)}) custom-call(s32[21]{0:T(128)} %add_convert_fusion.15.cont, bf16[2560,512]{1,0:T(8,128)(2,1)} %get-tuple-element.239.refs_0_.refs_11_.q, ...), custom_call_target="tpu_custom_call" | custom-call | flops 32212254720 | bytes 26214400 | tf_op jit(solution)/shard_map/attend_back/pallas_call | solution.py:431
  506.7 6.3 collective-permute-done.36
  513.0 4.4 collective-permute-done.41
  526.8 16.3 %input_grad.2 = (f32[2560,1024]{1,0:T(8,128)}, f32[16,1024]{1,0:T(8,128)}) custom-call(bf16[2560,1024]{1,0:T(8,128)(2,1)} %x.1, f32[2560,1024]{1,0:T(8,128)} %get-tuple-element.392.gm, f32[1,1024]{1,0:T(1,128)} %bitcast.49, bf16[2560,768]{1,0:T(8,128)(2,1)} %get-tuple-element.393.refs_0_, bf16[2560,768]{1,0:T(8,128)(2,1)} %get-tuple-element.394.refs_1_, ...), custom_call_target="tpu_custom_call" | custom-call | flops 8053063680 | bytes 20971520 | tf_op jit(solution)/shard_map/input_grad/pallas_call | solution.py:431
  544.1 5.8 collective-permute-done.45
  559.0 16.2 %input_grad.3 = (f32[2560,1024]{1,0:T(8,128)}, f32[16,1024]{1,0:T(8,128)}) custom-call(bf16[2560,1024]{1,0:T(8,128)(2,1)} %x.1, f32[2560,1024]{1,0:T(8,128)} %get-tuple-element.392.gm, f32[1,1024]{1,0:T(1,128)} %bitcast.50, bf16[2560,768]{1,0:T(8,128)(2,1)} %get-tuple-element.393.refs_0_, ...), custom_call_target="tpu_custom_call", output_to_operand_aliasing={{0}: (11, {})} | custom-call | flops 8053063680 | bytes 20971520 | tf_op jit(solution)/shard_map/input_grad/pallas_call | solution.py:431
  575.9 4.7 collective-permute-done.48
  586.7 8.2 %place.2 = f32[1024,1024]{1,0:T(8,128)} custom-call(s32[2]{0:T(128)} %pad_add_fusion.where, bf16[512,1024]{1,0:T(8,128)(2,1)} %copy-done, bf16[512,1024]{1,0:T(8,128)(2,1)} %copy-done.5, bf16[512,1024]{1,0:T(8,128)(2,1)} %copy-done.1, bf16[512,1024]{1,0:T(8,128)(2,1)} %copy-done.6), custom_call_target="tpu_custom_call" | custom-call | bytes 6291456 | tf_op jit(solution)/shard_map/place/pallas_call | solution.py:431
  594.9 5.2 collective-permute-done.51
  600.1 4.6 collective-permute-done.52
  619.9 7.8 %place.3 = f32[1024,1024]{1,0:T(8,128)} custom-call(s32[2]{0:T(128)} %pad_add_fusion.where, bf16[512,1024]{1,0:T(8,128)(2,1)} %copy-done, bf16[512,1024]{1,0:T(8,128)(2,1)} %copy-done.5, bf16[512,1024]{1,0:T(8,128)(2,1)} %copy-done.1, bf16[512,1024]{1,0:T(8,128)(2,1)} %copy-done.6), custom_call_target="tpu_custom_call" | custom-call | bytes 6291456 | tf_op jit(solution)/shard_map/place/pallas_call | solution.py:431
  (263 shorter events, 137.6 us)
Async XLA Ops:
  1.2 37.5 %collective-permute-start.6 = (bf16[1024,1024]{1,0:T(8,128)(2,1)}, bf16[1024,1024]{1,0:T(8,128)(2,1)}, u32[]{:S(2)}, u32[]{:S(2)}) collective-permute-start(bf16[1024,1024]{1,0:T(8,128)(2,1)} %refs_6_.1), channel_id=1, source_target_pairs={{0,1},{1,0},{2,3},{3,2},{4,5},{5,4},{6,7},{7,6},{8,9},{9,8},{10,11... | collective-permute-start | bytes 6291464 | tf_op jit(solution)/shard_map/ppermute | solution.py:454
  1.3 37.4 %collective-permute-start.7 = (bf16[1024,1024]{1,0:T(8,128)(2,1)}, bf16[1024,1024]{1,0:T(8,128)(2,1)}, u32[]{:S(2)}, u32[]{:S(2)}) collective-permute-start(bf16[1024,1024]{1,0:T(8,128)(2,1)} %refs_7_.3), channel_id=1, source_target_pairs={{0,1},{1,0},{2,3},{3,2},{4,5},{5,4},{6,7},{7,6},{8,9},{9,8},{10,11... | collective-permute-start | bytes 6291464 | tf_op jit(solution)/shard_map/ppermute | solution.py:454
  1.7 36.9 %collective-permute-start.3 = (bf16[1024,768]{1,0:T(8,128)(2,1)}, bf16[1024,768]{1,0:T(8,128)(2,1)S(1)}, u32[]{:S(2)}, u32[]{:S(2)}) collective-permute-start(bf16[1024,768]{1,0:T(8,128)(2,1)} %refs_4_.3), channel_id=1, source_target_pairs={{0,2},{1,3},{2,0},{3,1},{4,6},{5,7},{6,4},{7,5},{8,10},{9,11},{10,... | collective-permute-start | bytes 4718600 | tf_op jit(solution)/shard_map/ppermute | solution.py:454
  76.7 47.8 %collective-permute-start.14 = (bf16[1024,1024]{1,0:T(8,128)(2,1)}, bf16[1024,1024]{1,0:T(8,128)(2,1)}, u32[]{:S(2)}, u32[]{:S(2)}) collective-permute-start(bf16[1024,1024]{1,0:T(8,128)(2,1)} %refs_7_.3), channel_id=1, source_target_pairs={{0,2},{1,3},{2,0},{3,1},{4,6},{5,7},{6,4},{7,5},{8,10},{9,11},{10,... | collective-permute-start | bytes 6291464 | tf_op jit(solution)/shard_map/ppermute | solution.py:454
  124.5 52.3 %collective-permute-start.16 = (bf16[1024,1024]{1,0:T(8,128)(2,1)}, bf16[1024,1024]{1,0:T(8,128)(2,1)}, u32[]{:S(2)}, u32[]{:S(2)}) collective-permute-start(bf16[1024,1024]{1,0:T(8,128)(2,1)} %collective-permute-done.14.refs_9_), channel_id=1, source_target_pairs={{0,1},{1,0},{2,3},{3,2},{4,5},{5,4},{6,7},{7,6},{8,9},{9,8},{10,11... | collective-permute-start | bytes 6291464 | tf_op jit(solution)/shard_map/ppermute | solution.py:454
  124.5 52.3 %collective-permute-start.15 = (bf16[1024,1024]{1,0:T(8,128)(2,1)S(1)}, bf16[1024,1024]{1,0:T(8,128)(2,1)}, u32[]{:S(2)}, u32[]{:S(2)}) collective-permute-start(bf16[1024,1024]{1,0:T(8,128)(2,1)S(1)} %copy-done.7), channel_id=1, source_target_pairs={{0,2},{1,3},{2,0},{3,1},{4,6},{5,7},{6,4},{7,5},{8,10},{9,11},{10,... | collective-permute-start | bytes 6291464 | tf_op jit(solution)/shard_map/ppermute | solution.py:454
  177.7 56.7 %collective-permute-start.18 = (bf16[1024,1024]{1,0:T(8,128)(2,1)}, bf16[1024,1024]{1,0:T(8,128)(2,1)S(1)}, u32[]{:S(2)}, u32[]{:S(2)}) collective-permute-start(bf16[1024,1024]{1,0:T(8,128)(2,1)} %get-tuple-element.285), channel_id=1, source_target_pairs={{0,1},{1,0},{2,3},{3,2},{4,5},{5,4},{6,7},{7,6},{8,9},{9,8},{10,11... | collective-permute-start | bytes 6291464 | tf_op jit(solution)/shard_map/ppermute | solution.py:454
  242.7 54.8 %collective-permute-start.20 = (bf16[1024,1024]{1,0:T(8,128)(2,1)}, bf16[1024,1024]{1,0:T(8,128)(2,1)}, u32[]{:S(2)}, u32[]{:S(2)}) collective-permute-start(bf16[1024,1024]{1,0:T(8,128)(2,1)} %add_convert_fusion.2), channel_id=1, source_target_pairs={{0,2},{1,3},{2,0},{3,1},{4,6},{5,7},{6,4},{7,5},{8,10},{9,11},{10,... | collective-permute-start | bytes 6291464 | tf_op jit(solution)/shard_map/ppermute | solution.py:454
  302.4 35.6 %collective-permute-start.22 = (bf16[512,1024]{1,0:T(8,128)(2,1)}, bf16[512,1024]{1,0:T(8,128)(2,1)S(1)}, u32[]{:S(2)}, u32[]{:S(2)}) collective-permute-start(bf16[512,1024]{1,0:T(8,128)(2,1)} %get-tuple-element.310), channel_id=1, source_target_pairs={{0,4},{4,0},{8,12},{12,8},{16,20},{20,16},{24,28},{28,24},{1,5},{5... | collective-permute-start | bytes 3145736 | tf_op jit(solution)/shard_map/ppermute | solution.py:454
  339.0 60.5 %collective-permute-start.24 = (bf16[1024,1024]{1,0:T(8,128)(2,1)}, bf16[1024,1024]{1,0:T(8,128)(2,1)S(1)}, u32[]{:S(2)}, u32[]{:S(2)}) collective-permute-start(bf16[1024,1024]{1,0:T(8,128)(2,1)} %get-tuple-element.321), channel_id=1, source_target_pairs={{0,1},{1,0},{2,3},{3,2},{4,5},{5,4},{6,7},{7,6},{8,9},{9,8},{10,11... | collective-permute-start | bytes 6291464 | tf_op jit(solution)/shard_map/ppermute | solution.py:454
  339.2 60.4 %collective-permute-start.23 = (bf16[1024,1024]{1,0:T(8,128)(2,1)}, bf16[1024,1024]{1,0:T(8,128)(2,1)}, u32[]{:S(2)}, u32[]{:S(2)}) collective-permute-start(bf16[1024,1024]{1,0:T(8,128)(2,1)} %add_convert_fusion.1), channel_id=1, source_target_pairs={{0,2},{1,3},{2,0},{3,1},{4,6},{5,7},{6,4},{7,5},{8,10},{9,11},{10,... | collective-permute-start | bytes 6291464 | tf_op jit(solution)/shard_map/ppermute | solution.py:454
  342.1 57.4 %collective-permute-start.25 = (bf16[128,1024]{1,0:T(8,128)(2,1)S(1)}, bf16[128,1024]{1,0:T(8,128)(2,1)S(1)}, u32[]{:S(2)}, u32[]{:S(2)}) collective-permute-start(bf16[128,1024]{1,0:T(8,128)(2,1)S(1)} %get-tuple-element.324), channel_id=1, source_target_pairs={{0,8},{4,12},{8,0},{12,4},{16,24},{20,28},{24,16},{28,20},{1,9},{5... | collective-permute-start | bytes 786440 | tf_op jit(solution)/shard_map/ppermute | solution.py:454
  342.6 56.9 %collective-permute-start.26 = (bf16[128,1024]{1,0:T(8,128)(2,1)S(1)}, bf16[128,1024]{1,0:T(8,128)(2,1)S(1)}, u32[]{:S(2)}, u32[]{:S(2)}) collective-permute-start(bf16[128,1024]{1,0:T(8,128)(2,1)S(1)} %get-tuple-element.325), channel_id=1, source_target_pairs={{0,16},{4,20},{8,24},{12,28},{16,0},{20,4},{24,8},{28,12},{1,17},{... | collective-permute-start | bytes 786440 | tf_op jit(solution)/shard_map/ppermute | solution.py:454
  345.1 54.4 %collective-permute-start.27 = (bf16[128,1024]{1,0:T(8,128)(2,1)S(1)}, bf16[128,1024]{1,0:T(8,128)(2,1)S(1)}, u32[]{:S(2)}, u32[]{:S(2)}) collective-permute-start(bf16[128,1024]{1,0:T(8,128)(2,1)S(1)} %get-tuple-element.326), channel_id=1, source_target_pairs={{0,24},{4,28},{8,16},{12,20},{16,8},{20,12},{24,0},{28,4},{1,25},{... | collective-permute-start | bytes 786440 | tf_op jit(solution)/shard_map/ppermute | solution.py:454
  402.6 52.1 %collective-permute-start.32 = (bf16[128,1024]{1,0:T(8,128)(2,1)S(1)}, bf16[128,1024]{1,0:T(8,128)(2,1)}, u32[]{:S(2)}, u32[]{:S(2)}) collective-permute-start(bf16[128,1024]{1,0:T(8,128)(2,1)S(1)} %add_convert_fusion.14), channel_id=1, source_target_pairs={{0,8},{4,12},{8,0},{12,4},{16,24},{20,28},{24,16},{28,20},{1,9},{5... | collective-permute-start | bytes 786440 | tf_op jit(solution)/shard_map/ppermute | solution.py:454
  404.0 50.7 %collective-permute-start.33 = (bf16[128,1024]{1,0:T(8,128)(2,1)S(1)}, bf16[128,1024]{1,0:T(8,128)(2,1)}, u32[]{:S(2)}, u32[]{:S(2)}) collective-permute-start(bf16[128,1024]{1,0:T(8,128)(2,1)S(1)} %add_convert_fusion.14), channel_id=1, source_target_pairs={{0,16},{4,20},{8,24},{12,28},{16,0},{20,4},{24,8},{28,12},{1,17},{... | collective-permute-start | bytes 786440 | tf_op jit(solution)/shard_map/ppermute | solution.py:454
  410.9 43.8 %collective-permute-start.34 = (bf16[128,1024]{1,0:T(8,128)(2,1)S(1)}, bf16[128,1024]{1,0:T(8,128)(2,1)S(1)}, u32[]{:S(2)}, u32[]{:S(2)}) collective-permute-start(bf16[128,1024]{1,0:T(8,128)(2,1)S(1)} %add_convert_fusion.14), channel_id=1, source_target_pairs={{0,24},{4,28},{8,16},{12,20},{16,8},{20,12},{24,0},{28,4},{1,25},{... | collective-permute-start | bytes 786440 | tf_op jit(solution)/shard_map/ppermute | solution.py:454
  411.4 43.3 %collective-permute-start.31 = (bf16[512,1024]{1,0:T(8,128)(2,1)}, bf16[512,1024]{1,0:T(8,128)(2,1)S(1)}, u32[]{:S(2)}, u32[]{:S(2)}) collective-permute-start(bf16[512,1024]{1,0:T(8,128)(2,1)} %get-tuple-element.353), channel_id=1, source_target_pairs={{0,4},{4,0},{8,12},{12,8},{16,20},{20,16},{24,28},{28,24},{1,5},{5... | collective-permute-start | bytes 3145736 | tf_op jit(solution)/shard_map/ppermute | solution.py:454
  456.9 49.8 %collective-permute-start.40 = (bf16[512,1024]{1,0:T(8,128)(2,1)S(1)}, bf16[512,1024]{1,0:T(8,128)(2,1)S(1)}, u32[]{:S(2)}, u32[]{:S(2)}) collective-permute-start(bf16[512,1024]{1,0:T(8,128)(2,1)S(1)} %pad_maximum_fusion.refs_0_), channel_id=1, source_target_pairs={{0,4},{4,0},{8,12},{12,8},{16,20},{20,16},{24,28},{28,24},{1,5},{5... | collective-permute-start | bytes 3145736 | tf_op jit(solution)/shard_map/ppermute | solution.py:454
  458.2 48.4 %collective-permute-start.37 = (bf16[128,1024]{1,0:T(8,128)(2,1)S(1)}, bf16[128,1024]{1,0:T(8,128)(2,1)S(1)}, u32[]{:S(2)}, u32[]{:S(2)}) collective-permute-start(bf16[128,1024]{1,0:T(8,128)(2,1)S(1)} %get-tuple-element.371), channel_id=1, source_target_pairs={{0,8},{4,12},{8,0},{12,4},{16,24},{20,28},{24,16},{28,20},{1,9},{5... | collective-permute-start | bytes 786440 | tf_op jit(solution)/shard_map/ppermute | solution.py:454
  461.7 45.0 %collective-permute-start.38 = (bf16[128,1024]{1,0:T(8,128)(2,1)S(1)}, bf16[128,1024]{1,0:T(8,128)(2,1)S(1)}, u32[]{:S(2)}, u32[]{:S(2)}) collective-permute-start(bf16[128,1024]{1,0:T(8,128)(2,1)S(1)} %get-tuple-element.372), channel_id=1, source_target_pairs={{0,16},{4,20},{8,24},{12,28},{16,0},{20,4},{24,8},{28,12},{1,17},{... | collective-permute-start | bytes 786440 | tf_op jit(solution)/shard_map/ppermute | solution.py:454
  462.1 44.6 %collective-permute-start.39 = (bf16[128,1024]{1,0:T(8,128)(2,1)S(1)}, bf16[128,1024]{1,0:T(8,128)(2,1)S(1)}, u32[]{:S(2)}, u32[]{:S(2)}) collective-permute-start(bf16[128,1024]{1,0:T(8,128)(2,1)S(1)} %get-tuple-element.373), channel_id=1, source_target_pairs={{0,24},{4,28},{8,16},{12,20},{16,8},{20,12},{24,0},{28,4},{1,25},{... | collective-permute-start | bytes 786440 | tf_op jit(solution)/shard_map/ppermute | solution.py:454
  465.5 47.5 %collective-permute-start.36 = (bf16[1024,1024]{1,0:T(8,128)(2,1)}, bf16[1024,1024]{1,0:T(8,128)(2,1)}, u32[]{:S(2)}, u32[]{:S(2)}) collective-permute-start(bf16[1024,1024]{1,0:T(8,128)(2,1)} %add_convert_fusion), channel_id=1, source_target_pairs={{0,2},{1,3},{2,0},{3,1},{4,6},{5,7},{6,4},{7,5},{8,10},{9,11},{10,... | collective-permute-start | bytes 6291464 | tf_op jit(solution)/shard_map/ppermute | solution.py:454
  521.1 28.8 %collective-permute-start.42 = (bf16[512,1024]{1,0:T(8,128)(2,1)S(1)}, bf16[512,1024]{1,0:T(8,128)(2,1)S(1)}, u32[]{:S(2)}, u32[]{:S(2)}) collective-permute-start(bf16[512,1024]{1,0:T(8,128)(2,1)S(1)} %get-tuple-element.386), channel_id=1, source_target_pairs={{0,4},{4,0},{8,12},{12,8},{16,20},{20,16},{24,28},{28,24},{1,5},{5... | collective-permute-start | bytes 3145736 | tf_op jit(solution)/shard_map/ppermute | solution.py:454
  (69 other events, 968.2 us)

commit v4 on v3

--- a/solution.py
+++ b/solution.py
@@ -714,6 +714,7 @@
     blocks = 2 if nb % 2 == 0 else 1
     rows = blocks * STRETCH
     tiles = R // rows
+    many = 4 if nb % 4 == 0 else blocks
     gain1, shift1 = first_gain[None, :], first_shift[None, :]
     gain2, shift2 = second_gain[None, :], second_shift[None, :]
     like = jax.ShapeDtypeStruct
@@ -728,22 +729,23 @@
         return (value, vec)
 
     def project(source, pick, bias, fresh):
-        ins = [(source, full)]
+        tall, thin = rows_spec(many * STRETCH, D), rows_spec(many * STRETCH, HALF)
+        ins = [(source, tall)]
         if fresh:
             ins += [vector(gain1), vector(shift1)]
         ins += [(wa[k], whole_spec((D, PW))) for k in pick]
         ins += [(bias, whole_spec((1, 2 * PW)))]
-        outs = [narrow] * 3 + ([low] if fresh else [])
+        outs = [(narrow[0], thin)] * 3 + ([(low[0], tall)] if fresh else [])
         outs += [
             (like((state_rows, HALF), f32), sum_spec((state_rows, HALF))),
-            (like((nb * DH, HALF), f32), rows_spec(blocks * DH, HALF)),
-            (like((nb * 8, HALF), f32), rows_spec(blocks * 8, HALF)),
+            (like((nb * DH, HALF), f32), rows_spec(many * DH, HALF)),
+            (like((nb * 8, HALF), f32), rows_spec(many * 8, HALF)),
         ]
         return call(
-            functools.partial(qkv_kernel, blocks, fresh),
+            functools.partial(qkv_kernel, many, fresh),
             "qkv",
             (thr, cont),
-            tiles,
+            nb // many,
             ins,
             outs,
             [pltpu.VMEM((DH, HALF), f32), pltpu.VMEM((8, HALF), f32)],
@@ -779,24 +781,26 @@
     s_in = swap_state(jnp.concatenate([trail01, trail23], axis=1), before)
     if fast:
         w = Window(s_in)
-        wr_far = w.swap(reduce_weight, "head", 2)
+        we_cut, wr_cut = jnp.split(expand_weight, 2, axis=1), jnp.split(reduce_weight, 2)
+        wr_far = w.swap(wr_cut[0], "head", 2)
         (s_in,) = w.open(s_in)
 
+    tall, thin = rows_spec(many * STRETCH, D), rows_spec(many * STRETCH, HALF)
     att, rec, st, kt, middle, n2 = call(
-        functools.partial(attend_kernel, blocks),
+        functools.partial(attend_kernel, many),
         "attend",
         (first, thr),
-        tiles,
+        nb // many,
         [
             (a, spec)
             for part in ((q01, k01, v01, st01, kt01), (q23, k23, v23, st23, kt23))
             for a, spec in zip(
                 part,
-                [side] * 3 + [rows_spec(blocks * DH, HALF), rows_spec(blocks * 8, HALF)],
+                [thin] * 3 + [rows_spec(many * DH, HALF), rows_spec(many * 8, HALF)],
             )
         ]
         + [
-            (layer_input, full),
+            (layer_input, tall),
             (s_in, whole_spec((state_rows, D))),
             vector(output_bias[None, :]),
             vector(gain2),
@@ -804,12 +808,12 @@
         ]
         + [(w, whole_spec((QW, D))) for w in wo],
         [
-            low,
-            wide,
-            (like((nb * DH, D), bf16), rows_spec(blocks * DH, D)),
-            (like((nb * 8, D), f32), rows_spec(blocks * 8, D)),
-            wide,
-            low,
+            (low[0], tall),
+            (wide[0], tall),
+            (like((nb * DH, D), bf16), rows_spec(many * DH, D)),
+            (like((nb * 8, D), f32), rows_spec(many * 8, D)),
+            (wide[0], tall),
+            (low[0], tall),
         ],
         [],
         12 * R * D * D,
@@ -818,8 +822,8 @@
 
     if fast:
         att, rec, st, kt, middle, n2 = w.close(att, rec, st, kt, middle, n2)
-        we = [expand_weight, we_near.get(), None, None]
-        wr = [reduce_weight, wr_near.get(), wr_far.get(), None]
+        we = [expand_weight, we_near.get(), [None, None], [None, None]]
+        wr = [reduce_weight, wr_near.get(), [wr_far.get(), None], [None, None]]
 
     def ffn(picks, part, extra):
         widths = [FQ if half is None else FQ // 2 for _, half in picks]
@@ -828,8 +832,12 @@
         ins += [(be_slots[k][None, :], whole_spec((1, width), at)) for k, width, at in spots]
         if part is not None:
             ins += [(part[0], full), (part[1], full)]
-        ins += [(we[k], whole_spec((D, width), at)) for k, width, at in spots]
-        ins += [(wr[k], part_spec((width, D), at)) for k, width, at in spots]
+        for group, spec, dims in ((we, whole_spec, (D, None)), (wr, part_spec, (None, D))):
+            for k, width, at in spots:
+                shape = tuple(d or width for d in dims)
+                halves = isinstance(group[k], list)
+                weight = group[k][at] if halves else group[k]
+                ins.append((weight, spec(shape, 0 if halves else at)))
         outs = [(like((2 * w, D), bf16), whole_spec((2 * w, D))) for w in widths]
         outs += [(like((8, w), f32), sum_spec((8, w))) for w in widths]
         if extra is None:
@@ -873,18 +881,23 @@
 
     if fast:
         w = Window(n2)
-        we_far = w.swap(expand_weight, "head", 2)
-        wr_last = w.swap(wr[2], "head", 1)
+        we_far = w.swap(we_cut[0], "head", 2)
+        wr_far = w.swap(wr_cut[1], "head", 2)
+        wr_last = w.swap(wr[2][0], "head", 1)
         (n2,) = w.open(n2)
         (near, own), part = ffn([(1, 0), (0, 0)], None, None)
         n2, near, own, *part = w.close(n2, near, own, *part)
-        we[2], wr[3] = we_far.get(), wr_last.get()
-        we[3] = swap(we[2], "head", 1)
+        we[2][0], wr[2][1], wr[3][0] = we_far.get(), wr_far.get(), wr_last.get()
+        we[3][0] = swap(we[2][0], "head", 1)
         w = Window(part[0])
+        we_far = w.swap(we_cut[1], "head", 2)
+        wr_last = w.swap(wr[2][1], "head", 1)
         near = w.swap(near, "head", 1)
         (part[0],) = w.open(part[0])
         (last_far, far), part = ffn([(3, 0), (2, 0)], part, None)
         last_far, far, *part = w.close(last_far, far, *part)
+        we[2][1], wr[3][1] = we_far.get(), wr_last.get()
+        we[3][1] = swap(we[2][1], "head", 1)
         far = total(far, swap(last_far, "head", 1))
         near_a = near.get()
         w = Window(part[0])

time: 651 us -> 639 us (0.982)
  waiting for transfers between devices: 79.7 us -> 66 us
    ppermute x62 -> x66, waiting for transfers between devices: 79.7 us -> 66 us  [swap(): return lax.ppermute(value, axis, [(i, i ^ bit) for i in range(size)])]
    ppermute x62 -> x66, starting transfers between devices: 49.9 us -> 53.7 us  [swap(): return lax.ppermute(value, axis, [(i, i ^ bit) for i in range(size)])]
  transfers between devices with their start and end apart: 62 -> 66, of which waited for: 20 -> 19; matrix products, arithmetic and copies ran while one was open for 7% -> 8% of each run, Pallas kernels for 69% -> 70%
where the time goes in v4:
time: 639 us; the launch traced here: 630 us
  Pallas kernels  440 us (69%)
  waiting for transfers between devices  66 us (10%)
  starting transfers between devices  53.7 us (8%)
  other arithmetic  51.2 us (8%)
  local copies, waits for them, and re-layouts  16.4 us (3%)
    pallas_call x14, Pallas kernels, call(): pl.pallas_call(kernel, grid_spec=pltpu.PrefetchScalarGridSpec(num_scalar_...  440 us
    ppermute x66, waiting for transfers between devices, swap(): return lax.ppermute(value, axis, [(i, i ^ bit) for i in range(size)])  66 us
    ppermute x66, starting transfers between devices, swap(): return lax.ppermute(value, axis, [(i, i ^ bit) for i in range(size)])  53.7 us
    convert_element_type x3, other arithmetic, half(): return total.astype(bf16)  13.1 us
  transfers between devices with their start and end apart: 66, of which 19 were waited for; matrix products, arithmetic and copies ran while one was open for 8% of the time, Pallas kernels for 70%

profile of v4, /device:TPU:8, one launch (start us, length us, event | category | flops | bytes accessed | tf_op | source)
XLA Modules:
  0.0 629.9 jit_solution(14014186586134688546)
XLA Ops:
  12.4 19.1 %qkv.2 = (bf16[2560,512]{1,0:T(8,128)(2,1)}, bf16[2560,512]{1,0:T(8,128)(2,1)}, bf16[2560,512]{1,0:T(8,128)(2,1)}, bf16[2560,1024]{1,0:T(8,128)(2,1)}, f32[72,51...) custom-call(s32[20]{0:T(128)} %subtract_maximum_fusion.thr, s32[21]{0:T(128)} %add_convert_fusion.15.cont, ...), custom_call_target="tpu_custom_call" | custom-call | flops 8053063680 | bytes 24117248 | tf_op jit(solution)/shard_map/qkv/pallas_call | solution.py:431
  31.5 7.1 %collective-permute-done.4 = f32[3584]{0:T(1024)S(1)} collective-permute-done((f32[3584]{0:T(1024)S(1)}, f32[3584]{0:T(1024)S(1)}, u32[]{:S(2)}, u32[]{:S(2)}) %collective-permute-start.4) | collective-permute-done | bytes 14368 | tf_op jit(solution)/shard_map/ppermute | solution.py:454
  46.8 16.2 %qkv.3 = (bf16[2560,512]{1,0:T(8,128)(2,1)}, bf16[2560,512]{1,0:T(8,128)(2,1)}, bf16[2560,512]{1,0:T(8,128)(2,1)}, f32[72,512]{1,0:T(8,128)}, f32[1280,512]{1,0:T(8,128)}, /*index=5*/f32[160,512]{1,0:T(8,128)}) custom-call(s32[20]{0:T(128)} %subtract_maximum_fusion.thr, s32[21]{0:T(128)} %add_convert_fusion.15.cont, ...), custom_call_target="tpu_custom_call" | custom-call | flops 8053063680 | bytes 24117248 | tf_op jit(solution)/shard_map/qkv/pallas_call | solution.py:431
  77.7 34.8 %attend.1 = (bf16[2560,1024]{1,0:T(8,128)(2,1)}, f32[2560,1024]{1,0:T(8,128)}, bf16[1280,1024]{1,0:T(8,128)(2,1)}, f32[160,1024]{1,0:T(8,128)}, f32[2560,1024]{1,0:T(8,128)}, /*index=5*/bf16[2560,1024]{1,0:T(8,128)(2,1)}) custom-call(s32[20]{0:T(128)} %compare_convert_fusion.first.refs_0_, s32[20]{0:T(128)} %subtract_maximum_fusion.thr, ...), custom_call_target="tpu_custom_call" | custom-call | flops 32212254720 | bytes 52428800 | tf_op jit(solution)/shard_map/attend/pallas_call | solution.py:431
  114.7 52.0 %ffn.5 = (bf16[1024,1024]{1,0:T(8,128)(2,1)}, bf16[1024,1024]{1,0:T(8,128)(2,1)}, f32[8,512]{1,0:T(8,128)}, f32[8,512]{1,0:T(8,128)}, f32[2560,1024]{1,0:T(8,128)}, /*index=5*/f32[2560,1024]{1,0:T(8,128)}) custom-call(bf16[2560,1024]{1,0:T(8,128)(2,1)} %get-tuple-element.289.refs_0_.refs_1_, bf16[2560,1024]{1,0:T(8,128)(2,1)} %refs_2_.1, ...), custom_call_target="tpu_custom_call" | custom-call | flops 32212254720 | bytes 52428800 | tf_op jit(solution)/shard_map/ffn/pallas_call | solution.py:431
  169.8 52.8 %ffn.6 = (bf16[1024,1024]{1,0:T(8,128)(2,1)}, bf16[1024,1024]{1,0:T(8,128)(2,1)}, f32[8,512]{1,0:T(8,128)}, f32[8,512]{1,0:T(8,128)}, f32[2560,1024]{1,0:T(8,128)}, /*index=5*/f32[2560,1024]{1,0:T(8,128)}) custom-call(bf16[2560,1024]{1,0:T(8,128)(2,1)} %get-tuple-element.289.refs_0_.refs_1_, bf16[2560,1024]{1,0:T(8,128)(2,1)} %refs_2_.1, ...), custom_call_target="tpu_custom_call" | custom-call | flops 32212254720 | bytes 52428800 | tf_op jit(solution)/shard_map/ffn/pallas_call | solution.py:431
  233.3 53.2 %ffn.7 = (bf16[1024,1024]{1,0:T(8,128)(2,1)}, bf16[1024,1024]{1,0:T(8,128)(2,1)}, f32[8,512]{1,0:T(8,128)}, f32[8,512]{1,0:T(8,128)}, f32[2560,1024]{1,0:T(8,128)}, /*index=5*/f32[2560,1024]{1,0:T(8,128)}) custom-call(bf16[2560,1024]{1,0:T(8,128)(2,1)} %get-tuple-element.289.refs_0_.refs_1_, bf16[2560,1024]{1,0:T(8,128)(2,1)} %refs_2_.1, ...), custom_call_target="tpu_custom_call" | custom-call | flops 32212254720 | bytes 52428800 | tf_op jit(solution)/shard_map/ffn/pallas_call | solution.py:431
  286.7 4.8 add_convert_fusion.10
  297.0 30.3 %ffn.8 = (bf16[1024,1024]{1,0:T(8,128)(2,1)}, f32[8,512]{1,0:T(8,128)}, f32[2560,1024]{1,0:T(8,128)}, f32[2560,1024]{1,0:T(8,128)}) custom-call(bf16[2560,1024]{1,0:T(8,128)(2,1)} %get-tuple-element.289.refs_0_.refs_1_, bf16[2560,1024]{1,0:T(8,128)(2,1)} %refs_2_.1, f32[1,1024]{1,0:T(1,128)} %bitcast.61, f32[2560,1024]{1,0:T(8,128)} %get-tuple-element.324.refs_3_, ...), custom_call_target="tpu_custom_call" | custom-call | flops 16106127360 | bytes 52428800 | tf_op jit(solution)/shard_map/ffn/pallas_call | solution.py:431
  334.8 53.8 %ffn.9 = (bf16[1024,1024]{1,0:T(8,128)(2,1)}, f32[8,512]{1,0:T(8,128)}, bf16[2560,1024]{1,0:T(8,128)(2,1)}, f32[2560,1024]{1,0:T(8,128)}, bf16[2560,1024]{1,0:T(...) custom-call(s32[20]{0:T(128)} %compare_convert_fusion.first.refs_0_,, ...), custom_call_target="tpu_custom_call" | custom-call | flops 16106127360 | bytes 52428800 | tf_op jit(solution)/shard_map/ffn/pallas_call | solution.py:431
  395.4 4.6 add_convert_fusion.7
  404.2 39.9 %attend_back.2 = (bf16[2560,768]{1,0:T(8,128)(2,1)}, bf16[2560,768]{1,0:T(8,128)(2,1)}, bf16[1024,1024]{1,0:T(8,128)(2,1)}, bf16[1024,1024]{1,0:T(8,128)(2,1)}, f32[8,1536]{1,0:T(8,128)}) custom-call(s32[21]{0:T(128)} %add_convert_fusion.15.cont, bf16[2560,512]{1,0:T(8,128)(2,1)} %get-tuple-element.261.refs_5_.refs_12_.q, ...), custom_call_target="tpu_custom_call" | custom-call | flops 32212254720 | bytes 26214400 | tf_op jit(solution)/shard_map/attend_back/pallas_call | solution.py:431
  456.0 39.8 %attend_back.3 = (bf16[2560,768]{1,0:T(8,128)(2,1)}, bf16[2560,768]{1,0:T(8,128)(2,1)}, bf16[1024,1024]{1,0:T(8,128)(2,1)}, bf16[1024,1024]{1,0:T(8,128)(2,1)}, f32[8,1536]{1,0:T(8,128)}) custom-call(s32[21]{0:T(128)} %add_convert_fusion.15.cont, bf16[2560,512]{1,0:T(8,128)(2,1)} %get-tuple-element.245.refs_0_.refs_11_.q, ...), custom_call_target="tpu_custom_call" | custom-call | flops 32212254720 | bytes 26214400 | tf_op jit(solution)/shard_map/attend_back/pallas_call | solution.py:431
  495.8 6.4 %collective-permute-done.40 = bf16[1024,1024]{1,0:T(8,128)(2,1)} collective-permute-done((bf16[1024,1024]{1,0:T(8,128)(2,1)}, bf16[1024,1024]{1,0:T(8,128)(2,1)}, u32[]{:S(2)}, u32[]{:S(2)}) %collective-permute-start.40) | collective-permute-done | bytes 2097184 | tf_op jit(solution)/shard_map/ppermute | solution.py:454
  502.3 4.4 collective-permute-done.45
  516.2 16.2 %input_grad.2 = (f32[2560,1024]{1,0:T(8,128)}, f32[16,1024]{1,0:T(8,128)}) custom-call(bf16[2560,1024]{1,0:T(8,128)(2,1)} %x.1, f32[2560,1024]{1,0:T(8,128)} %get-tuple-element.404.gm, f32[1,1024]{1,0:T(1,128)} %bitcast.49, bf16[2560,768]{1,0:T(8,128)(2,1)} %get-tuple-element.405.refs_0_, bf16[2560,768]{1,0:T(8,128)(2,1)} %get-tuple-element.406.refs_1_, ...), custom_call_target="tpu_custom_call" | custom-call | flops 8053063680 | bytes 20971520 | tf_op jit(solution)/shard_map/input_grad/pallas_call | solution.py:431
  533.4 5.8 collective-permute-done.49
  548.2 16.5 %input_grad.3 = (f32[2560,1024]{1,0:T(8,128)}, f32[16,1024]{1,0:T(8,128)}) custom-call(bf16[2560,1024]{1,0:T(8,128)(2,1)} %x.1, f32[2560,1024]{1,0:T(8,128)} %get-tuple-element.404.gm, f32[1,1024]{1,0:T(1,128)} %bitcast.50, bf16[2560,768]{1,0:T(8,128)(2,1)} %get-tuple-element.405.refs_0_, ...), custom_call_target="tpu_custom_call", output_to_operand_aliasing={{0}: (11, {})} | custom-call | flops 8053063680 | bytes 20971520 | tf_op jit(solution)/shard_map/input_grad/pallas_call | solution.py:431
  565.2 4.6 collective-permute-done.52
  575.9 7.9 %place.2 = f32[1024,1024]{1,0:T(8,128)} custom-call(s32[2]{0:T(128)} %pad_add_fusion.where, bf16[512,1024]{1,0:T(8,128)(2,1)} %copy-done, bf16[512,1024]{1,0:T(8,128)(2,1)} %copy-done.5, bf16[512,1024]{1,0:T(8,128)(2,1)} %copy-done.1, bf16[512,1024]{1,0:T(8,128)(2,1)} %copy-done.6), custom_call_target="tpu_custom_call" | custom-call | bytes 6291456 | tf_op jit(solution)/shard_map/place/pallas_call | solution.py:431
  583.9 5.5 collective-permute-done.55
  589.4 4.5 collective-permute-done.56
  604.5 3.9 collective-permute-done.60
  609.0 7.8 %place.3 = f32[1024,1024]{1,0:T(8,128)} custom-call(s32[2]{0:T(128)} %pad_add_fusion.where, bf16[512,1024]{1,0:T(8,128)(2,1)} %copy-done, bf16[512,1024]{1,0:T(8,128)(2,1)} %copy-done.5, bf16[512,1024]{1,0:T(8,128)(2,1)} %copy-done.1, bf16[512,1024]{1,0:T(8,128)(2,1)} %copy-done.6), custom_call_target="tpu_custom_call" | custom-call | bytes 6291456 | tf_op jit(solution)/shard_map/place/pallas_call | solution.py:431
  (281 shorter events, 135.6 us)
Async XLA Ops:
  1.2 37.5 %collective-permute-start.6 = (bf16[1024,1024]{1,0:T(8,128)(2,1)}, bf16[1024,1024]{1,0:T(8,128)(2,1)}, u32[]{:S(2)}, u32[]{:S(2)}) collective-permute-start(bf16[1024,1024]{1,0:T(8,128)(2,1)} %refs_6_.1), channel_id=1, source_target_pairs={{0,1},{1,0},{2,3},{3,2},{4,5},{5,4},{6,7},{7,6},{8,9},{9,8},{10,11... | collective-permute-start | bytes 6291464 | tf_op jit(solution)/shard_map/ppermute | solution.py:454
  1.3 37.4 %collective-permute-start.7 = (bf16[1024,1024]{1,0:T(8,128)(2,1)}, bf16[1024,1024]{1,0:T(8,128)(2,1)}, u32[]{:S(2)}, u32[]{:S(2)}) collective-permute-start(bf16[1024,1024]{1,0:T(8,128)(2,1)} %refs_7_.3), channel_id=1, source_target_pairs={{0,1},{1,0},{2,3},{3,2},{4,5},{5,4},{6,7},{7,6},{8,9},{9,8},{10,11... | collective-permute-start | bytes 6291464 | tf_op jit(solution)/shard_map/ppermute | solution.py:454
  1.7 37.0 %collective-permute-start.3 = (bf16[1024,768]{1,0:T(8,128)(2,1)}, bf16[1024,768]{1,0:T(8,128)(2,1)}, u32[]{:S(2)}, u32[]{:S(2)}) collective-permute-start(bf16[1024,768]{1,0:T(8,128)(2,1)} %refs_4_.3), channel_id=1, source_target_pairs={{0,2},{1,3},{2,0},{3,1},{4,6},{5,7},{6,4},{7,5},{8,10},{9,11},{10,... | collective-permute-start | bytes 4718600 | tf_op jit(solution)/shard_map/ppermute | solution.py:454
  112.5 54.2 %collective-permute-start.17 = (bf16[512,1024]{1,0:T(8,128)(2,1)}, bf16[512,1024]{1,0:T(8,128)(2,1)}, u32[]{:S(2)}, u32[]{:S(2)}) collective-permute-start(bf16[512,1024]{1,0:T(8,128)(2,1)} %collective-permute-done.14.refs_9_), channel_id=1, source_target_pairs={{0,1},{1,0},{2,3},{3,2},{4,5},{5,4},{6,7},{7,6},{8,9},{9,8},{10,11... | collective-permute-start | bytes 3145736 | tf_op jit(solution)/shard_map/ppermute | solution.py:454
  112.6 54.1 %collective-permute-start.15 = (bf16[1024,512]{1,0:T(8,128)(2,1)S(1)}, bf16[1024,512]{1,0:T(8,128)(2,1)}, u32[]{:S(2)}, u32[]{:S(2)}) collective-permute-start(bf16[1024,512]{1,0:T(8,128)(2,1)S(1)} %get-tuple-element.278), channel_id=1, source_target_pairs={{0,2},{1,3},{2,0},{3,1},{4,6},{5,7},{6,4},{7,5},{8,10},{9,11},{10,... | collective-permute-start | bytes 3145736 | tf_op jit(solution)/shard_map/ppermute | solution.py:454
  114.0 52.8 %collective-permute-start.16 = (bf16[512,1024]{1,0:T(8,128)(2,1)S(1)}, bf16[512,1024]{1,0:T(8,128)(2,1)}, u32[]{:S(2)}, u32[]{:S(2)}) collective-permute-start(bf16[512,1024]{1,0:T(8,128)(2,1)S(1)} %copy-done.13), channel_id=1, source_target_pairs={{0,2},{1,3},{2,0},{3,1},{4,6},{5,7},{6,4},{7,5},{8,10},{9,11},{10,... | collective-permute-start | bytes 3145736 | tf_op jit(solution)/shard_map/ppermute | solution.py:454
  167.5 55.3 %collective-permute-start.21 = (bf16[1024,1024]{1,0:T(8,128)(2,1)}, bf16[1024,1024]{1,0:T(8,128)(2,1)S(1)}, u32[]{:S(2)}, u32[]{:S(2)}) collective-permute-start(bf16[1024,1024]{1,0:T(8,128)(2,1)} %get-tuple-element.295), channel_id=1, source_target_pairs={{0,1},{1,0},{2,3},{3,2},{4,5},{5,4},{6,7},{7,6},{8,9},{9,8},{10,11... | collective-permute-start | bytes 6291464 | tf_op jit(solution)/shard_map/ppermute | solution.py:454
  168.0 54.7 %collective-permute-start.20 = (bf16[512,1024]{1,0:T(8,128)(2,1)}, bf16[512,1024]{1,0:T(8,128)(2,1)}, u32[]{:S(2)}, u32[]{:S(2)}) collective-permute-start(bf16[512,1024]{1,0:T(8,128)(2,1)} %collective-permute-done.16.refs_9_), channel_id=1, source_target_pairs={{0,1},{1,0},{2,3},{3,2},{4,5},{5,4},{6,7},{7,6},{8,9},{9,8},{10,11... | collective-permute-start | bytes 3145736 | tf_op jit(solution)/shard_map/ppermute | solution.py:454
  168.0 54.7 %collective-permute-start.19 = (bf16[1024,512]{1,0:T(8,128)(2,1)S(1)}, bf16[1024,512]{1,0:T(8,128)(2,1)}, u32[]{:S(2)}, u32[]{:S(2)}) collective-permute-start(bf16[1024,512]{1,0:T(8,128)(2,1)S(1)} %get-tuple-element.291), channel_id=1, source_target_pairs={{0,2},{1,3},{2,0},{3,1},{4,6},{5,7},{6,4},{7,5},{8,10},{9,11},{10,... | collective-permute-start | bytes 3145736 | tf_op jit(solution)/shard_map/ppermute | solution.py:454
  231.0 55.5 %collective-permute-start.24 = (bf16[1024,1024]{1,0:T(8,128)(2,1)}, bf16[1024,1024]{1,0:T(8,128)(2,1)}, u32[]{:S(2)}, u32[]{:S(2)}) collective-permute-start(bf16[1024,1024]{1,0:T(8,128)(2,1)} %add_convert_fusion.2), channel_id=1, source_target_pairs={{0,2},{1,3},{2,0},{3,1},{4,6},{5,7},{6,4},{7,5},{8,10},{9,11},{10,... | collective-permute-start | bytes 6291464 | tf_op jit(solution)/shard_map/ppermute | solution.py:454
  328.3 60.3 %collective-permute-start.28 = (bf16[1024,1024]{1,0:T(8,128)(2,1)}, bf16[1024,1024]{1,0:T(8,128)(2,1)S(1)}, u32[]{:S(2)}, u32[]{:S(2)}) collective-permute-start(bf16[1024,1024]{1,0:T(8,128)(2,1)} %get-tuple-element.333), channel_id=1, source_target_pairs={{0,1},{1,0},{2,3},{3,2},{4,5},{5,4},{6,7},{7,6},{8,9},{9,8},{10,11... | collective-permute-start | bytes 6291464 | tf_op jit(solution)/shard_map/ppermute | solution.py:454
  328.4 60.2 %collective-permute-start.27 = (bf16[1024,1024]{1,0:T(8,128)(2,1)}, bf16[1024,1024]{1,0:T(8,128)(2,1)}, u32[]{:S(2)}, u32[]{:S(2)}) collective-permute-start(bf16[1024,1024]{1,0:T(8,128)(2,1)} %add_convert_fusion.1), channel_id=1, source_target_pairs={{0,2},{1,3},{2,0},{3,1},{4,6},{5,7},{6,4},{7,5},{8,10},{9,11},{10,... | collective-permute-start | bytes 6291464 | tf_op jit(solution)/shard_map/ppermute | solution.py:454
  331.3 57.3 %collective-permute-start.29 = (bf16[128,1024]{1,0:T(8,128)(2,1)S(1)}, bf16[128,1024]{1,0:T(8,128)(2,1)S(1)}, u32[]{:S(2)}, u32[]{:S(2)}) collective-permute-start(bf16[128,1024]{1,0:T(8,128)(2,1)S(1)} %get-tuple-element.336), channel_id=1, source_target_pairs={{0,8},{4,12},{8,0},{12,4},{16,24},{20,28},{24,16},{28,20},{1,9},{5... | collective-permute-start | bytes 786440 | tf_op jit(solution)/shard_map/ppermute | solution.py:454
  331.7 56.9 %collective-permute-start.30 = (bf16[128,1024]{1,0:T(8,128)(2,1)S(1)}, bf16[128,1024]{1,0:T(8,128)(2,1)S(1)}, u32[]{:S(2)}, u32[]{:S(2)}) collective-permute-start(bf16[128,1024]{1,0:T(8,128)(2,1)S(1)} %get-tuple-element.337), channel_id=1, source_target_pairs={{0,16},{4,20},{8,24},{12,28},{16,0},{20,4},{24,8},{28,12},{1,17},{... | collective-permute-start | bytes 786440 | tf_op jit(solution)/shard_map/ppermute | solution.py:454
  334.5 54.1 %collective-permute-start.31 = (bf16[128,1024]{1,0:T(8,128)(2,1)S(1)}, bf16[128,1024]{1,0:T(8,128)(2,1)S(1)}, u32[]{:S(2)}, u32[]{:S(2)}) collective-permute-start(bf16[128,1024]{1,0:T(8,128)(2,1)S(1)} %get-tuple-element.338), channel_id=1, source_target_pairs={{0,24},{4,28},{8,16},{12,20},{16,8},{20,12},{24,0},{28,4},{1,25},{... | collective-permute-start | bytes 786440 | tf_op jit(solution)/shard_map/ppermute | solution.py:454
  391.8 52.3 %collective-permute-start.36 = (bf16[128,1024]{1,0:T(8,128)(2,1)S(1)}, bf16[128,1024]{1,0:T(8,128)(2,1)}, u32[]{:S(2)}, u32[]{:S(2)}) collective-permute-start(bf16[128,1024]{1,0:T(8,128)(2,1)S(1)} %add_convert_fusion.14), channel_id=1, source_target_pairs={{0,8},{4,12},{8,0},{12,4},{16,24},{20,28},{24,16},{28,20},{1,9},{5... | collective-permute-start | bytes 786440 | tf_op jit(solution)/shard_map/ppermute | solution.py:454
  393.1 50.9 %collective-permute-start.37 = (bf16[128,1024]{1,0:T(8,128)(2,1)S(1)}, bf16[128,1024]{1,0:T(8,128)(2,1)}, u32[]{:S(2)}, u32[]{:S(2)}) collective-permute-start(bf16[128,1024]{1,0:T(8,128)(2,1)S(1)} %add_convert_fusion.14), channel_id=1, source_target_pairs={{0,16},{4,20},{8,24},{12,28},{16,0},{20,4},{24,8},{28,12},{1,17},{... | collective-permute-start | bytes 786440 | tf_op jit(solution)/shard_map/ppermute | solution.py:454
  400.0 44.1 %collective-permute-start.38 = (bf16[128,1024]{1,0:T(8,128)(2,1)S(1)}, bf16[128,1024]{1,0:T(8,128)(2,1)S(1)}, u32[]{:S(2)}, u32[]{:S(2)}) collective-permute-start(bf16[128,1024]{1,0:T(8,128)(2,1)S(1)} %add_convert_fusion.14), channel_id=1, source_target_pairs={{0,24},{4,28},{8,16},{12,20},{16,8},{20,12},{24,0},{28,4},{1,25},{... | collective-permute-start | bytes 786440 | tf_op jit(solution)/shard_map/ppermute | solution.py:454
  400.8 43.3 %collective-permute-start.35 = (bf16[512,1024]{1,0:T(8,128)(2,1)}, bf16[512,1024]{1,0:T(8,128)(2,1)S(1)}, u32[]{:S(2)}, u32[]{:S(2)}) collective-permute-start(bf16[512,1024]{1,0:T(8,128)(2,1)} %get-tuple-element.365), channel_id=1, source_target_pairs={{0,4},{4,0},{8,12},{12,8},{16,20},{20,16},{24,28},{28,24},{1,5},{5... | collective-permute-start | bytes 3145736 | tf_op jit(solution)/shard_map/ppermute | solution.py:454
  446.3 49.5 %collective-permute-start.44 = (bf16[512,1024]{1,0:T(8,128)(2,1)S(1)}, bf16[512,1024]{1,0:T(8,128)(2,1)S(1)}, u32[]{:S(2)}, u32[]{:S(2)}) collective-permute-start(bf16[512,1024]{1,0:T(8,128)(2,1)S(1)} %pad_maximum_fusion.refs_0_), channel_id=1, source_target_pairs={{0,4},{4,0},{8,12},{12,8},{16,20},{20,16},{24,28},{28,24},{1,5},{5... | collective-permute-start | bytes 3145736 | tf_op jit(solution)/shard_map/ppermute | solution.py:454
  447.8 48.0 %collective-permute-start.41 = (bf16[128,1024]{1,0:T(8,128)(2,1)S(1)}, bf16[128,1024]{1,0:T(8,128)(2,1)S(1)}, u32[]{:S(2)}, u32[]{:S(2)}) collective-permute-start(bf16[128,1024]{1,0:T(8,128)(2,1)S(1)} %get-tuple-element.383), channel_id=1, source_target_pairs={{0,8},{4,12},{8,0},{12,4},{16,24},{20,28},{24,16},{28,20},{1,9},{5... | collective-permute-start | bytes 786440 | tf_op jit(solution)/shard_map/ppermute | solution.py:454
  450.9 44.9 %collective-permute-start.42 = (bf16[128,1024]{1,0:T(8,128)(2,1)S(1)}, bf16[128,1024]{1,0:T(8,128)(2,1)S(1)}, u32[]{:S(2)}, u32[]{:S(2)}) collective-permute-start(bf16[128,1024]{1,0:T(8,128)(2,1)S(1)} %get-tuple-element.384), channel_id=1, source_target_pairs={{0,16},{4,20},{8,24},{12,28},{16,0},{20,4},{24,8},{28,12},{1,17},{... | collective-permute-start | bytes 786440 | tf_op jit(solution)/shard_map/ppermute | solution.py:454
  451.3 44.5 %collective-permute-start.43 = (bf16[128,1024]{1,0:T(8,128)(2,1)S(1)}, bf16[128,1024]{1,0:T(8,128)(2,1)S(1)}, u32[]{:S(2)}, u32[]{:S(2)}) collective-permute-start(bf16[128,1024]{1,0:T(8,128)(2,1)S(1)} %get-tuple-element.385), channel_id=1, source_target_pairs={{0,24},{4,28},{8,16},{12,20},{16,8},{20,12},{24,0},{28,4},{1,25},{... | collective-permute-start | bytes 786440 | tf_op jit(solution)/shard_map/ppermute | solution.py:454
  454.8 47.5 %collective-permute-start.40 = (bf16[1024,1024]{1,0:T(8,128)(2,1)}, bf16[1024,1024]{1,0:T(8,128)(2,1)}, u32[]{:S(2)}, u32[]{:S(2)}) collective-permute-start(bf16[1024,1024]{1,0:T(8,128)(2,1)} %add_convert_fusion), channel_id=1, source_target_pairs={{0,2},{1,3},{2,0},{3,1},{4,6},{5,7},{6,4},{7,5},{8,10},{9,11},{10,... | collective-permute-start | bytes 6291464 | tf_op jit(solution)/shard_map/ppermute | solution.py:454
  (77 other events, 1078.7 us)

commit v5 on v4

--- a/solution.py
+++ b/solution.py
@@ -828,10 +828,12 @@
     def ffn(picks, part, extra):
         widths = [FQ if half is None else FQ // 2 for _, half in picks]
         spots = [(k, width, half or 0) for (k, half), width in zip(picks, widths)]
-        ins = [(n2, full), (cotangent, full)]
+        high = rows if extra is not None else many * STRETCH
+        row = rows_spec(high, D)
+        ins = [(n2, row), (cotangent, row)]
         ins += [(be_slots[k][None, :], whole_spec((1, width), at)) for k, width, at in spots]
         if part is not None:
-            ins += [(part[0], full), (part[1], full)]
+            ins += [(part[0], row), (part[1], row)]
         for group, spec, dims in ((we, whole_spec, (D, None)), (wr, part_spec, (None, D))):
             for k, width, at in spots:
                 shape = tuple(d or width for d in dims)
@@ -841,7 +843,7 @@
         outs = [(like((2 * w, D), bf16), whole_spec((2 * w, D))) for w in widths]
         outs += [(like((8, w), f32), sum_spec((8, w))) for w in widths]
         if extra is None:
-            outs += [wide, wide]
+            outs += [(wide[0], row)] * 2
         else:
             ins += extra
             outs += [low, wide, low, low, low]
@@ -855,7 +857,7 @@
             functools.partial(ffn_kernel, blocks, widths, part is None, extra is not None),
             "ffn",
             (first,) if extra is not None else (),
-            tiles,
+            R // high,
             ins,
             outs,
             [pltpu.VMEM((2 * w, D), f32) for w in widths],
@@ -929,25 +931,26 @@
 
     def back(pick, q, k, v, state):
         count = len(pick)
+        steps, high = nb // many, many * STRETCH
         at, inner, width = pick[0] // count, (pick[0] % 2) // count, count * QW
         return call(
-            functools.partial(back_kernel, blocks, tiles, count),
+            functools.partial(back_kernel, many, steps, count),
             "attend_back",
             (cont,),
-            tiles,
-            [(a, back_spec(rows, width, tiles, inner)) for a in (q, k, v)]
-            + [(a, back_spec(rows, width, tiles, at)) for a in (gn, t)]
+            steps,
+            [(a, back_spec(high, width, steps, inner)) for a in (q, k, v)]
+            + [(a, back_spec(high, width, steps, at)) for a in (gn, t)]
             + [
-                (st, back_spec(blocks * DH, width, tiles, at)),
-                (kt, back_spec(blocks * 8, width, tiles, at)),
-                (pr, back_spec(blocks * DH, width, tiles, at)),
-                (kr, back_spec(blocks * 8, width, tiles, at)),
+                (st, back_spec(many * DH, width, steps, at)),
+                (kt, back_spec(many * 8, width, steps, at)),
+                (pr, back_spec(many * DH, width, steps, at)),
+                (kr, back_spec(many * 8, width, steps, at)),
                 (state, whole_spec((state_rows, width), at)),
-                (normed, back_spec(rows, D, tiles)),
-                (att, back_spec(rows, width, tiles, at)),
-                (branch, back_spec(rows, D, tiles)),
+                (normed, back_spec(high, D, steps)),
+                (att, back_spec(high, width, steps, at)),
+                (branch, back_spec(high, D, steps)),
             ],
-            [(like((R, PW), bf16), back_spec(rows, PW, tiles))] * count
+            [(like((R, PW), bf16), back_spec(high, PW, steps))] * count
             + [(like((PW + QW, D), bf16), whole_spec((PW + QW, D)))] * count
             + [(like((8, count * PW), f32), sum_spec((8, count * PW)))],
             [pltpu.VMEM((DH, width), f32), pltpu.VMEM((8, width), f32)]

time: 639 us -> 630 us (0.986)
  Pallas kernels: 440 us -> 432 us
    pallas_call x14, Pallas kernels: 440 us -> 432 us  [call(): pl.pallas_call(kernel, grid_spec=pltpu.PrefetchScalarGridSpec(num_scalar_...]
where the time goes in v5:
time: 630 us; the launch traced here: 621 us
  Pallas kernels  432 us (69%)
  waiting for transfers between devices  65.6 us (10%)
  starting transfers between devices  53.5 us (8%)
  other arithmetic  51.2 us (8%)
  local copies, waits for them, and re-layouts  16.4 us (3%)
    pallas_call x14, Pallas kernels, call(): pl.pallas_call(kernel, grid_spec=pltpu.PrefetchScalarGridSpec(num_scalar_...  432 us
    ppermute x66, waiting for transfers between devices, swap(): return lax.ppermute(value, axis, [(i, i ^ bit) for i in range(size)])  65.6 us
    ppermute x66, starting transfers between devices, swap(): return lax.ppermute(value, axis, [(i, i ^ bit) for i in range(size)])  53.5 us
    convert_element_type x3, other arithmetic, half(): return total.astype(bf16)  13.1 us
  transfers between devices with their start and end apart: 66, of which 19 were waited for; matrix products, arithmetic and copies ran while one was open for 8% of the time, Pallas kernels for 70%

profile of v5, /device:TPU:8, one launch (start us, length us, event | category | flops | bytes accessed | tf_op | source)
XLA Modules:
  0.0 621.2 jit_solution(11691513260458936195)
XLA Ops:
  12.4 19.1 %qkv.2 = (bf16[2560,512]{1,0:T(8,128)(2,1)}, bf16[2560,512]{1,0:T(8,128)(2,1)}, bf16[2560,512]{1,0:T(8,128)(2,1)}, bf16[2560,1024]{1,0:T(8,128)(2,1)}, f32[72,51...) custom-call(s32[20]{0:T(128)} %subtract_maximum_fusion.thr, s32[21]{0:T(128)} %add_convert_fusion.15.cont, ...), custom_call_target="tpu_custom_call" | custom-call | flops 8053063680 | bytes 24117248 | tf_op jit(solution)/shard_map/qkv/pallas_call | solution.py:431
  31.5 7.1 %collective-permute-done.4 = f32[3584]{0:T(1024)S(1)} collective-permute-done((f32[3584]{0:T(1024)S(1)}, f32[3584]{0:T(1024)S(1)}, u32[]{:S(2)}, u32[]{:S(2)}) %collective-permute-start.4) | collective-permute-done | bytes 14368 | tf_op jit(solution)/shard_map/ppermute | solution.py:454
  46.8 16.2 %qkv.3 = (bf16[2560,512]{1,0:T(8,128)(2,1)}, bf16[2560,512]{1,0:T(8,128)(2,1)}, bf16[2560,512]{1,0:T(8,128)(2,1)}, f32[72,512]{1,0:T(8,128)}, f32[1280,512]{1,0:T(8,128)}, /*index=5*/f32[160,512]{1,0:T(8,128)}) custom-call(s32[20]{0:T(128)} %subtract_maximum_fusion.thr, s32[21]{0:T(128)} %add_convert_fusion.15.cont, ...), custom_call_target="tpu_custom_call" | custom-call | flops 8053063680 | bytes 24117248 | tf_op jit(solution)/shard_map/qkv/pallas_call | solution.py:431
  77.7 34.9 %attend.1 = (bf16[2560,1024]{1,0:T(8,128)(2,1)}, f32[2560,1024]{1,0:T(8,128)}, bf16[1280,1024]{1,0:T(8,128)(2,1)}, f32[160,1024]{1,0:T(8,128)}, f32[2560,1024]{1,0:T(8,128)}, /*index=5*/bf16[2560,1024]{1,0:T(8,128)(2,1)}) custom-call(s32[20]{0:T(128)} %compare_convert_fusion.first.refs_0_, s32[20]{0:T(128)} %subtract_maximum_fusion.thr, ...), custom_call_target="tpu_custom_call" | custom-call | flops 32212254720 | bytes 52428800 | tf_op jit(solution)/shard_map/attend/pallas_call | solution.py:431
  114.8 49.2 %ffn.5 = (bf16[1024,1024]{1,0:T(8,128)(2,1)}, bf16[1024,1024]{1,0:T(8,128)(2,1)}, f32[8,512]{1,0:T(8,128)}, f32[8,512]{1,0:T(8,128)}, f32[2560,1024]{1,0:T(8,128)}, /*index=5*/f32[2560,1024]{1,0:T(8,128)}) custom-call(bf16[2560,1024]{1,0:T(8,128)(2,1)} %get-tuple-element.289.refs_0_.refs_1_, bf16[2560,1024]{1,0:T(8,128)(2,1)} %refs_2_.1, ...), custom_call_target="tpu_custom_call" | custom-call | flops 32212254720 | bytes 52428800 | tf_op jit(solution)/shard_map/ffn/pallas_call | solution.py:431
  167.0 50.7 %ffn.6 = (bf16[1024,1024]{1,0:T(8,128)(2,1)}, bf16[1024,1024]{1,0:T(8,128)(2,1)}, f32[8,512]{1,0:T(8,128)}, f32[8,512]{1,0:T(8,128)}, f32[2560,1024]{1,0:T(8,128)}, /*index=5*/f32[2560,1024]{1,0:T(8,128)}) custom-call(bf16[2560,1024]{1,0:T(8,128)(2,1)} %get-tuple-element.289.refs_0_.refs_1_, bf16[2560,1024]{1,0:T(8,128)(2,1)} %refs_2_.1, ...), custom_call_target="tpu_custom_call" | custom-call | flops 32212254720 | bytes 52428800 | tf_op jit(solution)/shard_map/ffn/pallas_call | solution.py:431
  228.4 50.9 %ffn.7 = (bf16[1024,1024]{1,0:T(8,128)(2,1)}, bf16[1024,1024]{1,0:T(8,128)(2,1)}, f32[8,512]{1,0:T(8,128)}, f32[8,512]{1,0:T(8,128)}, f32[2560,1024]{1,0:T(8,128)}, /*index=5*/f32[2560,1024]{1,0:T(8,128)}) custom-call(bf16[2560,1024]{1,0:T(8,128)(2,1)} %get-tuple-element.289.refs_0_.refs_1_, bf16[2560,1024]{1,0:T(8,128)(2,1)} %refs_2_.1, ...), custom_call_target="tpu_custom_call" | custom-call | flops 32212254720 | bytes 52428800 | tf_op jit(solution)/shard_map/ffn/pallas_call | solution.py:431
  279.5 4.8 add_convert_fusion.10
  285.6 3.9 add_convert_fusion.1
  289.5 29.0 %ffn.8 = (bf16[1024,1024]{1,0:T(8,128)(2,1)}, f32[8,512]{1,0:T(8,128)}, f32[2560,1024]{1,0:T(8,128)}, f32[2560,1024]{1,0:T(8,128)}) custom-call(bf16[2560,1024]{1,0:T(8,128)(2,1)} %get-tuple-element.289.refs_0_.refs_1_, bf16[2560,1024]{1,0:T(8,128)(2,1)} %refs_2_.1, f32[1,1024]{1,0:T(1,128)} %bitcast.61, f32[2560,1024]{1,0:T(8,128)} %get-tuple-element.324.refs_3_, ...), custom_call_target="tpu_custom_call" | custom-call | flops 16106127360 | bytes 52428800 | tf_op jit(solution)/shard_map/ffn/pallas_call | solution.py:431
  326.3 53.8 %ffn.9 = (bf16[1024,1024]{1,0:T(8,128)(2,1)}, f32[8,512]{1,0:T(8,128)}, bf16[2560,1024]{1,0:T(8,128)(2,1)}, f32[2560,1024]{1,0:T(8,128)}, bf16[2560,1024]{1,0:T(...) custom-call(s32[20]{0:T(128)} %compare_convert_fusion.first.refs_0_,, ...), custom_call_target="tpu_custom_call" | custom-call | flops 16106127360 | bytes 52428800 | tf_op jit(solution)/shard_map/ffn/pallas_call | solution.py:431
  386.8 4.6 add_convert_fusion.7
  395.5 39.8 %attend_back.2 = (bf16[2560,768]{1,0:T(8,128)(2,1)}, bf16[2560,768]{1,0:T(8,128)(2,1)}, bf16[1024,1024]{1,0:T(8,128)(2,1)}, bf16[1024,1024]{1,0:T(8,128)(2,1)}, f32[8,1536]{1,0:T(8,128)}) custom-call(s32[21]{0:T(128)} %add_convert_fusion.15.cont, bf16[2560,512]{1,0:T(8,128)(2,1)} %get-tuple-element.261.refs_5_.refs_12_.q, ...), custom_call_target="tpu_custom_call" | custom-call | flops 32212254720 | bytes 26214400 | tf_op jit(solution)/shard_map/attend_back/pallas_call | solution.py:431
  447.3 40.2 %attend_back.3 = (bf16[2560,768]{1,0:T(8,128)(2,1)}, bf16[2560,768]{1,0:T(8,128)(2,1)}, bf16[1024,1024]{1,0:T(8,128)(2,1)}, bf16[1024,1024]{1,0:T(8,128)(2,1)}, f32[8,1536]{1,0:T(8,128)}) custom-call(s32[21]{0:T(128)} %add_convert_fusion.15.cont, bf16[2560,512]{1,0:T(8,128)(2,1)} %get-tuple-element.245.refs_0_.refs_11_.q, ...), custom_call_target="tpu_custom_call" | custom-call | flops 32212254720 | bytes 26214400 | tf_op jit(solution)/shard_map/attend_back/pallas_call | solution.py:431
  487.6 6.0 collective-permute-done.40
  493.6 4.4 collective-permute-done.45
  507.7 16.3 %input_grad.2 = (f32[2560,1024]{1,0:T(8,128)}, f32[16,1024]{1,0:T(8,128)}) custom-call(bf16[2560,1024]{1,0:T(8,128)(2,1)} %x.1, f32[2560,1024]{1,0:T(8,128)} %get-tuple-element.404.gm, f32[1,1024]{1,0:T(1,128)} %bitcast.49, bf16[2560,768]{1,0:T(8,128)(2,1)} %get-tuple-element.405.refs_0_, bf16[2560,768]{1,0:T(8,128)(2,1)} %get-tuple-element.406.refs_1_, ...), custom_call_target="tpu_custom_call" | custom-call | flops 8053063680 | bytes 20971520 | tf_op jit(solution)/shard_map/input_grad/pallas_call | solution.py:431
  524.5 6.2 collective-permute-done.49
  539.6 16.5 %input_grad.3 = (f32[2560,1024]{1,0:T(8,128)}, f32[16,1024]{1,0:T(8,128)}) custom-call(bf16[2560,1024]{1,0:T(8,128)(2,1)} %x.1, f32[2560,1024]{1,0:T(8,128)} %get-tuple-element.404.gm, f32[1,1024]{1,0:T(1,128)} %bitcast.50, bf16[2560,768]{1,0:T(8,128)(2,1)} %get-tuple-element.405.refs_0_, ...), custom_call_target="tpu_custom_call", output_to_operand_aliasing={{0}: (11, {})} | custom-call | flops 8053063680 | bytes 20971520 | tf_op jit(solution)/shard_map/input_grad/pallas_call | solution.py:431
  556.5 4.7 collective-permute-done.52
  567.3 7.9 %place.2 = f32[1024,1024]{1,0:T(8,128)} custom-call(s32[2]{0:T(128)} %pad_add_fusion.where, bf16[512,1024]{1,0:T(8,128)(2,1)} %copy-done, bf16[512,1024]{1,0:T(8,128)(2,1)} %copy-done.5, bf16[512,1024]{1,0:T(8,128)(2,1)} %copy-done.1, bf16[512,1024]{1,0:T(8,128)(2,1)} %copy-done.6), custom_call_target="tpu_custom_call" | custom-call | bytes 6291456 | tf_op jit(solution)/shard_map/place/pallas_call | solution.py:431
  575.3 5.5 collective-permute-done.55
  580.7 4.6 collective-permute-done.56
  600.2 7.8 %place.3 = f32[1024,1024]{1,0:T(8,128)} custom-call(s32[2]{0:T(128)} %pad_add_fusion.where, bf16[512,1024]{1,0:T(8,128)(2,1)} %copy-done, bf16[512,1024]{1,0:T(8,128)(2,1)} %copy-done.5, bf16[512,1024]{1,0:T(8,128)(2,1)} %copy-done.1, bf16[512,1024]{1,0:T(8,128)(2,1)} %copy-done.6), custom_call_target="tpu_custom_call" | custom-call | bytes 6291456 | tf_op jit(solution)/shard_map/place/pallas_call | solution.py:431
  (281 shorter events, 135.1 us)
Async XLA Ops:
  1.2 37.5 %collective-permute-start.6 = (bf16[1024,1024]{1,0:T(8,128)(2,1)}, bf16[1024,1024]{1,0:T(8,128)(2,1)}, u32[]{:S(2)}, u32[]{:S(2)}) collective-permute-start(bf16[1024,1024]{1,0:T(8,128)(2,1)} %refs_6_.1), channel_id=1, source_target_pairs={{0,1},{1,0},{2,3},{3,2},{4,5},{5,4},{6,7},{7,6},{8,9},{9,8},{10,11... | collective-permute-start | bytes 6291464 | tf_op jit(solution)/shard_map/ppermute | solution.py:454
  1.3 37.4 %collective-permute-start.7 = (bf16[1024,1024]{1,0:T(8,128)(2,1)}, bf16[1024,1024]{1,0:T(8,128)(2,1)}, u32[]{:S(2)}, u32[]{:S(2)}) collective-permute-start(bf16[1024,1024]{1,0:T(8,128)(2,1)} %refs_7_.3), channel_id=1, source_target_pairs={{0,1},{1,0},{2,3},{3,2},{4,5},{5,4},{6,7},{7,6},{8,9},{9,8},{10,11... | collective-permute-start | bytes 6291464 | tf_op jit(solution)/shard_map/ppermute | solution.py:454
  1.7 37.0 %collective-permute-start.3 = (bf16[1024,768]{1,0:T(8,128)(2,1)}, bf16[1024,768]{1,0:T(8,128)(2,1)}, u32[]{:S(2)}, u32[]{:S(2)}) collective-permute-start(bf16[1024,768]{1,0:T(8,128)(2,1)} %refs_4_.3), channel_id=1, source_target_pairs={{0,2},{1,3},{2,0},{3,1},{4,6},{5,7},{6,4},{7,5},{8,10},{9,11},{10,... | collective-permute-start | bytes 4718600 | tf_op jit(solution)/shard_map/ppermute | solution.py:454
  112.6 51.3 %collective-permute-start.17 = (bf16[512,1024]{1,0:T(8,128)(2,1)}, bf16[512,1024]{1,0:T(8,128)(2,1)}, u32[]{:S(2)}, u32[]{:S(2)}) collective-permute-start(bf16[512,1024]{1,0:T(8,128)(2,1)} %collective-permute-done.14.refs_9_), channel_id=1, source_target_pairs={{0,1},{1,0},{2,3},{3,2},{4,5},{5,4},{6,7},{7,6},{8,9},{9,8},{10,11... | collective-permute-start | bytes 3145736 | tf_op jit(solution)/shard_map/ppermute | solution.py:454
  112.7 51.3 %collective-permute-start.15 = (bf16[1024,512]{1,0:T(8,128)(2,1)S(1)}, bf16[1024,512]{1,0:T(8,128)(2,1)}, u32[]{:S(2)}, u32[]{:S(2)}) collective-permute-start(bf16[1024,512]{1,0:T(8,128)(2,1)S(1)} %get-tuple-element.278), channel_id=1, source_target_pairs={{0,2},{1,3},{2,0},{3,1},{4,6},{5,7},{6,4},{7,5},{8,10},{9,11},{10,... | collective-permute-start | bytes 3145736 | tf_op jit(solution)/shard_map/ppermute | solution.py:454
  114.1 49.8 %collective-permute-start.16 = (bf16[512,1024]{1,0:T(8,128)(2,1)S(1)}, bf16[512,1024]{1,0:T(8,128)(2,1)}, u32[]{:S(2)}, u32[]{:S(2)}) collective-permute-start(bf16[512,1024]{1,0:T(8,128)(2,1)S(1)} %copy-done.13), channel_id=1, source_target_pairs={{0,2},{1,3},{2,0},{3,1},{4,6},{5,7},{6,4},{7,5},{8,10},{9,11},{10,... | collective-permute-start | bytes 3145736 | tf_op jit(solution)/shard_map/ppermute | solution.py:454
  164.7 53.1 %collective-permute-start.21 = (bf16[1024,1024]{1,0:T(8,128)(2,1)}, bf16[1024,1024]{1,0:T(8,128)(2,1)S(1)}, u32[]{:S(2)}, u32[]{:S(2)}) collective-permute-start(bf16[1024,1024]{1,0:T(8,128)(2,1)} %get-tuple-element.295), channel_id=1, source_target_pairs={{0,1},{1,0},{2,3},{3,2},{4,5},{5,4},{6,7},{7,6},{8,9},{9,8},{10,11... | collective-permute-start | bytes 6291464 | tf_op jit(solution)/shard_map/ppermute | solution.py:454
  165.1 52.6 %collective-permute-start.20 = (bf16[512,1024]{1,0:T(8,128)(2,1)}, bf16[512,1024]{1,0:T(8,128)(2,1)}, u32[]{:S(2)}, u32[]{:S(2)}) collective-permute-start(bf16[512,1024]{1,0:T(8,128)(2,1)} %collective-permute-done.16.refs_9_), channel_id=1, source_target_pairs={{0,1},{1,0},{2,3},{3,2},{4,5},{5,4},{6,7},{7,6},{8,9},{9,8},{10,11... | collective-permute-start | bytes 3145736 | tf_op jit(solution)/shard_map/ppermute | solution.py:454
  165.2 52.6 %collective-permute-start.19 = (bf16[1024,512]{1,0:T(8,128)(2,1)S(1)}, bf16[1024,512]{1,0:T(8,128)(2,1)}, u32[]{:S(2)}, u32[]{:S(2)}) collective-permute-start(bf16[1024,512]{1,0:T(8,128)(2,1)S(1)} %get-tuple-element.291), channel_id=1, source_target_pairs={{0,2},{1,3},{2,0},{3,1},{4,6},{5,7},{6,4},{7,5},{8,10},{9,11},{10,... | collective-permute-start | bytes 3145736 | tf_op jit(solution)/shard_map/ppermute | solution.py:454
  226.1 53.3 %collective-permute-start.24 = (bf16[1024,1024]{1,0:T(8,128)(2,1)}, bf16[1024,1024]{1,0:T(8,128)(2,1)}, u32[]{:S(2)}, u32[]{:S(2)}) collective-permute-start(bf16[1024,1024]{1,0:T(8,128)(2,1)} %add_convert_fusion.2), channel_id=1, source_target_pairs={{0,2},{1,3},{2,0},{3,1},{4,6},{5,7},{6,4},{7,5},{8,10},{9,11},{10,... | collective-permute-start | bytes 6291464 | tf_op jit(solution)/shard_map/ppermute | solution.py:454
  319.4 60.7 %collective-permute-start.28 = (bf16[1024,1024]{1,0:T(8,128)(2,1)}, bf16[1024,1024]{1,0:T(8,128)(2,1)S(1)}, u32[]{:S(2)}, u32[]{:S(2)}) collective-permute-start(bf16[1024,1024]{1,0:T(8,128)(2,1)} %get-tuple-element.333), channel_id=1, source_target_pairs={{0,1},{1,0},{2,3},{3,2},{4,5},{5,4},{6,7},{7,6},{8,9},{9,8},{10,11... | collective-permute-start | bytes 6291464 | tf_op jit(solution)/shard_map/ppermute | solution.py:454
  319.6 60.5 %collective-permute-start.27 = (bf16[1024,1024]{1,0:T(8,128)(2,1)}, bf16[1024,1024]{1,0:T(8,128)(2,1)}, u32[]{:S(2)}, u32[]{:S(2)}) collective-permute-start(bf16[1024,1024]{1,0:T(8,128)(2,1)} %add_convert_fusion.1), channel_id=1, source_target_pairs={{0,2},{1,3},{2,0},{3,1},{4,6},{5,7},{6,4},{7,5},{8,10},{9,11},{10,... | collective-permute-start | bytes 6291464 | tf_op jit(solution)/shard_map/ppermute | solution.py:454
  322.7 57.4 %collective-permute-start.29 = (bf16[128,1024]{1,0:T(8,128)(2,1)S(1)}, bf16[128,1024]{1,0:T(8,128)(2,1)S(1)}, u32[]{:S(2)}, u32[]{:S(2)}) collective-permute-start(bf16[128,1024]{1,0:T(8,128)(2,1)S(1)} %get-tuple-element.336), channel_id=1, source_target_pairs={{0,8},{4,12},{8,0},{12,4},{16,24},{20,28},{24,16},{28,20},{1,9},{5... | collective-permute-start | bytes 786440 | tf_op jit(solution)/shard_map/ppermute | solution.py:454
  323.0 57.1 %collective-permute-start.30 = (bf16[128,1024]{1,0:T(8,128)(2,1)S(1)}, bf16[128,1024]{1,0:T(8,128)(2,1)S(1)}, u32[]{:S(2)}, u32[]{:S(2)}) collective-permute-start(bf16[128,1024]{1,0:T(8,128)(2,1)S(1)} %get-tuple-element.337), channel_id=1, source_target_pairs={{0,16},{4,20},{8,24},{12,28},{16,0},{20,4},{24,8},{28,12},{1,17},{... | collective-permute-start | bytes 786440 | tf_op jit(solution)/shard_map/ppermute | solution.py:454
  325.8 54.4 %collective-permute-start.31 = (bf16[128,1024]{1,0:T(8,128)(2,1)S(1)}, bf16[128,1024]{1,0:T(8,128)(2,1)S(1)}, u32[]{:S(2)}, u32[]{:S(2)}) collective-permute-start(bf16[128,1024]{1,0:T(8,128)(2,1)S(1)} %get-tuple-element.338), channel_id=1, source_target_pairs={{0,24},{4,28},{8,16},{12,20},{16,8},{20,12},{24,0},{28,4},{1,25},{... | collective-permute-start | bytes 786440 | tf_op jit(solution)/shard_map/ppermute | solution.py:454
  383.2 52.1 %collective-permute-start.36 = (bf16[128,1024]{1,0:T(8,128)(2,1)S(1)}, bf16[128,1024]{1,0:T(8,128)(2,1)}, u32[]{:S(2)}, u32[]{:S(2)}) collective-permute-start(bf16[128,1024]{1,0:T(8,128)(2,1)S(1)} %add_convert_fusion.14), channel_id=1, source_target_pairs={{0,8},{4,12},{8,0},{12,4},{16,24},{20,28},{24,16},{28,20},{1,9},{5... | collective-permute-start | bytes 786440 | tf_op jit(solution)/shard_map/ppermute | solution.py:454
  384.7 50.7 %collective-permute-start.37 = (bf16[128,1024]{1,0:T(8,128)(2,1)S(1)}, bf16[128,1024]{1,0:T(8,128)(2,1)}, u32[]{:S(2)}, u32[]{:S(2)}) collective-permute-start(bf16[128,1024]{1,0:T(8,128)(2,1)S(1)} %add_convert_fusion.14), channel_id=1, source_target_pairs={{0,16},{4,20},{8,24},{12,28},{16,0},{20,4},{24,8},{28,12},{1,17},{... | collective-permute-start | bytes 786440 | tf_op jit(solution)/shard_map/ppermute | solution.py:454
  391.4 44.0 %collective-permute-start.38 = (bf16[128,1024]{1,0:T(8,128)(2,1)S(1)}, bf16[128,1024]{1,0:T(8,128)(2,1)S(1)}, u32[]{:S(2)}, u32[]{:S(2)}) collective-permute-start(bf16[128,1024]{1,0:T(8,128)(2,1)S(1)} %add_convert_fusion.14), channel_id=1, source_target_pairs={{0,24},{4,28},{8,16},{12,20},{16,8},{20,12},{24,0},{28,4},{1,25},{... | collective-permute-start | bytes 786440 | tf_op jit(solution)/shard_map/ppermute | solution.py:454
  392.1 43.3 %collective-permute-start.35 = (bf16[512,1024]{1,0:T(8,128)(2,1)}, bf16[512,1024]{1,0:T(8,128)(2,1)S(1)}, u32[]{:S(2)}, u32[]{:S(2)}) collective-permute-start(bf16[512,1024]{1,0:T(8,128)(2,1)} %get-tuple-element.365), channel_id=1, source_target_pairs={{0,4},{4,0},{8,12},{12,8},{16,20},{20,16},{24,28},{28,24},{1,5},{5... | collective-permute-start | bytes 3145736 | tf_op jit(solution)/shard_map/ppermute | solution.py:454
  437.6 50.0 %collective-permute-start.44 = (bf16[512,1024]{1,0:T(8,128)(2,1)S(1)}, bf16[512,1024]{1,0:T(8,128)(2,1)S(1)}, u32[]{:S(2)}, u32[]{:S(2)}) collective-permute-start(bf16[512,1024]{1,0:T(8,128)(2,1)S(1)} %pad_maximum_fusion.refs_0_), channel_id=1, source_target_pairs={{0,4},{4,0},{8,12},{12,8},{16,20},{20,16},{24,28},{28,24},{1,5},{5... | collective-permute-start | bytes 3145736 | tf_op jit(solution)/shard_map/ppermute | solution.py:454
  439.0 48.5 %collective-permute-start.41 = (bf16[128,1024]{1,0:T(8,128)(2,1)S(1)}, bf16[128,1024]{1,0:T(8,128)(2,1)S(1)}, u32[]{:S(2)}, u32[]{:S(2)}) collective-permute-start(bf16[128,1024]{1,0:T(8,128)(2,1)S(1)} %get-tuple-element.383), channel_id=1, source_target_pairs={{0,8},{4,12},{8,0},{12,4},{16,24},{20,28},{24,16},{28,20},{1,9},{5... | collective-permute-start | bytes 786440 | tf_op jit(solution)/shard_map/ppermute | solution.py:454
  442.3 45.3 %collective-permute-start.42 = (bf16[128,1024]{1,0:T(8,128)(2,1)S(1)}, bf16[128,1024]{1,0:T(8,128)(2,1)S(1)}, u32[]{:S(2)}, u32[]{:S(2)}) collective-permute-start(bf16[128,1024]{1,0:T(8,128)(2,1)S(1)} %get-tuple-element.384), channel_id=1, source_target_pairs={{0,16},{4,20},{8,24},{12,28},{16,0},{20,4},{24,8},{28,12},{1,17},{... | collective-permute-start | bytes 786440 | tf_op jit(solution)/shard_map/ppermute | solution.py:454
  442.7 44.9 %collective-permute-start.43 = (bf16[128,1024]{1,0:T(8,128)(2,1)S(1)}, bf16[128,1024]{1,0:T(8,128)(2,1)S(1)}, u32[]{:S(2)}, u32[]{:S(2)}) collective-permute-start(bf16[128,1024]{1,0:T(8,128)(2,1)S(1)} %get-tuple-element.385), channel_id=1, source_target_pairs={{0,24},{4,28},{8,16},{12,20},{16,8},{20,12},{24,0},{28,4},{1,25},{... | collective-permute-start | bytes 786440 | tf_op jit(solution)/shard_map/ppermute | solution.py:454
  446.1 47.5 %collective-permute-start.40 = (bf16[1024,1024]{1,0:T(8,128)(2,1)}, bf16[1024,1024]{1,0:T(8,128)(2,1)}, u32[]{:S(2)}, u32[]{:S(2)}) collective-permute-start(bf16[1024,1024]{1,0:T(8,128)(2,1)} %add_convert_fusion), channel_id=1, source_target_pairs={{0,2},{1,3},{2,0},{3,1},{4,6},{5,7},{6,4},{7,5},{8,10},{9,11},{10,... | collective-permute-start | bytes 6291464 | tf_op jit(solution)/shard_map/ppermute | solution.py:454
  (77 other events, 1072.3 us)

commit v6 on v5

--- a/solution.py
+++ b/solution.py
@@ -828,7 +828,7 @@
     def ffn(picks, part, extra):
         widths = [FQ if half is None else FQ // 2 for _, half in picks]
         spots = [(k, width, half or 0) for (k, half), width in zip(picks, widths)]
-        high = rows if extra is not None else many * STRETCH
+        high = many * STRETCH
         row = rows_spec(high, D)
         ins = [(n2, row), (cotangent, row)]
         ins += [(be_slots[k][None, :], whole_spec((1, width), at)) for k, width, at in spots]
@@ -846,15 +846,15 @@
             outs += [(wide[0], row)] * 2
         else:
             ins += extra
-            outs += [low, wide, low, low, low]
+            outs += [(kind[0], row) for kind in (low, wide, low, low, low)]
             outs += [
                 (like((state_rows, D), f32), sum_spec((state_rows, D))),
-                (like((nb * DH, D), f32), rows_spec(blocks * DH, D)),
-                (like((nb * 8, D), f32), rows_spec(blocks * 8, D)),
+                (like((nb * DH, D), f32), rows_spec(many * DH, D)),
+                (like((nb * 8, D), f32), rows_spec(many * 8, D)),
                 (like((32, D), f32), sum_spec((32, D))),
             ]
         results = call(
-            functools.partial(ffn_kernel, blocks, widths, part is None, extra is not None),
+            functools.partial(ffn_kernel, many, widths, part is None, extra is not None),
             "ffn",
             (first,) if extra is not None else (),
             R // high,
@@ -870,11 +870,11 @@
 
     eb = [[], [], [], []]
     extra = [
-        (middle, full),
-        (att, full),
-        (rec, full),
-        (q01, side),
-        (q23, side),
+        (middle, tall),
+        (att, tall),
+        (rec, tall),
+        (q01, thin),
+        (q23, thin),
         vector(gain2),
         vector(reduce_bias[None, :]),
     ] + [(w, whole_spec((QW, D))) for w in wo]

time: 630 us -> 631 us (level)
  no operation moved by 1% of the time
where the time goes in v6:
time: 631 us; the launch traced here: 621 us
  Pallas kernels  433 us (69%)
  waiting for transfers between devices  66.6 us (11%)
  starting transfers between devices  52.7 us (8%)
  other arithmetic  51.2 us (8%)
  local copies, waits for them, and re-layouts  16.4 us (3%)
    pallas_call x14, Pallas kernels, call(): pl.pallas_call(kernel, grid_spec=pltpu.PrefetchScalarGridSpec(num_scalar_...  433 us
    ppermute x66, waiting for transfers between devices, swap(): return lax.ppermute(value, axis, [(i, i ^ bit) for i in range(size)])  66.6 us
    ppermute x66, starting transfers between devices, swap(): return lax.ppermute(value, axis, [(i, i ^ bit) for i in range(size)])  52.7 us
    convert_element_type x3, other arithmetic, half(): return total.astype(bf16)  13.1 us
  transfers between devices with their start and end apart: 66, of which 19 were waited for; matrix products, arithmetic and copies ran while one was open for 8% of the time, Pallas kernels for 70%

profile of v6, /device:TPU:8, one launch (start us, length us, event | category | flops | bytes accessed | tf_op | source)
XLA Modules:
  0.0 621.4 jit_solution(17663817945058162952)
XLA Ops:
  12.4 19.1 %qkv.2 = (bf16[2560,512]{1,0:T(8,128)(2,1)}, bf16[2560,512]{1,0:T(8,128)(2,1)}, bf16[2560,512]{1,0:T(8,128)(2,1)}, bf16[2560,1024]{1,0:T(8,128)(2,1)}, f32[72,51...) custom-call(s32[20]{0:T(128)} %subtract_maximum_fusion.thr, s32[21]{0:T(128)} %add_convert_fusion.15.cont, ...), custom_call_target="tpu_custom_call" | custom-call | flops 8053063680 | bytes 24117248 | tf_op jit(solution)/shard_map/qkv/pallas_call | solution.py:431
  31.5 7.1 %collective-permute-done.4 = f32[3584]{0:T(1024)S(1)} collective-permute-done((f32[3584]{0:T(1024)S(1)}, f32[3584]{0:T(1024)S(1)}, u32[]{:S(2)}, u32[]{:S(2)}) %collective-permute-start.4) | collective-permute-done | bytes 14368 | tf_op jit(solution)/shard_map/ppermute | solution.py:454
  46.8 16.2 %qkv.3 = (bf16[2560,512]{1,0:T(8,128)(2,1)}, bf16[2560,512]{1,0:T(8,128)(2,1)}, bf16[2560,512]{1,0:T(8,128)(2,1)}, f32[72,512]{1,0:T(8,128)}, f32[1280,512]{1,0:T(8,128)}, /*index=5*/f32[160,512]{1,0:T(8,128)}) custom-call(s32[20]{0:T(128)} %subtract_maximum_fusion.thr, s32[21]{0:T(128)} %add_convert_fusion.15.cont, ...), custom_call_target="tpu_custom_call" | custom-call | flops 8053063680 | bytes 24117248 | tf_op jit(solution)/shard_map/qkv/pallas_call | solution.py:431
  77.7 35.0 %attend.1 = (bf16[2560,1024]{1,0:T(8,128)(2,1)}, f32[2560,1024]{1,0:T(8,128)}, bf16[1280,1024]{1,0:T(8,128)(2,1)}, f32[160,1024]{1,0:T(8,128)}, f32[2560,1024]{1,0:T(8,128)}, /*index=5*/bf16[2560,1024]{1,0:T(8,128)(2,1)}) custom-call(s32[20]{0:T(128)} %compare_convert_fusion.first.refs_0_, s32[20]{0:T(128)} %subtract_maximum_fusion.thr, ...), custom_call_target="tpu_custom_call" | custom-call | flops 32212254720 | bytes 52428800 | tf_op jit(solution)/shard_map/attend/pallas_call | solution.py:431
  114.9 48.9 %ffn.5 = (bf16[1024,1024]{1,0:T(8,128)(2,1)}, bf16[1024,1024]{1,0:T(8,128)(2,1)}, f32[8,512]{1,0:T(8,128)}, f32[8,512]{1,0:T(8,128)}, f32[2560,1024]{1,0:T(8,128)}, /*index=5*/f32[2560,1024]{1,0:T(8,128)}) custom-call(bf16[2560,1024]{1,0:T(8,128)(2,1)} %get-tuple-element.289.refs_0_.refs_1_, bf16[2560,1024]{1,0:T(8,128)(2,1)} %refs_2_.1, ...), custom_call_target="tpu_custom_call" | custom-call | flops 32212254720 | bytes 52428800 | tf_op jit(solution)/shard_map/ffn/pallas_call | solution.py:431
  166.8 50.8 %ffn.6 = (bf16[1024,1024]{1,0:T(8,128)(2,1)}, bf16[1024,1024]{1,0:T(8,128)(2,1)}, f32[8,512]{1,0:T(8,128)}, f32[8,512]{1,0:T(8,128)}, f32[2560,1024]{1,0:T(8,128)}, /*index=5*/f32[2560,1024]{1,0:T(8,128)}) custom-call(bf16[2560,1024]{1,0:T(8,128)(2,1)} %get-tuple-element.289.refs_0_.refs_1_, bf16[2560,1024]{1,0:T(8,128)(2,1)} %refs_2_.1, ...), custom_call_target="tpu_custom_call" | custom-call | flops 32212254720 | bytes 52428800 | tf_op jit(solution)/shard_map/ffn/pallas_call | solution.py:431
  228.1 51.2 %ffn.7 = (bf16[1024,1024]{1,0:T(8,128)(2,1)}, bf16[1024,1024]{1,0:T(8,128)(2,1)}, f32[8,512]{1,0:T(8,128)}, f32[8,512]{1,0:T(8,128)}, f32[2560,1024]{1,0:T(8,128)}, /*index=5*/f32[2560,1024]{1,0:T(8,128)}) custom-call(bf16[2560,1024]{1,0:T(8,128)(2,1)} %get-tuple-element.289.refs_0_.refs_1_, bf16[2560,1024]{1,0:T(8,128)(2,1)} %refs_2_.1, ...), custom_call_target="tpu_custom_call" | custom-call | flops 32212254720 | bytes 52428800 | tf_op jit(solution)/shard_map/ffn/pallas_call | solution.py:431
  279.3 4.8 add_convert_fusion.10
  289.6 28.8 %ffn.8 = (bf16[1024,1024]{1,0:T(8,128)(2,1)}, f32[8,512]{1,0:T(8,128)}, f32[2560,1024]{1,0:T(8,128)}, f32[2560,1024]{1,0:T(8,128)}) custom-call(bf16[2560,1024]{1,0:T(8,128)(2,1)} %get-tuple-element.289.refs_0_.refs_1_, bf16[2560,1024]{1,0:T(8,128)(2,1)} %refs_2_.1, f32[1,1024]{1,0:T(1,128)} %bitcast.61, f32[2560,1024]{1,0:T(8,128)} %get-tuple-element.324.refs_3_, ...), custom_call_target="tpu_custom_call" | custom-call | flops 16106127360 | bytes 52428800 | tf_op jit(solution)/shard_map/ffn/pallas_call | solution.py:431
  326.1 53.9 %ffn.9 = (bf16[1024,1024]{1,0:T(8,128)(2,1)}, f32[8,512]{1,0:T(8,128)}, bf16[2560,1024]{1,0:T(8,128)(2,1)}, f32[2560,1024]{1,0:T(8,128)}, bf16[2560,1024]{1,0:T(...) custom-call(s32[20]{0:T(128)} %compare_convert_fusion.first.refs_0_,, ...), custom_call_target="tpu_custom_call" | custom-call | flops 16106127360 | bytes 52428800 | tf_op jit(solution)/shard_map/ffn/pallas_call | solution.py:431
  386.7 4.6 add_convert_fusion.7
  395.4 40.2 %attend_back.2 = (bf16[2560,768]{1,0:T(8,128)(2,1)}, bf16[2560,768]{1,0:T(8,128)(2,1)}, bf16[1024,1024]{1,0:T(8,128)(2,1)}, bf16[1024,1024]{1,0:T(8,128)(2,1)}, f32[8,1536]{1,0:T(8,128)}) custom-call(s32[21]{0:T(128)} %add_convert_fusion.15.cont, bf16[2560,512]{1,0:T(8,128)(2,1)} %get-tuple-element.261.refs_5_.refs_12_.q, ...), custom_call_target="tpu_custom_call" | custom-call | flops 32212254720 | bytes 26214400 | tf_op jit(solution)/shard_map/attend_back/pallas_call | solution.py:431
  447.6 40.2 %attend_back.3 = (bf16[2560,768]{1,0:T(8,128)(2,1)}, bf16[2560,768]{1,0:T(8,128)(2,1)}, bf16[1024,1024]{1,0:T(8,128)(2,1)}, bf16[1024,1024]{1,0:T(8,128)(2,1)}, f32[8,1536]{1,0:T(8,128)}) custom-call(s32[21]{0:T(128)} %add_convert_fusion.15.cont, bf16[2560,512]{1,0:T(8,128)(2,1)} %get-tuple-element.245.refs_0_.refs_11_.q, ...), custom_call_target="tpu_custom_call" | custom-call | flops 32212254720 | bytes 26214400 | tf_op jit(solution)/shard_map/attend_back/pallas_call | solution.py:431
  487.8 6.2 %collective-permute-done.40 = bf16[1024,1024]{1,0:T(8,128)(2,1)} collective-permute-done((bf16[1024,1024]{1,0:T(8,128)(2,1)}, bf16[1024,1024]{1,0:T(8,128)(2,1)}, u32[]{:S(2)}, u32[]{:S(2)}) %collective-permute-start.40) | collective-permute-done | bytes 2097184 | tf_op jit(solution)/shard_map/ppermute | solution.py:454
  494.0 4.4 collective-permute-done.45
  508.0 16.3 %input_grad.2 = (f32[2560,1024]{1,0:T(8,128)}, f32[16,1024]{1,0:T(8,128)}) custom-call(bf16[2560,1024]{1,0:T(8,128)(2,1)} %x.1, f32[2560,1024]{1,0:T(8,128)} %get-tuple-element.404.gm, f32[1,1024]{1,0:T(1,128)} %bitcast.49, bf16[2560,768]{1,0:T(8,128)(2,1)} %get-tuple-element.405.refs_0_, bf16[2560,768]{1,0:T(8,128)(2,1)} %get-tuple-element.406.refs_1_, ...), custom_call_target="tpu_custom_call" | custom-call | flops 8053063680 | bytes 20971520 | tf_op jit(solution)/shard_map/input_grad/pallas_call | solution.py:431
  524.8 6.2 collective-permute-done.49
  540.0 16.5 %input_grad.3 = (f32[2560,1024]{1,0:T(8,128)}, f32[16,1024]{1,0:T(8,128)}) custom-call(bf16[2560,1024]{1,0:T(8,128)(2,1)} %x.1, f32[2560,1024]{1,0:T(8,128)} %get-tuple-element.404.gm, f32[1,1024]{1,0:T(1,128)} %bitcast.50, bf16[2560,768]{1,0:T(8,128)(2,1)} %get-tuple-element.405.refs_0_, ...), custom_call_target="tpu_custom_call", output_to_operand_aliasing={{0}: (11, {})} | custom-call | flops 8053063680 | bytes 20971520 | tf_op jit(solution)/shard_map/input_grad/pallas_call | solution.py:431
  556.9 4.7 collective-permute-done.52
  567.7 7.9 %place.2 = f32[1024,1024]{1,0:T(8,128)} custom-call(s32[2]{0:T(128)} %pad_add_fusion.where, bf16[512,1024]{1,0:T(8,128)(2,1)} %copy-done, bf16[512,1024]{1,0:T(8,128)(2,1)} %copy-done.5, bf16[512,1024]{1,0:T(8,128)(2,1)} %copy-done.1, bf16[512,1024]{1,0:T(8,128)(2,1)} %copy-done.6), custom_call_target="tpu_custom_call" | custom-call | bytes 6291456 | tf_op jit(solution)/shard_map/place/pallas_call | solution.py:431
  575.7 5.5 collective-permute-done.55
  581.1 4.6 collective-permute-done.56
  596.2 4.2 collective-permute-done.60
  600.6 7.8 %place.3 = f32[1024,1024]{1,0:T(8,128)} custom-call(s32[2]{0:T(128)} %pad_add_fusion.where, bf16[512,1024]{1,0:T(8,128)(2,1)} %copy-done, bf16[512,1024]{1,0:T(8,128)(2,1)} %copy-done.5, bf16[512,1024]{1,0:T(8,128)(2,1)} %copy-done.1, bf16[512,1024]{1,0:T(8,128)(2,1)} %copy-done.6), custom_call_target="tpu_custom_call" | custom-call | bytes 6291456 | tf_op jit(solution)/shard_map/place/pallas_call | solution.py:431
  (281 shorter events, 134.7 us)
Async XLA Ops:
  1.2 37.5 %collective-permute-start.6 = (bf16[1024,1024]{1,0:T(8,128)(2,1)}, bf16[1024,1024]{1,0:T(8,128)(2,1)}, u32[]{:S(2)}, u32[]{:S(2)}) collective-permute-start(bf16[1024,1024]{1,0:T(8,128)(2,1)} %refs_6_.1), channel_id=1, source_target_pairs={{0,1},{1,0},{2,3},{3,2},{4,5},{5,4},{6,7},{7,6},{8,9},{9,8},{10,11... | collective-permute-start | bytes 6291464 | tf_op jit(solution)/shard_map/ppermute | solution.py:454
  1.3 37.4 %collective-permute-start.7 = (bf16[1024,1024]{1,0:T(8,128)(2,1)}, bf16[1024,1024]{1,0:T(8,128)(2,1)}, u32[]{:S(2)}, u32[]{:S(2)}) collective-permute-start(bf16[1024,1024]{1,0:T(8,128)(2,1)} %refs_7_.3), channel_id=1, source_target_pairs={{0,1},{1,0},{2,3},{3,2},{4,5},{5,4},{6,7},{7,6},{8,9},{9,8},{10,11... | collective-permute-start | bytes 6291464 | tf_op jit(solution)/shard_map/ppermute | solution.py:454
  1.7 37.0 %collective-permute-start.3 = (bf16[1024,768]{1,0:T(8,128)(2,1)}, bf16[1024,768]{1,0:T(8,128)(2,1)}, u32[]{:S(2)}, u32[]{:S(2)}) collective-permute-start(bf16[1024,768]{1,0:T(8,128)(2,1)} %refs_4_.3), channel_id=1, source_target_pairs={{0,2},{1,3},{2,0},{3,1},{4,6},{5,7},{6,4},{7,5},{8,10},{9,11},{10,... | collective-permute-start | bytes 4718600 | tf_op jit(solution)/shard_map/ppermute | solution.py:454
  112.7 51.0 %collective-permute-start.17 = (bf16[512,1024]{1,0:T(8,128)(2,1)}, bf16[512,1024]{1,0:T(8,128)(2,1)}, u32[]{:S(2)}, u32[]{:S(2)}) collective-permute-start(bf16[512,1024]{1,0:T(8,128)(2,1)} %collective-permute-done.14.refs_9_), channel_id=1, source_target_pairs={{0,1},{1,0},{2,3},{3,2},{4,5},{5,4},{6,7},{7,6},{8,9},{9,8},{10,11... | collective-permute-start | bytes 3145736 | tf_op jit(solution)/shard_map/ppermute | solution.py:454
  112.8 51.0 %collective-permute-start.15 = (bf16[1024,512]{1,0:T(8,128)(2,1)S(1)}, bf16[1024,512]{1,0:T(8,128)(2,1)}, u32[]{:S(2)}, u32[]{:S(2)}) collective-permute-start(bf16[1024,512]{1,0:T(8,128)(2,1)S(1)} %get-tuple-element.278), channel_id=1, source_target_pairs={{0,2},{1,3},{2,0},{3,1},{4,6},{5,7},{6,4},{7,5},{8,10},{9,11},{10,... | collective-permute-start | bytes 3145736 | tf_op jit(solution)/shard_map/ppermute | solution.py:454
  114.0 49.8 %collective-permute-start.16 = (bf16[512,1024]{1,0:T(8,128)(2,1)S(1)}, bf16[512,1024]{1,0:T(8,128)(2,1)}, u32[]{:S(2)}, u32[]{:S(2)}) collective-permute-start(bf16[512,1024]{1,0:T(8,128)(2,1)S(1)} %copy-done.13), channel_id=1, source_target_pairs={{0,2},{1,3},{2,0},{3,1},{4,6},{5,7},{6,4},{7,5},{8,10},{9,11},{10,... | collective-permute-start | bytes 3145736 | tf_op jit(solution)/shard_map/ppermute | solution.py:454
  164.4 53.2 %collective-permute-start.21 = (bf16[1024,1024]{1,0:T(8,128)(2,1)}, bf16[1024,1024]{1,0:T(8,128)(2,1)S(1)}, u32[]{:S(2)}, u32[]{:S(2)}) collective-permute-start(bf16[1024,1024]{1,0:T(8,128)(2,1)} %get-tuple-element.295), channel_id=1, source_target_pairs={{0,1},{1,0},{2,3},{3,2},{4,5},{5,4},{6,7},{7,6},{8,9},{9,8},{10,11... | collective-permute-start | bytes 6291464 | tf_op jit(solution)/shard_map/ppermute | solution.py:454
  164.9 52.7 %collective-permute-start.20 = (bf16[512,1024]{1,0:T(8,128)(2,1)}, bf16[512,1024]{1,0:T(8,128)(2,1)}, u32[]{:S(2)}, u32[]{:S(2)}) collective-permute-start(bf16[512,1024]{1,0:T(8,128)(2,1)} %collective-permute-done.16.refs_9_), channel_id=1, source_target_pairs={{0,1},{1,0},{2,3},{3,2},{4,5},{5,4},{6,7},{7,6},{8,9},{9,8},{10,11... | collective-permute-start | bytes 3145736 | tf_op jit(solution)/shard_map/ppermute | solution.py:454
  165.0 52.7 %collective-permute-start.19 = (bf16[1024,512]{1,0:T(8,128)(2,1)S(1)}, bf16[1024,512]{1,0:T(8,128)(2,1)}, u32[]{:S(2)}, u32[]{:S(2)}) collective-permute-start(bf16[1024,512]{1,0:T(8,128)(2,1)S(1)} %get-tuple-element.291), channel_id=1, source_target_pairs={{0,2},{1,3},{2,0},{3,1},{4,6},{5,7},{6,4},{7,5},{8,10},{9,11},{10,... | collective-permute-start | bytes 3145736 | tf_op jit(solution)/shard_map/ppermute | solution.py:454
  225.9 53.3 %collective-permute-start.24 = (bf16[1024,1024]{1,0:T(8,128)(2,1)}, bf16[1024,1024]{1,0:T(8,128)(2,1)}, u32[]{:S(2)}, u32[]{:S(2)}) collective-permute-start(bf16[1024,1024]{1,0:T(8,128)(2,1)} %add_convert_fusion.2), channel_id=1, source_target_pairs={{0,2},{1,3},{2,0},{3,1},{4,6},{5,7},{6,4},{7,5},{8,10},{9,11},{10,... | collective-permute-start | bytes 6291464 | tf_op jit(solution)/shard_map/ppermute | solution.py:454
  319.3 60.7 %collective-permute-start.28 = (bf16[1024,1024]{1,0:T(8,128)(2,1)}, bf16[1024,1024]{1,0:T(8,128)(2,1)S(1)}, u32[]{:S(2)}, u32[]{:S(2)}) collective-permute-start(bf16[1024,1024]{1,0:T(8,128)(2,1)} %get-tuple-element.333), channel_id=1, source_target_pairs={{0,1},{1,0},{2,3},{3,2},{4,5},{5,4},{6,7},{7,6},{8,9},{9,8},{10,11... | collective-permute-start | bytes 6291464 | tf_op jit(solution)/shard_map/ppermute | solution.py:454
  319.5 60.5 %collective-permute-start.27 = (bf16[1024,1024]{1,0:T(8,128)(2,1)}, bf16[1024,1024]{1,0:T(8,128)(2,1)}, u32[]{:S(2)}, u32[]{:S(2)}) collective-permute-start(bf16[1024,1024]{1,0:T(8,128)(2,1)} %add_convert_fusion.1), channel_id=1, source_target_pairs={{0,2},{1,3},{2,0},{3,1},{4,6},{5,7},{6,4},{7,5},{8,10},{9,11},{10,... | collective-permute-start | bytes 6291464 | tf_op jit(solution)/shard_map/ppermute | solution.py:454
  322.5 57.5 %collective-permute-start.29 = (bf16[128,1024]{1,0:T(8,128)(2,1)S(1)}, bf16[128,1024]{1,0:T(8,128)(2,1)S(1)}, u32[]{:S(2)}, u32[]{:S(2)}) collective-permute-start(bf16[128,1024]{1,0:T(8,128)(2,1)S(1)} %get-tuple-element.336), channel_id=1, source_target_pairs={{0,8},{4,12},{8,0},{12,4},{16,24},{20,28},{24,16},{28,20},{1,9},{5... | collective-permute-start | bytes 786440 | tf_op jit(solution)/shard_map/ppermute | solution.py:454
  323.0 57.0 %collective-permute-start.30 = (bf16[128,1024]{1,0:T(8,128)(2,1)S(1)}, bf16[128,1024]{1,0:T(8,128)(2,1)S(1)}, u32[]{:S(2)}, u32[]{:S(2)}) collective-permute-start(bf16[128,1024]{1,0:T(8,128)(2,1)S(1)} %get-tuple-element.337), channel_id=1, source_target_pairs={{0,16},{4,20},{8,24},{12,28},{16,0},{20,4},{24,8},{28,12},{1,17},{... | collective-permute-start | bytes 786440 | tf_op jit(solution)/shard_map/ppermute | solution.py:454
  325.5 54.5 %collective-permute-start.31 = (bf16[128,1024]{1,0:T(8,128)(2,1)S(1)}, bf16[128,1024]{1,0:T(8,128)(2,1)S(1)}, u32[]{:S(2)}, u32[]{:S(2)}) collective-permute-start(bf16[128,1024]{1,0:T(8,128)(2,1)S(1)} %get-tuple-element.338), channel_id=1, source_target_pairs={{0,24},{4,28},{8,16},{12,20},{16,8},{20,12},{24,0},{28,4},{1,25},{... | collective-permute-start | bytes 786440 | tf_op jit(solution)/shard_map/ppermute | solution.py:454
  383.1 52.5 %collective-permute-start.36 = (bf16[128,1024]{1,0:T(8,128)(2,1)S(1)}, bf16[128,1024]{1,0:T(8,128)(2,1)}, u32[]{:S(2)}, u32[]{:S(2)}) collective-permute-start(bf16[128,1024]{1,0:T(8,128)(2,1)S(1)} %add_convert_fusion.14), channel_id=1, source_target_pairs={{0,8},{4,12},{8,0},{12,4},{16,24},{20,28},{24,16},{28,20},{1,9},{5... | collective-permute-start | bytes 786440 | tf_op jit(solution)/shard_map/ppermute | solution.py:454
  384.6 51.0 %collective-permute-start.37 = (bf16[128,1024]{1,0:T(8,128)(2,1)S(1)}, bf16[128,1024]{1,0:T(8,128)(2,1)}, u32[]{:S(2)}, u32[]{:S(2)}) collective-permute-start(bf16[128,1024]{1,0:T(8,128)(2,1)S(1)} %add_convert_fusion.14), channel_id=1, source_target_pairs={{0,16},{4,20},{8,24},{12,28},{16,0},{20,4},{24,8},{28,12},{1,17},{... | collective-permute-start | bytes 786440 | tf_op jit(solution)/shard_map/ppermute | solution.py:454
  391.4 44.3 %collective-permute-start.38 = (bf16[128,1024]{1,0:T(8,128)(2,1)S(1)}, bf16[128,1024]{1,0:T(8,128)(2,1)S(1)}, u32[]{:S(2)}, u32[]{:S(2)}) collective-permute-start(bf16[128,1024]{1,0:T(8,128)(2,1)S(1)} %add_convert_fusion.14), channel_id=1, source_target_pairs={{0,24},{4,28},{8,16},{12,20},{16,8},{20,12},{24,0},{28,4},{1,25},{... | collective-permute-start | bytes 786440 | tf_op jit(solution)/shard_map/ppermute | solution.py:454
  392.1 43.6 %collective-permute-start.35 = (bf16[512,1024]{1,0:T(8,128)(2,1)}, bf16[512,1024]{1,0:T(8,128)(2,1)S(1)}, u32[]{:S(2)}, u32[]{:S(2)}) collective-permute-start(bf16[512,1024]{1,0:T(8,128)(2,1)} %get-tuple-element.365), channel_id=1, source_target_pairs={{0,4},{4,0},{8,12},{12,8},{16,20},{20,16},{24,28},{28,24},{1,5},{5... | collective-permute-start | bytes 3145736 | tf_op jit(solution)/shard_map/ppermute | solution.py:454
  437.9 49.9 %collective-permute-start.44 = (bf16[512,1024]{1,0:T(8,128)(2,1)S(1)}, bf16[512,1024]{1,0:T(8,128)(2,1)S(1)}, u32[]{:S(2)}, u32[]{:S(2)}) collective-permute-start(bf16[512,1024]{1,0:T(8,128)(2,1)S(1)} %pad_maximum_fusion.refs_0_), channel_id=1, source_target_pairs={{0,4},{4,0},{8,12},{12,8},{16,20},{20,16},{24,28},{28,24},{1,5},{5... | collective-permute-start | bytes 3145736 | tf_op jit(solution)/shard_map/ppermute | solution.py:454
  439.4 48.3 %collective-permute-start.41 = (bf16[128,1024]{1,0:T(8,128)(2,1)S(1)}, bf16[128,1024]{1,0:T(8,128)(2,1)S(1)}, u32[]{:S(2)}, u32[]{:S(2)}) collective-permute-start(bf16[128,1024]{1,0:T(8,128)(2,1)S(1)} %get-tuple-element.383), channel_id=1, source_target_pairs={{0,8},{4,12},{8,0},{12,4},{16,24},{20,28},{24,16},{28,20},{1,9},{5... | collective-permute-start | bytes 786440 | tf_op jit(solution)/shard_map/ppermute | solution.py:454
  442.7 45.1 %collective-permute-start.42 = (bf16[128,1024]{1,0:T(8,128)(2,1)S(1)}, bf16[128,1024]{1,0:T(8,128)(2,1)S(1)}, u32[]{:S(2)}, u32[]{:S(2)}) collective-permute-start(bf16[128,1024]{1,0:T(8,128)(2,1)S(1)} %get-tuple-element.384), channel_id=1, source_target_pairs={{0,16},{4,20},{8,24},{12,28},{16,0},{20,4},{24,8},{28,12},{1,17},{... | collective-permute-start | bytes 786440 | tf_op jit(solution)/shard_map/ppermute | solution.py:454
  443.0 44.7 %collective-permute-start.43 = (bf16[128,1024]{1,0:T(8,128)(2,1)S(1)}, bf16[128,1024]{1,0:T(8,128)(2,1)S(1)}, u32[]{:S(2)}, u32[]{:S(2)}) collective-permute-start(bf16[128,1024]{1,0:T(8,128)(2,1)S(1)} %get-tuple-element.385), channel_id=1, source_target_pairs={{0,24},{4,28},{8,16},{12,20},{16,8},{20,12},{24,0},{28,4},{1,25},{... | collective-permute-start | bytes 786440 | tf_op jit(solution)/shard_map/ppermute | solution.py:454
  446.5 47.5 %collective-permute-start.40 = (bf16[1024,1024]{1,0:T(8,128)(2,1)}, bf16[1024,1024]{1,0:T(8,128)(2,1)}, u32[]{:S(2)}, u32[]{:S(2)}) collective-permute-start(bf16[1024,1024]{1,0:T(8,128)(2,1)} %add_convert_fusion), channel_id=1, source_target_pairs={{0,2},{1,3},{2,0},{3,1},{4,6},{5,7},{6,4},{7,5},{8,10},{9,11},{10,... | collective-permute-start | bytes 6291464 | tf_op jit(solution)/shard_map/ppermute | solution.py:454
  (77 other events, 1072.5 us)
